TPU v7x, 256 devices: a whole 4x4x8 slice. The times are simulated.
256 devices in a mesh: ocean: 32 (over y, z_hi, core), sht: 8 (over z_lo, x).
Axes of the slice: x: 4, y: 4, z: 8 (z_hi: 4, z_lo: 2; z = z_hi * 2 + z_lo), core: 2. Of those that a mesh axis runs over, the one named last changes fastest.
Arguments:
- height: float32 [512, 2048], P('ocean', 'sht'), may hold values from -6 to 6
- east: float32 [512, 2048], P('ocean', 'sht'), may hold values from -3 to 3
- north: float32 [512, 2048], P('ocean', 'sht'), may hold values from -3 to 3
- depth: float32 [512, 2048], P('ocean', 'sht'), may hold values from 0.3 to 1.5
- equilibrium: float32 [512, 2048], P('ocean', 'sht'), may hold values from -3 to 3
- mask: int32 [512, 2048], P('ocean', 'sht'), may hold values from 0 to 1, as said below
- sines: float32 [512], P('ocean'), may hold values from -0.95 to 0.95, as said below
- legendre: float32 [512, 1024, 1024], P('ocean', None, 'sht'), as said below
- love: float32 [1024], replicated, may hold values from 0.01 to 0.3
Outputs:
- level_out: float32 [512, 2048], P('ocean', 'sht')
- east_out: float32 [512, 2048], P('ocean', 'sht')
- north_out: float32 [512, 2048], P('ocean', 'sht')
Inputs may be any that keep to these rules, and one draw needn't show every extreme that they name: `mask`: 1 marks ocean, 0 land; rows 0 and 511 and columns 0 and 2047 are land. `sines`: ascending; row j lies within 0.2 / 512 * 1.9 of -0.95 + 1.9 (j + 0.5) / 512. legendre[j, l, m] is the fully normalized associated Legendre function of degree l and order m at sines[j] (unit integral of its square over -1 to 1), zero where l < m.
All inputs are finite; a program needn't handle non-finite values.
Results may differ from a plain program's by a relative error of at most 0.0003.
Values sent between devices are 32-bit elements; how exact they have to be, the bound alone decides.
No kernel may reach another device: no remote copies, remote signals or barrier semaphores. Data moves between devices by JAX's collectives and lax.ppermute only.
A program may use at most 128 MiB of HBM per device.

v0:
```python
import math

import jax
import jax.numpy as jnp
from jax import lax
from jax.sharding import PartitionSpec as P

STEPS = 3


COURANT = 0.12
ROTATION = 0.5
FRICTION = 0.3
HIGHEST = lax.Precision.HIGHEST


def extended(x, sides, width):
    for axis, dim in sides:
        peers, length = (lax.axis_size(axis), x.shape[dim])
        up = [(i, (i + 1) % peers) for i in range(peers - 1)]
        down = [(j, i) for i, j in up]
        last = lax.slice_in_dim(x, length - width, length, axis=dim)
        initial = lax.slice_in_dim(x, 0, width, axis=dim)
        before = lax.ppermute(last, axis, up)
        after = lax.ppermute(initial, axis, down)
        x = jnp.concatenate([before, x, after], axis=dim)
    return x


def decode_columns(width, order_dev):
    column = jnp.arange(width, dtype=jnp.int32)
    owner = column // (2 * order_dev)
    within = column % (2 * order_dev)
    component = within // order_dev
    order = owner * order_dev + within % order_dev
    return (component, order)


def phases(first, second, lon_total):
    phase_index = first[:, None] * second[None, :] % lon_total
    return phase_index.astype(jnp.float32) * (2.0 * math.pi / lon_total)


def per_device(height, east, north, depth, equilibrium, mask, sines, legendre, love):
    lat_rows, lon_cols = height.shape
    order_dev = legendre.shape[2]
    sht_count = lax.axis_size("sht")
    ocean_count = lax.axis_size("ocean")
    lon_total = lon_cols * sht_count
    lat_total = lat_rows * ocean_count
    longitude = lax.axis_index("sht") * lon_cols + jnp.arange(lon_cols, dtype=jnp.int32)
    component, order = decode_columns(2 * order_dev * sht_count, order_dev)
    angles = phases(longitude, order, lon_total)
    analysis = jnp.where(component[None, :] == 0, jnp.cos(angles), -jnp.sin(angles)) / lon_total
    order_angles = phases(order, longitude, lon_total)
    doubling = jnp.where(order == 0, 1.0, 2.0).astype(jnp.float32)[:, None]
    synth_table = (
        jnp.where(component[:, None] == 0, jnp.cos(order_angles), -jnp.sin(order_angles)) * doubling
    )
    wet_cells = mask == 1
    east_coef = (COURANT / jnp.sqrt(1.0 - sines * sines))[:, None]
    coriolis = (ROTATION * sines)[:, None]
    level = jnp.where(wet_cells, height, 0.0)
    eastward, northward = (east, north)
    damping = FRICTION / depth
    for step_index in range(STEPS):
        partial_spectra = jnp.dot(
            level, analysis, precision=HIGHEST, preferred_element_type=jnp.float32
        )
        spectra = lax.psum_scatter(partial_spectra, "sht", scatter_dimension=1, tiled=True)
        weighted = spectra.reshape(lat_rows, 2, order_dev) * (2.0 / lat_total)
        partial_coefs = jnp.einsum("jlm,jcm->lcm", legendre, weighted, precision=HIGHEST)
        coefs = lax.psum(partial_coefs, "ocean")
        loaded = coefs * love[:, None, None]
        synth = jnp.einsum("jlm,lcm->jcm", legendre, loaded, precision=HIGHEST)
        flat_synth = synth.reshape(lat_rows, 2 * order_dev)
        potential = (
            level
            - jnp.dot(
                lax.all_gather(flat_synth, "sht", axis=1, tiled=True),
                synth_table,
                precision=HIGHEST,
                preferred_element_type=jnp.float32,
            )
            - equilibrium
        )
        padded = extended(potential, (("ocean", 0), ("sht", 1)), 1)
        grad_east = east_coef * (padded[1:-1, 2:] - padded[1:-1, :-2])
        grad_north = COURANT * (padded[2:, 1:-1] - padded[:-2, 1:-1])
        new_east = jnp.where(
            wet_cells, eastward + coriolis * northward - grad_east - damping * eastward, 0.0
        )
        new_north = jnp.where(
            wet_cells, northward - coriolis * eastward - grad_north - damping * northward, 0.0
        )
        fluxes = extended(
            jnp.stack([depth * new_east, depth * new_north]), (("ocean", 1), ("sht", 2)), 1
        )
        divergence = east_coef * (fluxes[0, 1:-1, 2:] - fluxes[0, 1:-1, :-2]) + COURANT * (
            fluxes[1, 2:, 1:-1] - fluxes[1, :-2, 1:-1]
        )
        level = jnp.where(wet_cells, level - divergence, 0.0)
        eastward, northward = (new_east, new_north)
    return (level, eastward, northward)


def solution(mesh):
    in_specs = (
        P("ocean", "sht"),
        P("ocean", "sht"),
        P("ocean", "sht"),
        P("ocean", "sht"),
        P("ocean", "sht"),
        P("ocean", "sht"),
        P("ocean"),
        P("ocean", None, "sht"),
        P(),
    )
    out_specs = (P("ocean", "sht"), P("ocean", "sht"), P("ocean", "sht"))
    return jax.shard_map(
        per_device, mesh=mesh, in_specs=in_specs, out_specs=out_specs, check_vma=False
    )
```

profile of v0, /device:TPU:1, one launch (start us, length us, event | category | flops | bytes accessed | tf_op | source)
XLA Modules:
  0.0 1284.8 jit_solution(12782789291308798590)
XLA Ops:
  8.0 10.9 fusion.14
  19.2 8.9 copy.19
  28.1 28.9 %reduce-scatter.4.cloned.1.call-done = f32[16,256]{1,0:T(8,128)} async-done(((f32[16,2048]{1,0:T(8,128)}), f32[16,256]{1,0:T(8,128)}) %reduce-scatter.4.cloned.1.call-update) | async-done | bytes 16400 | tf_op jit(solution)/shard_map/reduce_scatter | solution.py:70
  57.9 7.3 convolution_bitcast_fusion.2
  65.3 290.0 %all-reduce.4.cloned.1.call-done = f32[1024,2,128]{0,1,2:T(2,128)} async-done(((f32[1024,2,128]{0,1,2:T(2,128)}), f32[1024,2,128]{0,1,2:T(2,128)}) %all-reduce.4.cloned.1.call-update) | async-done | bytes 1048592 | tf_op jit(solution)/shard_map/psum | solution.py:73
  355.3 11.4 convolution_bitcast_fusion.5
  366.9 22.5 %all_gather.9 = f32[16,2048]{1,0:T(8,128)S(1)} all-gather(f32[16,256]{1,0:T(8,128)S(1)} %bitcast.93), channel_id=1, replica_groups=mesh['ocean'=32,'sht'=8] {'sht'}, dimensions={1}, use_global_device_ids=true | all-gather | bytes 147456 | tf_op jit(solution)/shard_map/all_gather | solution.py:80
  389.5 9.5 fusion.8
  399.0 8.4 collective-permute-start.1
  432.1 10.2 fusion.13
  442.4 36.9 %reduce-scatter.6.cloned.1.call-done = f32[16,256]{1,0:T(8,128)} async-done(((f32[16,2048]{1,0:T(8,128)}), f32[16,256]{1,0:T(8,128)}) %reduce-scatter.6.cloned.1.call-update) | async-done | bytes 16400 | tf_op jit(solution)/shard_map/reduce_scatter | solution.py:70
  480.1 7.3 convolution_bitcast_fusion.1
  487.5 290.1 %all-reduce.6.cloned.1.call-done = f32[1024,2,128]{0,1,2:T(2,128)} async-done(((f32[1024,2,128]{0,1,2:T(2,128)}), f32[1024,2,128]{0,1,2:T(2,128)}) %all-reduce.6.cloned.1.call-update) | async-done | bytes 1048592 | tf_op jit(solution)/shard_map/psum | solution.py:73
  777.6 11.4 convolution_bitcast_fusion.4
  789.2 22.5 %all_gather.10 = f32[16,2048]{1,0:T(8,128)S(1)} all-gather(f32[16,256]{1,0:T(8,128)S(1)} %bitcast.95), channel_id=1, replica_groups=mesh['ocean'=32,'sht'=8] {'sht'}, dimensions={1}, use_global_device_ids=true | all-gather | bytes 147456 | tf_op jit(solution)/shard_map/all_gather | solution.py:80
  811.7 9.5 fusion.7
  821.2 8.4 collective-permute-start.9
  854.3 10.2 fusion.12
  864.6 36.9 %reduce-scatter.8.cloned.1.call-done = f32[16,256]{1,0:T(8,128)} async-done(((f32[16,2048]{1,0:T(8,128)}), f32[16,256]{1,0:T(8,128)}) %reduce-scatter.8.cloned.1.call-update) | async-done | bytes 16400 | tf_op jit(solution)/shard_map/reduce_scatter | solution.py:70
  909.7 290.2 %all-reduce.8.cloned.1.call-done = f32[1024,2,128]{0,1,2:T(2,128)} async-done(((f32[1024,2,128]{0,1,2:T(2,128)}), f32[1024,2,128]{0,1,2:T(2,128)}) %all-reduce.8.cloned.1.call-update) | async-done | bytes 1048592 | tf_op jit(solution)/shard_map/psum | solution.py:73
  1199.9 11.4 convolution_bitcast_fusion.3
  1211.4 22.4 %all_gather.11 = f32[16,2048]{1,0:T(8,128)S(1)} all-gather(f32[16,256]{1,0:T(8,128)S(1)} %bitcast.97), channel_id=1, replica_groups=mesh['ocean'=32,'sht'=8] {'sht'}, dimensions={1}, use_global_device_ids=true | all-gather | bytes 147456 | tf_op jit(solution)/shard_map/all_gather | solution.py:80
  1233.8 9.5 fusion.6
  1243.3 8.4 collective-permute-start.17
  (119 shorter events, 86.5 us)
Async XLA Ops:
  7.2 49.9 %reduce-scatter.4.cloned.1.call-start = ((), (), s32[]{:S(2)}) async-start(), calls=%async_computation.3 | async-start | bytes 147456 | tf_op jit(solution)/shard_map/reduce_scatter | solution.py:70
  18.9 336.4 %all-reduce.4.cloned.1.call-start = ((), (), s32[]{:S(2)}) async-start(), calls=%async_computation.4 | async-start | bytes 2097152 | tf_op jit(solution)/shard_map/psum | solution.py:73
  65.2 414.1 %reduce-scatter.6.cloned.1.call-start = ((), (), s32[]{:S(2)}) async-start(), calls=%async_computation.5 | async-start | bytes 147456 | tf_op jit(solution)/shard_map/reduce_scatter | solution.py:70
  399.0 10.3 collective-permute-start.1
  410.5 5.3 collective-permute-start.2
  416.7 7.7 collective-permute-start.5
  419.9 5.2 collective-permute-start.4
  425.2 6.0 collective-permute-start.6
  426.5 5.5 collective-permute-start.7
  442.4 335.3 %all-reduce.6.cloned.1.call-start = ((), (), s32[]{:S(2)}) async-start(), calls=%async_computation.6 | async-start | bytes 2097152 | tf_op jit(solution)/shard_map/psum | solution.py:73
  487.5 414.0 %reduce-scatter.8.cloned.1.call-start = ((), (), s32[]{:S(2)}) async-start(), calls=%async_computation.7 | async-start | bytes 147456 | tf_op jit(solution)/shard_map/reduce_scatter | solution.py:70
  821.2 10.3 collective-permute-start.9
  832.7 5.3 collective-permute-start.10
  838.9 7.7 collective-permute-start.13
  842.2 5.2 collective-permute-start.12
  847.5 6.0 collective-permute-start.14
  848.8 5.5 collective-permute-start.15
  864.6 335.3 %all-reduce.8.cloned.1.call-start = ((), (), s32[]{:S(2)}) async-start(), calls=%async_computation.8 | async-start | bytes 2097152 | tf_op jit(solution)/shard_map/psum | solution.py:73
  1243.3 10.3 collective-permute-start.17
  1254.8 5.3 collective-permute-start.18
  1261.6 7.7 collective-permute-start.21
  1264.8 5.2 collective-permute-start.20
  1270.1 5.8 collective-permute-start.22
  1271.4 5.5 collective-permute-start.23
  (14 other events, 1097.6 us)
Sparse Core Ops, SparseCore 0:
  19.1 37.9 reduce-scatter.3
  65.3 289.9 all-reduce.3
  442.5 36.7 reduce-scatter.5
  487.6 290.0 all-reduce.5
  864.7 36.7 reduce-scatter.7
  909.8 290.0 all-reduce.7
where the time goes:
time: 1300 us; the launch traced here: 1280 us
  waiting for transfers between devices  983 us (76%)
  matrix products  116 us (9%)
  starting transfers between devices  88.1 us (7%)
  blocking collectives  67.5 us (5%)
  between operations  15 us (1%)
    psum x3, waiting for transfers between devices, per_device(): coefs = lax.psum(partial_coefs, 'ocean')  870 us
    reduce_scatter x3, waiting for transfers between devices, per_device(): lax.psum_scatter(partial_spectra, 'sht', scatter_dimension=1, tiled=True)  103 us
    all_gather x3, blocking collectives, per_device(): lax.all_gather(flat_synth, 'sht', axis=1, tiled=True)  67.5 us
    ppermute x12, starting transfers between devices, extended(): before = lax.ppermute(last, axis, up)  45.2 us
    ppermute x12, starting transfers between devices, extended(): after = lax.ppermute(initial, axis, down)  42.4 us
    dot_general x3, matrix products, per_device(): synth = jnp.einsum('jlm,lcm->jcm', legendre, loaded, precision=HIGHEST)  34.3 us
    dot_general x3, matrix products, per_device(): jnp.dot(level, analysis, precision=HIGHEST, preferred_element_type=jnp.fl...  31.4 us
    dot_general x3, matrix products, per_device(): jnp.dot(lax.all_gather(flat_synth, 'sht', axis=1, tiled=True), synth_tabl...  28.5 us
  transfers between devices with their start and end apart: 30, of which 18 were waited for; matrix products, arithmetic and copies ran while one was open for 1% of the time, Pallas kernels for 0%

commit v1 on v0

v1 whole, which is shorter than its diff:
```python
import functools

import jax
import jax.numpy as jnp
import ml_dtypes
import numpy as np
from jax import lax
from jax.experimental import pallas as pl
from jax.experimental.pallas import tpu as pltpu
from jax.sharding import PartitionSpec as P

STEPS = 3
COURANT = 0.12
ROTATION = 0.5
FRICTION = 0.3

NLON = 2048
ROWS = 16
COLS = 256
ORD = 128
SHT = 8
OCEAN = 32
CHIPS = OCEAN // 2
LDEG = 1024
HALF = LDEG // 2
CHUNK = HALF // CHIPS
BLOCK = 128
EXT = 384
LANE = 128
EROWS = 32

F32 = jnp.float32
BF16 = jnp.bfloat16


def split(table):
    high = table.astype(ml_dtypes.bfloat16)
    low = (table - high.astype(np.float64)).astype(ml_dtypes.bfloat16)
    return high, low


def tables():
    kappa = np.arange(COLS)[:, None]
    order = np.arange(ORD)[None, :]
    turn = 2.0 * np.pi * (kappa * order % NLON) / NLON
    cosine, sine = np.cos(turn), np.sin(turn)
    analysis = split(np.block([[cosine, -sine], [sine, cosine]]))

    column = np.arange(EXT)
    column = np.where(column < COLS + LANE // 2, column, column - EXT)
    turn = 2.0 * np.pi * (order.T * column[None, :] % NLON) / NLON
    cosine, sine = np.cos(turn), np.sin(turn)
    synthesis = split(np.block([[cosine, sine], [-sine, cosine]]))

    owner = np.arange(SHT)[:, None]
    turn = 2.0 * np.pi * (np.arange(COLS)[None, :] * owner % 16) / 16
    by_owner = np.stack([np.cos(turn), -np.sin(turn)], 1).astype(np.float32)
    turn = 2.0 * np.pi * (np.arange(ORD)[None, :] * owner % 8) / 8
    by_block = np.stack([np.cos(turn), np.sin(turn)], 0).astype(np.float32)
    turn = 2.0 * np.pi * (column[None, :] * owner % 16) / 16
    at_columns = np.stack([np.cos(turn), np.sin(turn)], 0).astype(np.float32)
    doubling = np.full((SHT, 1, ORD), 2.0, np.float32)
    doubling[0, 0, 0] = 1.0
    return analysis, synthesis, by_owner, by_block, at_columns, doubling


def dot3(a, high, low):
    a_high = a.astype(BF16)
    a_low = (a - a_high.astype(F32)).astype(BF16)
    dot = functools.partial(jnp.dot, preferred_element_type=F32)
    return dot(a_high, high) + (dot(a_low, high) + dot(a_high, low))


def start_kernel(height, mask, level, spread):
    value = jnp.where(mask[...] == 1, height[...], 0.0)
    level[...] = value
    for t in range(SHT):
        spread[t] = value


def multiply_rows(weights, legendre, partial):
    wide = [
        [jnp.broadcast_to(weights[c, j : j + 1, :], (8, ORD)) for j in range(ROWS)]
        for c in range(2)
    ]
    for tile in range(BLOCK // 8):
        h, r = divmod(8 * tile, CHUNK)
        sums = [None, None]
        for j in range(ROWS):
            p = legendre[j, 8 * tile : 8 * tile + 8, :]
            for c in range(2):
                term = p * wide[c][j]
                sums[c] = term if sums[c] is None else sums[c] + term
        for c in range(2):
            partial[h, c, r : r + 8, :] = sums[c]


def transform_kernel(half, gathered, rotation, high, low, by_block, legendre, partial, spectra):
    @pl.when(pl.program_id(0) == 0)
    def _():
        z = gathered[...].reshape(SHT * ROWS, COLS)
        a = jnp.concatenate([z * rotation[0:1, :], z * rotation[1:2, :]], 1)
        y = dot3(a, high[...], low[...]).reshape(SHT, ROWS, 2 * ORD)
        re, im = y[:, :, :ORD], y[:, :, ORD:]
        c, s = by_block[0][:, None, :], by_block[1][:, None, :]
        scale = 1.0 / NLON * (2.0 / (ROWS * OCEAN))
        spectra[0] = jnp.sum(re * c + im * s, axis=0) * scale
        spectra[1] = jnp.sum(im * c - re * s, axis=0) * scale

    multiply_rows(spectra[...], legendre, partial)


def rows_kernel(half, spectra, legendre, partial):
    multiply_rows(spectra[...], legendre, partial)


def add_degrees(coefs, legendre, sums):
    acc = [[sums[c, j] for j in range(ROWS)] for c in range(2)]
    for tile in range(BLOCK // 8):
        h, r = divmod(8 * tile, CHUNK)
        x = [coefs[h, c, r : r + 8, :] for c in range(2)]
        for j in range(ROWS):
            p = legendre[j, 8 * tile : 8 * tile + 8, :]
            for c in range(2):
                acc[c][j] = acc[c][j] + p * x[c]
    for c in range(2):
        for j in range(ROWS):
            sums[c, j] = acc[c][j]


def degrees_kernel(half, coefs, legendre, sums):
    @pl.when(pl.program_id(0) == 0)
    def _():
        sums[...] = jnp.zeros_like(sums)

    add_degrees(coefs, legendre, sums)


def finish_kernel(half, before, coefs, legendre, spread, sums, synth):
    @pl.when(pl.program_id(0) == 0)
    def _():
        sums[...] = before[...]

    add_degrees(coefs, legendre, sums)

    @pl.when(pl.program_id(0) == pl.num_programs(0) - 1)
    def _():
        for c in range(2):
            for j in range(ROWS):
                synth[c, j : j + 1, :] = jnp.sum(sums[c, j], axis=0, keepdims=True)
        value = synth[...]
        for t in range(SHT):
            spread[t] = value


def potential_kernel(
    place, synth, rotation, doubling, high, low, at_columns, gathered, equilibrium, pot, first, last
):
    t = place[0]
    c, s = rotation[0:1, :][None], rotation[1:2, :][None]
    e = doubling[...]
    s0, s1 = synth[:, 0] * e, synth[:, 1] * e
    vr = (s0 * c - s1 * s).reshape(SHT * ROWS, ORD)
    vi = (s0 * s + s1 * c).reshape(SHT * ROWS, ORD)
    g = dot3(jnp.concatenate([vr, vi], 1), high[...], low[...]).reshape(SHT, ROWS, 2 * EXT)
    sal = jnp.sum(
        g[:, :, :EXT] * at_columns[0][:, None, :] - g[:, :, EXT:] * at_columns[1][:, None, :], axis=0
    )
    right = gathered[lax.rem(t + 1, SHT)][:, :LANE]
    left = gathered[lax.rem(t + SHT - 1, SHT)][:, LANE:]
    lane = lax.broadcasted_iota(jnp.int32, (ROWS, LANE), 1)
    level = jnp.concatenate([gathered[t], jnp.where(lane < LANE // 2, right, left)], 1)
    pot[...] = level - sal - equilibrium[...]
    first[...] = pot[0:2, :]
    last[...] = pot[ROWS - 2 : ROWS, :]


def step_kernel(
    place, pot, above, below, east, north, depth, wet, damping, east_coef, coriolis, gathered, *rest
):
    *outs, field = rest
    field[...] = jnp.zeros_like(field)
    field[6:8, :] = above[...]
    field[8:24, :] = pot[...]
    field[24:26, :] = below[...]
    p = field[...]
    plus_col = lambda x: pltpu.roll(x, EXT - 1, 1)
    minus_col = lambda x: pltpu.roll(x, 1, 1)
    plus_row = lambda x: pltpu.roll(x, EROWS - 1, 0)
    minus_row = lambda x: pltpu.roll(x, 1, 0)
    ec = east_coef[...]
    u, v, f, d = east[...], north[...], coriolis[...], damping[...]
    ocean = wet[...] > 0.5
    grad_east = ec * (plus_col(p) - minus_col(p))
    grad_north = COURANT * (plus_row(p) - minus_row(p))
    new_u = jnp.where(ocean, u + f * v - grad_east - d * u, 0.0)
    new_v = jnp.where(ocean, v - f * u - grad_north - d * v, 0.0)
    flux_u, flux_v = depth[...] * new_u, depth[...] * new_v
    div = ec * (plus_col(flux_u) - minus_col(flux_u)) + COURANT * (
        plus_row(flux_v) - minus_row(flux_v)
    )
    inner = (slice(8, 24), slice(0, COLS))
    level = jnp.where(ocean[inner], gathered[place[0]] - div[inner], 0.0)
    if len(outs) == 3 and outs[0].shape == (EROWS, EXT):
        outs[0][...] = new_u
        outs[1][...] = new_v
        for t in range(SHT):
            outs[2][t] = level
    else:
        outs[0][...] = level
        outs[1][...] = new_u[inner]
        outs[2][...] = new_v[inner]


def shape(*dims):
    return jax.ShapeDtypeStruct(dims, F32)


PARAMS = pltpu.CompilerParams(vmem_limit_bytes=56 * 1024 * 1024)
COST = pl.CostEstimate(flops=2 * ROWS * HALF * ORD * 2, bytes_accessed=9 << 20, transcendentals=0)
WHOLE = pl.BlockSpec(memory_space=pltpu.VMEM)
SCALAR = pl.BlockSpec(memory_space=pltpu.SMEM)


def streamed(kernel, in_specs, out_specs, out_shape, scratch=()):
    return pl.pallas_call(
        kernel,
        grid_spec=pltpu.PrefetchScalarGridSpec(
            num_scalar_prefetch=1,
            grid=(HALF // BLOCK,),
            in_specs=in_specs,
            out_specs=out_specs,
            scratch_shapes=list(scratch),
        ),
        out_shape=out_shape,
        compiler_params=PARAMS,
        cost_estimate=COST,
    )


def fixed(*dims):
    return pl.BlockSpec(dims, lambda i, half: (0,) * len(dims))


LEGENDRE = pl.BlockSpec((ROWS, BLOCK, ORD), lambda i, half: (0, half[0] * (HALF // BLOCK) + i, 0))
COEFS = pl.BlockSpec((BLOCK // CHUNK, 2, CHUNK, ORD), lambda i, half: (i, 0, 0, 0))


def per_device(height, east, north, depth, equilibrium, mask, sines, legendre, love):
    analysis, synthesis, by_owner, by_block, at_columns, doubling = tables()
    sht = lax.axis_index("sht")
    ocean = lax.axis_index("ocean")
    core = lax.rem(ocean, 2)
    place = sht.astype(jnp.int32).reshape(1)
    own_half = core.astype(jnp.int32).reshape(1)
    other_half = 1 - own_half
    owner_rotation = lax.dynamic_index_in_dim(jnp.asarray(by_owner), sht, 0, False)
    block_rotation = lax.dynamic_index_in_dim(jnp.asarray(by_block), sht, 1, False)
    a_high, a_low = (jnp.asarray(x) for x in analysis)
    s_high, s_low = (jnp.asarray(x) for x in synthesis)

    cores = [(i, i ^ 1) for i in range(OCEAN)]
    groups = [[2 * h + c for h in range(CHIPS)] for c in range(2)]
    next_row = [(i, i + 1) for i in range(OCEAN - 1)]
    prev_row = [(j, i) for i, j in next_row]
    next_col = [(i, i + 1) for i in range(SHT - 1)]
    prev_col = [(j, i) for i, j in next_col]

    level, spread = pl.pallas_call(
        start_kernel,
        in_specs=[WHOLE, WHOLE],
        out_specs=[WHOLE, WHOLE],
        out_shape=[shape(ROWS, COLS), shape(SHT, ROWS, COLS)],
    )(height, mask)

    wet = (mask == 1).astype(F32)
    stack = jnp.stack([equilibrium, east, north, depth, wet])
    from_right = lax.ppermute(stack[:, :, :LANE], "sht", prev_col)
    from_left = lax.ppermute(stack[:, :, COLS - LANE :], "sht", next_col)
    lane = lax.broadcasted_iota(jnp.int32, from_right.shape, 2)
    stack = jnp.concatenate([stack, jnp.where(lane < LANE // 2, from_right, from_left)], 2)
    equilibrium_ext = stack[0]
    stack = jnp.concatenate(
        [stack[1:], jnp.broadcast_to(sines[None, :, None], (1, ROWS, EXT))], 0
    )
    from_below = lax.ppermute(stack[:, :8], "ocean", prev_row)
    from_above = lax.ppermute(stack[:, ROWS - 8 :], "ocean", next_row)
    stack = jnp.concatenate([from_above, stack, from_below], 1)
    u, v, depth_ext, wet_ext, sines_ext = (stack[i] for i in range(5))
    damping = FRICTION / jnp.where(wet_ext > 0.5, depth_ext, 1.0)
    east_coef = COURANT / jnp.sqrt(1.0 - sines_ext * sines_ext)
    coriolis = ROTATION * sines_ext

    own_chunk = core * HALF + (ocean // 2) * CHUNK
    own_love = lax.dynamic_slice_in_dim(love, own_chunk, CHUNK)[None, :, None]

    partial_shape = shape(CHIPS, 2, CHUNK, ORD)
    for step_index in range(STEPS):
        gathered = lax.all_to_all(spread, "sht", 0, 0, tiled=True)
        given, spectra = streamed(
            transform_kernel,
            [
                fixed(SHT, ROWS, COLS),
                fixed(2, COLS),
                fixed(2 * COLS, 2 * ORD),
                fixed(2 * COLS, 2 * ORD),
                fixed(2, SHT, ORD),
                LEGENDRE,
            ],
            [COEFS, fixed(2, ROWS, ORD)],
            [partial_shape, shape(2, ROWS, ORD)],
        )(other_half, gathered, owner_rotation, a_high, a_low, by_block, legendre)
        taken = lax.ppermute(given, "ocean", cores)
        kept = streamed(rows_kernel, [fixed(2, ROWS, ORD), LEGENDRE], COEFS, partial_shape)(
            own_half, spectra, legendre
        )
        parts = lax.all_to_all(
            kept + taken, "ocean", 0, 0, tiled=True, axis_index_groups=groups
        )
        loaded = jnp.sum(parts, axis=0) * own_love
        own = lax.all_to_all(
            jnp.broadcast_to(loaded[None], (CHIPS, 2, CHUNK, ORD)),
            "ocean",
            0,
            0,
            tiled=True,
            axis_index_groups=groups,
        )
        other = lax.ppermute(own, "ocean", cores)
        sums = streamed(
            degrees_kernel, [COEFS, LEGENDRE], fixed(2, ROWS, 8, ORD), shape(2, ROWS, 8, ORD)
        )(own_half, own, legendre)
        synth_spread = streamed(
            finish_kernel,
            [fixed(2, ROWS, 8, ORD), COEFS, LEGENDRE],
            fixed(SHT, 2, ROWS, ORD),
            shape(SHT, 2, ROWS, ORD),
            [pltpu.VMEM((2, ROWS, 8, ORD), F32), pltpu.VMEM((2, ROWS, ORD), F32)],
        )(other_half, sums, other, legendre)
        synth = lax.all_to_all(synth_spread, "sht", 0, 0, tiled=True)
        pot, first, last = pl.pallas_call(
            potential_kernel,
            in_specs=[SCALAR] + [WHOLE] * 8,
            out_specs=[WHOLE] * 3,
            out_shape=[shape(ROWS, EXT), shape(2, EXT), shape(2, EXT)],
            compiler_params=PARAMS,
        )(
            place,
            synth,
            block_rotation,
            doubling,
            s_high,
            s_low,
            at_columns,
            gathered,
            equilibrium_ext,
        )
        below = lax.ppermute(first, "ocean", prev_row)
        above = lax.ppermute(last, "ocean", next_row)
        final = step_index == STEPS - 1
        block = shape(ROWS, COLS)
        extended = shape(EROWS, EXT)
        results = pl.pallas_call(
            step_kernel,
            in_specs=[SCALAR] + [WHOLE] * 11,
            out_specs=[WHOLE] * 3,
            out_shape=[block] * 3 if final else [extended, extended, shape(SHT, ROWS, COLS)],
            scratch_shapes=[pltpu.VMEM((EROWS, EXT), F32)],
            compiler_params=PARAMS,
        )(
            place,
            pot,
            above,
            below,
            u,
            v,
            depth_ext,
            wet_ext,
            damping,
            east_coef,
            coriolis,
            gathered,
        )
        if final:
            return tuple(results)
        u, v, spread = results


def solution(mesh):
    in_specs = (
        P("ocean", "sht"),
        P("ocean", "sht"),
        P("ocean", "sht"),
        P("ocean", "sht"),
        P("ocean", "sht"),
        P("ocean", "sht"),
        P("ocean"),
        P("ocean", None, "sht"),
        P(),
    )
    out_specs = (P("ocean", "sht"), P("ocean", "sht"), P("ocean", "sht"))
    return jax.shard_map(
        per_device, mesh=mesh, in_specs=in_specs, out_specs=out_specs, check_vma=False
    )
```

time: 1300 us -> 327 us (0.25)
  waiting for transfers between devices: 983 us -> 51.9 us
  matrix products: 116 us -> 0 us
  Pallas kernels: 0 us -> 64 us
  blocking collectives: 67.5 us -> 131 us
  starting transfers between devices: 88.1 us -> 60.8 us
  between operations: 15 us -> 0.97 us
    psum x3 -> x0, waiting for transfers between devices: 870 us -> none  [per_device(): coefs = lax.psum(partial_coefs, 'ocean')]
    all_to_all x0 -> x8, blocking collectives: none -> 131 us  [the longest x2 50.4 us: per_device(): lax.all_to_all(kept + taken, 'ocean', 0, 0, tiled=True, axis_index_groups...]
    dot_general x12 -> x0, matrix products: 116 us -> none  [the longest x3 34.3 us: per_device(): synth = jnp.einsum('jlm,lcm->jcm', legendre, loaded, precision=HIGHEST)]
    reduce_scatter x3 -> x0, waiting for transfers between devices: 103 us -> none  [per_device(): lax.psum_scatter(partial_spectra, 'sht', scatter_dimension=1, tiled=True)]
    all_gather x3 -> x0, blocking collectives: 67.5 us -> none  [per_device(): lax.all_gather(flat_synth, 'sht', axis=1, tiled=True)]
    pallas_call x0 -> x19, Pallas kernels: none -> 64 us  [the longest x3 13.7 us: per_device(): streamed(transform_kernel, [fixed(SHT, ROWS, COLS), fixed(2, COLS), fixed...]
    ppermute x24 -> x16, starting transfers between devices: 87.6 us -> 37.1 us  [the longest x3 11.9 us: per_device(): above = lax.ppermute(last, 'ocean', next_row)]
    all_to_all x0 -> x4, waiting for transfers between devices: none -> 35.7 us  [the longest x1 17 us: per_device(): lax.all_to_all(kept + taken, 'ocean', 0, 0, tiled=True, axis_index_groups...]
  transfers between devices with their start and end apart: 30 -> 20, of which waited for: 18 -> 8; matrix products, arithmetic and copies ran while one was open for 1% -> 2% of each run, Pallas kernels for 0% -> 7%
where the time goes in v1:
time: 327 us; the launch traced here: 325 us
  blocking collectives  131 us (40%)
  Pallas kernels  64 us (20%)
  starting transfers between devices  60.8 us (19%)
  waiting for transfers between devices  51.9 us (16%)
  local copies, waits for them, and re-layouts  9.84 us (3%)
  other arithmetic  6.56 us (2%)
    all_to_all x2, blocking collectives, per_device(): lax.all_to_all(kept + taken, 'ocean', 0, 0, tiled=True, axis_index_groups...  50.4 us
    all_to_all x2, blocking collectives, per_device(): lax.all_to_all(jnp.broadcast_to(loaded[None], (CHIPS, 2, CHUNK, ORD)), 'o...  42.3 us
    all_to_all x2, blocking collectives, per_device(): synth = lax.all_to_all(synth_spread, 'sht', 0, 0, tiled=True)  19 us
    all_to_all x2, blocking collectives, per_device(): gathered = lax.all_to_all(spread, 'sht', 0, 0, tiled=True)  18.8 us
    all_to_all x1, waiting for transfers between devices, per_device(): lax.all_to_all(kept + taken, 'ocean', 0, 0, tiled=True, axis_index_groups...  17 us
    pallas_call x3, Pallas kernels, per_device(): streamed(transform_kernel, [fixed(SHT, ROWS, COLS), fixed(2, COLS), fixed...  13.7 us
    pallas_call x3, Pallas kernels, per_device(): streamed(rows_kernel, [fixed(2, ROWS, ORD), LEGENDRE], COEFS, partial_shape)  12.4 us
    pallas_call x3, Pallas kernels, per_device(): streamed(finish_kernel, [fixed(2, ROWS, 8, ORD), COEFS, LEGENDRE], fixed(...  12.1 us
  transfers between devices with their start and end apart: 20, of which 8 were waited for; matrix products, arithmetic and copies ran while one was open for 2% of the time, Pallas kernels for 7%

profile of v1, /device:TPU:1, one launch (start us, length us, event | category | flops | bytes accessed | tf_op | source)
XLA Modules:
  0.0 324.5 jit_solution(15391725191863988203)
XLA Ops:
  2.0 6.2 %all-to-all-start = ((f32[8,16,256]{2,1,0:T(8,128)}), f32[8,16,256]{2,1,0:T(8,128)S(1)}, u32[]{:S(2)}, u32[]{:S(2)}) async-start(f32[8,16,256]{2,1,0:T(8,128)} %get-tuple-element.25), calls=%async_computation | async-start | bytes 262144 | tf_op jit(solution)/shard_map/all_to_all | solution.py:299
  9.5 4.2 %all-to-all-done.gathered = f32[8,16,256]{2,1,0:T(8,128)S(1)} async-done(((f32[8,16,256]{2,1,0:T(8,128)}), f32[8,16,256]{2,1,0:T(8,128)S(1)}, u32[]{:S(2)}, u32[]{:S(2)}) %all-to-all-start) | async-done | bytes 131104 | tf_op jit(solution)/shard_map/all_to_all | solution.py:299
  14.3 4.6 %shard_map.185 = (f32[16,2,32,128]{3,2,1,0:T(8,128)}, f32[2,16,128]{2,1,0:T(8,128)}) custom-call(s32[1]{0:T(128)S(6)} %sub.12.half, f32[8,16,256]{2,1,0:T(8,128)} %copy-done, f32[2,256]{1,0:T(2,128)} %dynamic-slice_bitcast_fusion.rotation, bf16[512,256]{1,0:T(8,128)(2,1)} %constant.73.clone.high, bf16[512,256]{1,0:T(8,128)(2,1)} %constant.74.clone.low, ...), custom_call_target="tpu_custom_call" | custom-call | flops 4194304 | bytes 9437184 | tf_op jit(solution)/shard_map/pallas_call | solution.py:300
  21.1 4.1 %shard_map.186 = f32[16,2,32,128]{3,2,1,0:T(8,128)} custom-call(s32[1]{0:T(128)} %bitcast.1.half, f32[2,16,128]{2,1,0:T(8,128)} %get-tuple-element.26.spectra, f32[16,1024,128]{2,1,0:T(8,128)} %legendre.23), custom_call_target="tpu_custom_call" | custom-call | flops 4194304 | bytes 9437184 | tf_op jit(solution)/shard_map/pallas_call | solution.py:314
  27.2 10.0 %all-to-all-start.1 = ((f32[16,2,32,128]{3,2,1,0:T(8,128)}), f32[16,2,32,128]{3,2,1,0:T(8,128)S(1)}, u32[]{:S(2)}, u32[]{:S(2)}) async-start(f32[16,2,32,128]{3,2,1,0:T(8,128)} %add.23), calls=%async_computation.1 | async-start | bytes 1048576 | tf_op jit(solution)/shard_map/all_to_all | solution.py:317
  38.0 17.0 %all-to-all-done.1 = f32[16,2,32,128]{3,2,1,0:T(8,128)S(1)} async-done(((f32[16,2,32,128]{3,2,1,0:T(8,128)}), f32[16,2,32,128]{3,2,1,0:T(8,128)S(1)}, u32[]{:S(2)}, u32[]{:S(2)}) %all-to-all-start.1) | async-done | bytes 524320 | tf_op jit(solution)/shard_map/all_to_all | solution.py:317
  66.7 9.9 %all-to-all-done.2.coefs = f32[16,2,32,128]{3,2,1,0:T(8,128)S(1)} async-done(((f32[16,2,32,128]{3,2,1,0:T(8,128)}), f32[16,2,32,128]{3,2,1,0:T(8,128)S(1)}, u32[]{:S(2)}, u32[]{:S(2)}) %all-to-all-start.2) | async-done | bytes 524320 | tf_op jit(solution)/shard_map/all_to_all | solution.py:321
  84.8 4.5 %collective-permute-done.7 = f32[5,8,384]{2,1,0:T(8,128)S(1)} collective-permute-done((f32[5,8,384]{2,1,0:T(8,128)S(1)}, f32[5,8,384]{2,1,0:T(8,128)S(1)}, u32[]{:S(2)}, u32[]{:S(2)}) %collective-permute-start.7) | collective-permute-done | bytes 61472 | tf_op jit(solution)/shard_map/ppermute | solution.py:286
  102.3 4.6 %all-to-all-done.3.synth = f32[8,2,16,128]{3,2,1,0:T(8,128)S(1)} async-done(((f32[8,2,16,128]{3,2,1,0:T(8,128)}), f32[8,2,16,128]{3,2,1,0:T(8,128)S(1)}, u32[]{:S(2)}, u32[]{:S(2)}) %all-to-all-start.3) | async-done | bytes 131104 | tf_op jit(solution)/shard_map/all_to_all | solution.py:340
  121.4 9.4 %all_to_all.60.gathered = f32[8,16,256]{2,1,0:T(8,128)} all-to-all(f32[8,16,256]{2,1,0:T(8,128)} %get-tuple-element.31), channel_id=1, replica_groups=mesh['ocean'=32,'sht'=8] {'sht'}, dimensions={0} | all-to-all | bytes 262144 | tf_op jit(solution)/shard_map/all_to_all | solution.py:299
  130.8 4.6 %shard_map.191 = (f32[16,2,32,128]{3,2,1,0:T(8,128)}, f32[2,16,128]{2,1,0:T(8,128)}) custom-call(s32[1]{0:T(128)S(6)} %sub.12.half, f32[8,16,256]{2,1,0:T(8,128)} %all_to_all.60.gathered, f32[2,256]{1,0:T(2,128)} %dynamic-slice_bitcast_fusion.rotation, bf16[512,256]{1,0:T(8,128)(2,1)} %constant.73.clone.high, bf16[512,256]{1,0:T(8,128)(2,1)} %constant.74.clone.low, ...), custom_call_target="tpu_custom_call" | custom-call | flops 4194304 | bytes 9437184 | tf_op jit(solution)/shard_map/pallas_call | solution.py:300
  135.4 4.1 %shard_map.192 = f32[16,2,32,128]{3,2,1,0:T(8,128)} custom-call(s32[1]{0:T(128)} %bitcast.1.half, f32[2,16,128]{2,1,0:T(8,128)} %get-tuple-element.32.spectra, f32[16,1024,128]{2,1,0:T(8,128)} %legendre.23), custom_call_target="tpu_custom_call" | custom-call | flops 4194304 | bytes 9437184 | tf_op jit(solution)/shard_map/pallas_call | solution.py:314
  140.7 25.9 %all_to_all.61 = f32[16,2,32,128]{3,2,1,0:T(8,128)S(1)} all-to-all(f32[16,2,32,128]{3,2,1,0:T(8,128)S(1)} %add.26), channel_id=1, replica_groups={{0,16,32,48,64,80,96,112,128,144,160,176,192,208,224,240},{8,24,40,56,7..., dimensions={0} | all-to-all | bytes 1048576 | tf_op jit(solution)/shard_map/all_to_all | solution.py:317
  166.8 21.2 %all_to_all.62.coefs = f32[16,2,32,128]{3,2,1,0:T(8,128)S(1)} all-to-all(f32[16,2,32,128]{3,2,1,0:T(8,128)S(1)} %broadcast_in_dim.18), channel_id=1, replica_groups={{0,16,32,48,64,80,96,112,128,144,160,176,192,208,224,240},{8,24,40,56,7..., dimensions={0} | all-to-all | bytes 1048576 | tf_op jit(solution)/shard_map/all_to_all | solution.py:321
  199.0 9.5 %all_to_all.63.synth = f32[8,2,16,128]{3,2,1,0:T(8,128)} all-to-all(f32[8,2,16,128]{3,2,1,0:T(8,128)} %shard_map.194), channel_id=1, replica_groups=mesh['ocean'=32,'sht'=8] {'sht'}, dimensions={0} | all-to-all | bytes 262144 | tf_op jit(solution)/shard_map/all_to_all | solution.py:340
  210.7 4.5 %collective-permute-start.10 = (f32[2,384]{1,0:T(2,128)}, f32[2,384]{1,0:T(2,128)S(1)}, u32[]{:S(2)}, u32[]{:S(2)}) collective-permute-start(f32[2,384]{1,0:T(2,128)} %get-tuple-element.35), channel_id=1, source_target_pairs={{0,8},{8,16},{16,24},{24,32},{32,40},{40,48},{48,56},{56,64},{64,7... | collective-permute-start | bytes 9224 | tf_op jit(solution)/shard_map/ppermute | solution.py:359
  223.7 9.4 %all_to_all.64.gathered = f32[8,16,256]{2,1,0:T(8,128)} all-to-all(f32[8,16,256]{2,1,0:T(8,128)} %get-tuple-element.39), channel_id=1, replica_groups=mesh['ocean'=32,'sht'=8] {'sht'}, dimensions={0} | all-to-all | bytes 262144 | tf_op jit(solution)/shard_map/all_to_all | solution.py:299
  233.1 4.6 %shard_map.197 = (f32[16,2,32,128]{3,2,1,0:T(8,128)}, f32[2,16,128]{2,1,0:T(8,128)}) custom-call(s32[1]{0:T(128)S(6)} %sub.12.half, f32[8,16,256]{2,1,0:T(8,128)} %all_to_all.64.gathered, f32[2,256]{1,0:T(2,128)} %dynamic-slice_bitcast_fusion.rotation, bf16[512,256]{1,0:T(8,128)(2,1)} %constant.73.clone.high, bf16[512,256]{1,0:T(8,128)(2,1)} %constant.74.clone.low, ...), custom_call_target="tpu_custom_call" | custom-call | flops 4194304 | bytes 9437184 | tf_op jit(solution)/shard_map/pallas_call | solution.py:300
  237.7 4.1 %shard_map.198 = f32[16,2,32,128]{3,2,1,0:T(8,128)} custom-call(s32[1]{0:T(128)} %bitcast.1.half, f32[2,16,128]{2,1,0:T(8,128)} %get-tuple-element.40.spectra, f32[16,1024,128]{2,1,0:T(8,128)} %legendre.23), custom_call_target="tpu_custom_call" | custom-call | flops 4194304 | bytes 9437184 | tf_op jit(solution)/shard_map/pallas_call | solution.py:314
  243.0 24.5 %all_to_all.65 = f32[16,2,32,128]{3,2,1,0:T(8,128)S(1)} all-to-all(f32[16,2,32,128]{3,2,1,0:T(8,128)S(1)} %add.27), channel_id=1, replica_groups={{0,16,32,48,64,80,96,112,128,144,160,176,192,208,224,240},{8,24,40,56,7..., dimensions={0} | all-to-all | bytes 1048576 | tf_op jit(solution)/shard_map/all_to_all | solution.py:317
  267.6 21.1 %all_to_all.66.coefs = f32[16,2,32,128]{3,2,1,0:T(8,128)S(1)} all-to-all(f32[16,2,32,128]{3,2,1,0:T(8,128)S(1)} %broadcast_in_dim.36), channel_id=1, replica_groups={{0,16,32,48,64,80,96,112,128,144,160,176,192,208,224,240},{8,24,40,56,7..., dimensions={0} | all-to-all | bytes 1048576 | tf_op jit(solution)/shard_map/all_to_all | solution.py:321
  299.9 9.5 %all_to_all.67.synth = f32[8,2,16,128]{3,2,1,0:T(8,128)} all-to-all(f32[8,2,16,128]{3,2,1,0:T(8,128)} %shard_map.200), channel_id=1, replica_groups=mesh['ocean'=32,'sht'=8] {'sht'}, dimensions={0} | all-to-all | bytes 262144 | tf_op jit(solution)/shard_map/all_to_all | solution.py:340
  311.6 4.4 %collective-permute-start.14 = (f32[2,384]{1,0:T(2,128)}, f32[2,384]{1,0:T(2,128)S(1)}, u32[]{:S(2)}, u32[]{:S(2)}) collective-permute-start(f32[2,384]{1,0:T(2,128)} %get-tuple-element.43), channel_id=1, source_target_pairs={{0,8},{8,16},{16,24},{24,32},{32,40},{40,48},{48,56},{56,64},{64,7... | collective-permute-start | bytes 9224 | tf_op jit(solution)/shard_map/ppermute | solution.py:359
  318.0 4.1 %collective-permute-done.15.below = f32[2,384]{1,0:T(2,128)S(1)} collective-permute-done((f32[2,384]{1,0:T(2,128)}, f32[2,384]{1,0:T(2,128)S(1)}, u32[]{:S(2)}, u32[]{:S(2)}) %collective-permute-start.15) | collective-permute-done | bytes 3104 | tf_op jit(solution)/shard_map/ppermute | solution.py:358
  (113 shorter events, 97.5 us)
Async XLA Ops:
  2.0 11.7 %all-to-all-start = ((f32[8,16,256]{2,1,0:T(8,128)}), f32[8,16,256]{2,1,0:T(8,128)S(1)}, u32[]{:S(2)}, u32[]{:S(2)}) async-start(f32[8,16,256]{2,1,0:T(8,128)} %get-tuple-element.25), calls=%async_computation | async-start | bytes 262144 | tf_op jit(solution)/shard_map/all_to_all | solution.py:299
  18.9 41.2 %copy-start.11 = (f32[16,256]{1,0:T(8,128)S(1)}, f32[16,256]{1,0:T(8,128)}, u32[]{:S(2)}) copy-start(f32[16,256]{1,0:T(8,128)} %param.19) | copy-start | bytes 49156
  18.9 41.2 %copy-start.12 = (f32[16,256]{1,0:T(8,128)S(1)}, f32[16,256]{1,0:T(8,128)}, u32[]{:S(2)}) copy-start(f32[16,256]{1,0:T(8,128)} %param.20) | copy-start | bytes 49156
  18.9 41.2 %copy-start.8 = (s32[16,256]{1,0:T(8,128)S(1)}, s32[16,256]{1,0:T(8,128)}, u32[]{:S(2)}) copy-start(s32[16,256]{1,0:T(8,128)} %mask.1) | copy-start | bytes 49156
  18.9 60.2 %copy-start.19 = (f32[16]{0:T(128)S(1)}, f32[16]{0:T(128)}, u32[]{:S(2)}) copy-start(f32[16]{0:T(128)} %param.23) | copy-start | bytes 196
  18.9 6.3 %collective-permute-start = (f32[16,2,32,128]{3,2,1,0:T(8,128)}, f32[16,2,32,128]{3,2,1,0:T(8,128)S(1)}, u32[]{:S(2)}, u32[]{:S(2)}) collective-permute-start(f32[16,2,32,128]{3,2,1,0:T(8,128)} %get-tuple-element.27), channel_id=1, source_target_pairs={{0,8},{8,0},{16,24},{24,16},{32,40},{40,32},{48,56},{56,48},{64,72... | collective-permute-start | bytes 1572872 | tf_op jit(solution)/shard_map/ppermute | solution.py:313
  27.2 27.8 %all-to-all-start.1 = ((f32[16,2,32,128]{3,2,1,0:T(8,128)}), f32[16,2,32,128]{3,2,1,0:T(8,128)S(1)}, u32[]{:S(2)}, u32[]{:S(2)}) async-start(f32[16,2,32,128]{3,2,1,0:T(8,128)} %add.23), calls=%async_computation.1 | async-start | bytes 1048576 | tf_op jit(solution)/shard_map/all_to_all | solution.py:317
  56.0 20.6 %all-to-all-start.2 = ((f32[16,2,32,128]{3,2,1,0:T(8,128)}), f32[16,2,32,128]{3,2,1,0:T(8,128)S(1)}, u32[]{:S(2)}, u32[]{:S(2)}) async-start(f32[16,2,32,128]{3,2,1,0:T(8,128)} %broadcast_in_dim.14), calls=%async_computation.2 | async-start | bytes 1048576 | tf_op jit(solution)/shard_map/all_to_all | solution.py:321
  60.1 19.0 %collective-permute-start.2 = (f32[5,16,128]{2,1,0:T(8,128)S(1)}, f32[5,16,128]{2,1,0:T(8,128)S(1)}, u32[]{:S(2)}, u32[]{:S(2)}) collective-permute-start(f32[5,16,128]{2,1,0:T(8,128)S(1)} %get-tuple-element.56), channel_id=1, source_target_pairs={{1,0},{2,1},{3,2},{4,3},{5,4},{6,5},{7,6},{9,8},{10,9},{11,10},{12... | collective-permute-start | bytes 122888 | tf_op jit(solution)/shard_map/ppermute | solution.py:278
  61.4 17.7 %collective-permute-start.3 = (f32[5,16,128]{2,1,0:T(8,128)S(1)}, f32[5,16,128]{2,1,0:T(8,128)S(1)}, u32[]{:S(2)}, u32[]{:S(2)}) collective-permute-start(f32[5,16,128]{2,1,0:T(8,128)S(1)} %get-tuple-element.55), channel_id=1, source_target_pairs={{0,1},{1,2},{2,3},{3,4},{4,5},{5,6},{6,7},{8,9},{9,10},{10,11},{11... | collective-permute-start | bytes 122888 | tf_op jit(solution)/shard_map/ppermute | solution.py:279
  76.6 16.8 %collective-permute-start.1 = (f32[16,2,32,128]{3,2,1,0:T(8,128)S(1)}, f32[16,2,32,128]{3,2,1,0:T(8,128)S(1)}, u32[]{:S(2)}, u32[]{:S(2)}) collective-permute-start(f32[16,2,32,128]{3,2,1,0:T(8,128)S(1)} %all-to-all-done.2.coefs), channel_id=1, source_target_pairs={{0,8},{8,0},{16,24},{24,16},{32,40},{40,32},{48,56},{56,48},{64,72... | collective-permute-start | bytes 1572872 | tf_op jit(solution)/shard_map/ppermute | solution.py:329
  79.3 5.6 %collective-permute-start.6 = (f32[5,8,384]{2,1,0:T(8,128)S(1)}, f32[5,8,384]{2,1,0:T(8,128)S(1)}, u32[]{:S(2)}, u32[]{:S(2)}) collective-permute-start(f32[5,8,384]{2,1,0:T(8,128)S(1)} %get-tuple-element.53), channel_id=1, source_target_pairs={{0,8},{8,16},{16,24},{24,32},{32,40},{40,48},{48,56},{56,64},{64,7... | collective-permute-start | bytes 184328 | tf_op jit(solution)/shard_map/ppermute | solution.py:287
  82.3 7.1 %collective-permute-start.7 = (f32[5,8,384]{2,1,0:T(8,128)S(1)}, f32[5,8,384]{2,1,0:T(8,128)S(1)}, u32[]{:S(2)}, u32[]{:S(2)}) collective-permute-start(f32[5,8,384]{2,1,0:T(8,128)S(1)} %get-tuple-element.54), channel_id=1, source_target_pairs={{8,0},{16,8},{24,16},{32,24},{40,32},{48,40},{56,48},{64,56},{72,6... | collective-permute-start | bytes 184328 | tf_op jit(solution)/shard_map/ppermute | solution.py:286
  98.2 8.7 %all-to-all-start.3 = ((f32[8,2,16,128]{3,2,1,0:T(8,128)}), f32[8,2,16,128]{3,2,1,0:T(8,128)S(1)}, u32[]{:S(2)}, u32[]{:S(2)}) async-start(f32[8,2,16,128]{3,2,1,0:T(8,128)} %shard_map.188), calls=%async_computation.3 | async-start | bytes 262144 | tf_op jit(solution)/shard_map/all_to_all | solution.py:340
  109.8 5.6 %collective-permute-start.4 = (f32[2,384]{1,0:T(2,128)}, f32[2,384]{1,0:T(2,128)S(1)}, u32[]{:S(2)}, u32[]{:S(2)}) collective-permute-start(f32[2,384]{1,0:T(2,128)} %get-tuple-element.29), channel_id=1, source_target_pairs={{0,8},{8,16},{16,24},{24,32},{32,40},{40,48},{48,56},{56,64},{64,7... | collective-permute-start | bytes 9224 | tf_op jit(solution)/shard_map/ppermute | solution.py:359
  112.8 6.0 %collective-permute-start.5 = (f32[2,384]{1,0:T(2,128)}, f32[2,384]{1,0:T(2,128)S(1)}, u32[]{:S(2)}, u32[]{:S(2)}) collective-permute-start(f32[2,384]{1,0:T(2,128)} %get-tuple-element.30), channel_id=1, source_target_pairs={{8,0},{16,8},{24,16},{32,24},{40,32},{48,40},{56,48},{64,56},{72,6... | collective-permute-start | bytes 9224 | tf_op jit(solution)/shard_map/ppermute | solution.py:358
  135.4 4.1 %collective-permute-start.8 = (f32[16,2,32,128]{3,2,1,0:T(8,128)}, f32[16,2,32,128]{3,2,1,0:T(8,128)S(1)}, u32[]{:S(2)}, u32[]{:S(2)}) collective-permute-start(f32[16,2,32,128]{3,2,1,0:T(8,128)} %get-tuple-element.33), channel_id=1, source_target_pairs={{0,8},{8,0},{16,24},{24,16},{32,40},{40,32},{48,56},{56,48},{64,72... | collective-permute-start | bytes 1572872 | tf_op jit(solution)/shard_map/ppermute | solution.py:313
  187.9 6.2 %collective-permute-start.9 = (f32[16,2,32,128]{3,2,1,0:T(8,128)S(1)}, f32[16,2,32,128]{3,2,1,0:T(8,128)S(1)}, u32[]{:S(2)}, u32[]{:S(2)}) collective-permute-start(f32[16,2,32,128]{3,2,1,0:T(8,128)S(1)} %all_to_all.62.coefs), channel_id=1, source_target_pairs={{0,8},{8,0},{16,24},{24,16},{32,40},{40,32},{48,56},{56,48},{64,72... | collective-permute-start | bytes 1572872 | tf_op jit(solution)/shard_map/ppermute | solution.py:329
  210.7 6.4 %collective-permute-start.10 = (f32[2,384]{1,0:T(2,128)}, f32[2,384]{1,0:T(2,128)S(1)}, u32[]{:S(2)}, u32[]{:S(2)}) collective-permute-start(f32[2,384]{1,0:T(2,128)} %get-tuple-element.35), channel_id=1, source_target_pairs={{0,8},{8,16},{16,24},{24,32},{32,40},{40,48},{48,56},{56,64},{64,7... | collective-permute-start | bytes 9224 | tf_op jit(solution)/shard_map/ppermute | solution.py:359
  215.2 6.0 %collective-permute-start.11 = (f32[2,384]{1,0:T(2,128)}, f32[2,384]{1,0:T(2,128)S(1)}, u32[]{:S(2)}, u32[]{:S(2)}) collective-permute-start(f32[2,384]{1,0:T(2,128)} %get-tuple-element.36), channel_id=1, source_target_pairs={{8,0},{16,8},{24,16},{32,24},{40,32},{48,40},{56,48},{64,56},{72,6... | collective-permute-start | bytes 9224 | tf_op jit(solution)/shard_map/ppermute | solution.py:358
  237.7 4.1 %collective-permute-start.12 = (f32[16,2,32,128]{3,2,1,0:T(8,128)}, f32[16,2,32,128]{3,2,1,0:T(8,128)S(1)}, u32[]{:S(2)}, u32[]{:S(2)}) collective-permute-start(f32[16,2,32,128]{3,2,1,0:T(8,128)} %get-tuple-element.41), channel_id=1, source_target_pairs={{0,8},{8,0},{16,24},{24,16},{32,40},{40,32},{48,56},{56,48},{64,72... | collective-permute-start | bytes 1572872 | tf_op jit(solution)/shard_map/ppermute | solution.py:313
  288.7 6.3 %collective-permute-start.13 = (f32[16,2,32,128]{3,2,1,0:T(8,128)S(1)}, f32[16,2,32,128]{3,2,1,0:T(8,128)S(1)}, u32[]{:S(2)}, u32[]{:S(2)}) collective-permute-start(f32[16,2,32,128]{3,2,1,0:T(8,128)S(1)} %all_to_all.66.coefs), channel_id=1, source_target_pairs={{0,8},{8,0},{16,24},{24,16},{32,40},{40,32},{48,56},{56,48},{64,72... | collective-permute-start | bytes 1572872 | tf_op jit(solution)/shard_map/ppermute | solution.py:329
  311.6 6.4 %collective-permute-start.14 = (f32[2,384]{1,0:T(2,128)}, f32[2,384]{1,0:T(2,128)S(1)}, u32[]{:S(2)}, u32[]{:S(2)}) collective-permute-start(f32[2,384]{1,0:T(2,128)} %get-tuple-element.43), channel_id=1, source_target_pairs={{0,8},{8,16},{16,24},{24,32},{32,40},{40,48},{48,56},{56,64},{64,7... | collective-permute-start | bytes 9224 | tf_op jit(solution)/shard_map/ppermute | solution.py:359
  316.0 6.0 %collective-permute-start.15 = (f32[2,384]{1,0:T(2,128)}, f32[2,384]{1,0:T(2,128)S(1)}, u32[]{:S(2)}, u32[]{:S(2)}) collective-permute-start(f32[2,384]{1,0:T(2,128)} %get-tuple-element.44), channel_id=1, source_target_pairs={{8,0},{16,8},{24,16},{32,24},{40,32},{48,40},{56,48},{64,56},{72,6... | collective-permute-start | bytes 9224 | tf_op jit(solution)/shard_map/ppermute | solution.py:358
  (16 other events, 91.4 us)

commit v2 on v0

v2 whole, which is shorter than its diff:
```python
import functools

import jax
import jax.numpy as jnp
import ml_dtypes
import numpy as np
from jax import lax
from jax.experimental import pallas as pl
from jax.experimental.pallas import tpu as pltpu
from jax.sharding import PartitionSpec as P

STEPS = 3
COURANT = 0.12
ROTATION = 0.5
FRICTION = 0.3

NLON = 2048
ROWS = 16
COLS = 256
ORD = 128
SHT = 8
OCEAN = 32
LDEG = 1024
CHUNK = 128
PEERS = 4
EROWS = 32
FIELDS = 5

F32 = jnp.float32
BF16 = jnp.bfloat16


def split(table):
    high = table.astype(ml_dtypes.bfloat16)
    low = (table - high.astype(np.float64)).astype(ml_dtypes.bfloat16)
    return high, low


def tables():
    kappa = np.arange(COLS)[:, None]
    order = np.arange(ORD)[None, :]
    turn = 2.0 * np.pi * (kappa * order % NLON) / NLON
    cosine, sine = np.cos(turn), np.sin(turn)
    analysis = np.stack(split(np.block([[cosine, sine]])))
    cosine, sine = cosine.T, sine.T
    synthesis = split(np.block([[cosine, sine], [-sine, cosine]]))

    owner = np.arange(SHT)[:, None]
    turn = 2.0 * np.pi * (np.arange(COLS)[None, :] * owner % 16) / 16
    by_owner = np.stack([np.cos(turn), np.sin(turn)], 0).astype(np.float32)
    turn = 2.0 * np.pi * (np.arange(ORD)[None, :] * owner % 8) / 8
    by_block = np.stack([np.cos(turn), np.sin(turn)], 0).astype(np.float32)
    doubling = np.full((SHT, 1, ORD), 2.0, np.float32)
    doubling[0, 0, 0] = 1.0
    turns = np.concatenate([by_owner, by_block], 2)
    return analysis, synthesis, turns, doubling


def dot3(a, high, low):
    a_high = a.astype(BF16)
    a_low = (a - a_high.astype(F32)).astype(BF16)
    dot = functools.partial(jnp.dot, preferred_element_type=F32)
    return dot(a_high, high) + (dot(a_low, high) + dot(a_high, low))


def start_kernel(height, equilibrium, east, north, depth, mask, spread, floats, ints, sems):
    copies = [
        pltpu.make_async_copy(source, floats.at[i], sems.at[i])
        for i, source in enumerate((height, equilibrium, east, north, depth))
    ]
    copies.append(pltpu.make_async_copy(mask, ints, sems.at[5]))
    for copy in copies:
        copy.start()
    for copy in copies:
        copy.wait()
    ocean = ints[...] == 1
    for i in range(FIELDS):
        field = floats[i]
        if i in (0, FIELDS - 1):
            field = jnp.where(ocean, field, 0.0)
        for t in range(SHT):
            spread[t, ROWS * i : ROWS * (i + 1), :] = field


def degrees_of(half, y, k, tile):
    first = (half * PEERS + (y ^ k)) * CHUNK + tile * 8
    return pl.ds(pl.multiple_of(first, 8), 8)


def multiply_rows(half, y, weights, legendre, partial):
    wide = [
        [jnp.broadcast_to(weights[c, j : j + 1, :], (8, ORD)) for j in range(ROWS)]
        for c in range(2)
    ]

    def some(i, _):
        for k in range(PEERS):
            for n in range(2):
                tile = 2 * i + n
                degrees = degrees_of(half, y, k, tile)
                sums = [None, None]
                for j in range(ROWS):
                    p = legendre[j, degrees, :]
                    for c in range(2):
                        term = p * wide[c][j]
                        sums[c] = term if sums[c] is None else sums[c] + term
                for c in range(2):
                    partial[k, c, pl.ds(pl.multiple_of(8 * tile, 8), 8), :] = sums[c]
        return 0

    lax.fori_loop(0, CHUNK // 16, some, 0)


def transform_kernel(sht, core, y, level, turns, table, legendre, partial, spectra):
    z = level[:, 0:ROWS, :].reshape(SHT * ROWS, COLS)
    c, s = turns[0, pl.ds(sht[0], 1), :COLS], turns[1, pl.ds(sht[0], 1), :COLS]
    a = jnp.concatenate([z * c, z * -s], 0)
    out = dot3(a, table[0], table[1]).reshape(2, SHT, ROWS, 2 * ORD)
    re = out[0, :, :, :ORD] + out[1, :, :, ORD:]
    im = out[1, :, :, :ORD] - out[0, :, :, ORD:]
    c, s = turns[0, :, COLS:][:, None, :], turns[1, :, COLS:][:, None, :]
    scale = 1.0 / NLON * (2.0 / (ROWS * OCEAN))
    spectra[0] = jnp.sum(re * c + im * s, axis=0) * scale
    spectra[1] = jnp.sum(im * c - re * s, axis=0) * scale
    multiply_rows(1 - core[0], y[0], spectra[...], legendre, partial)


def rows_kernel(core, y, spectra, legendre, partial):
    multiply_rows(core[0], y[0], spectra[...], legendre, partial)


def column_of(line):
    n = line.shape[1]
    row = lax.broadcasted_iota(jnp.int32, (n, n), 0)
    lane = lax.broadcasted_iota(jnp.int32, (n, n), 1)
    return jnp.sum(jnp.where(row == lane, line, 0.0), axis=1, keepdims=True)


def love_kernel(core, y, own, one, two, three, love, loaded):
    factor = column_of(love[pl.ds(core[0] * PEERS + y[0], 1), :])
    for c in range(2):
        loaded[c] = ((own[c] + one[c]) + (two[c] + three[c])) * factor


def add_degrees(half, y, before, coefs, legendre):
    def some(i, acc):
        acc = list(acc)
        for k in range(PEERS):
            for n in range(2):
                tile = 2 * i + n
                degrees = degrees_of(half, y, k, tile)
                at = pl.ds(pl.multiple_of(8 * tile, 8), 8)
                x = [coefs[k][c, at, :] for c in range(2)]
                for j in range(ROWS):
                    p = legendre[j, degrees, :]
                    for c in range(2):
                        acc[c * ROWS + j] = acc[c * ROWS + j] + p * x[c]
        return tuple(acc)

    return lax.fori_loop(0, CHUNK // 16, some, tuple(before))


def degrees_kernel(core, y, *refs):
    *coefs, legendre, sums = refs
    zero = jnp.zeros((8, ORD), F32)
    acc = add_degrees(core[0], y[0], [zero] * (2 * ROWS), coefs, legendre)
    for i in range(2 * ROWS):
        sums[i] = acc[i]


def finish_kernel(core, y, before, *refs):
    *coefs, legendre, spread, synth = refs
    acc = add_degrees(1 - core[0], y[0], [before[i] for i in range(2 * ROWS)], coefs, legendre)
    for i in range(2 * ROWS):
        synth[i : i + 1, :] = jnp.sum(acc[i], axis=0, keepdims=True)
    value = synth[...]
    for t in range(SHT):
        spread[t] = value


def potential_kernel(
    core, synth, turns, doubling, high, low, level, fields, *rest
):
    *sines, pot, to_core, to_chip, sides, edges = rest
    e = doubling[...]
    s0, s1 = synth[:, 0:ROWS, :] * e, synth[:, ROWS:, :] * e
    for t in range(SHT):
        rows = slice(SHT * ROWS * t, SHT * ROWS * (t + 1))
        c, s = turns[0, t : t + 1, COLS:][None], turns[1, t : t + 1, COLS:][None]
        sides[rows, :ORD] = (s0 * c - s1 * s).reshape(SHT * ROWS, ORD)
        sides[rows, ORD:] = (s0 * s + s1 * c).reshape(SHT * ROWS, ORD)
    g = dot3(sides[...], high[...], low[...]).reshape(SHT, SHT, ROWS, 2 * COLS)
    c, s = turns[0, :, :COLS][:, None, :], turns[1, :, :COLS][:, None, :]
    for t in range(SHT):
        sal = jnp.sum(g[t, :, :, :COLS] * c - g[t, :, :, COLS:] * s, axis=0)
        value = level[t, 0:ROWS, :] - sal - fields[t, ROWS : 2 * ROWS, :]
        cols = slice(COLS * t, COLS * (t + 1))
        pot[:, cols] = value
        edges[0, 0:2, cols] = value[0:2, :]
        edges[1, 0:2, cols] = value[ROWS - 2 :, :]
        if sines:
            for side, row in ((0, 0), (1, ROWS - 1)):
                for i in range(3):
                    at = ROWS * (i + 2) + row
                    edges[side, 2 + i : 3 + i, cols] = fields[t, at : at + 1, :]
    if sines:
        wide = column_of(sines[0][...])
        for side, row in ((0, 0), (1, ROWS - 1)):
            edges[side, 5:6, :] = jnp.broadcast_to(wide[row : row + 1, :], (1, NLON))
            edges[side, 6:8, :] = jnp.zeros((2, NLON), F32)
    first_core = core[0] == 0
    to_core[...] = jnp.where(first_core, edges[1], edges[0])
    to_chip[...] = jnp.where(first_core, edges[0], edges[1])


def above_and_below(core, from_core, from_chip):
    first_core = core[0] == 0
    a, b = from_core[...], from_chip[...]
    return jnp.where(first_core, b, a), jnp.where(first_core, a, b)


def advance(field, pot, above, below, u, v, depth, damping, east_coef, coriolis):
    field[0:8, :] = jnp.zeros((8, NLON), F32)
    field[24:32, :] = jnp.zeros((8, NLON), F32)
    field[6:8, :] = above
    field[8:24, :] = pot[...]
    field[24:26, :] = below
    p = field[...]
    plus_col = lambda x: pltpu.roll(x, NLON - 1, 1)
    minus_col = lambda x: pltpu.roll(x, 1, 1)
    plus_row = lambda x: pltpu.roll(x, EROWS - 1, 0)
    minus_row = lambda x: pltpu.roll(x, 1, 0)
    ec = east_coef[...]
    old_u, old_v, f, d = u[...], v[...], coriolis[...], damping[...]
    ocean = depth[...] > 0.0
    grad_east = ec * (plus_col(p) - minus_col(p))
    grad_north = COURANT * (plus_row(p) - minus_row(p))
    new_u = jnp.where(ocean, old_u + f * old_v - grad_east - d * old_u, 0.0)
    new_v = jnp.where(ocean, old_v - f * old_u - grad_north - d * old_v, 0.0)
    flux_u, flux_v = depth[...] * new_u, depth[...] * new_v
    div = ec * (plus_col(flux_u) - minus_col(flux_u)) + COURANT * (
        plus_row(flux_v) - minus_row(flux_v)
    )
    return new_u, new_v, div, ocean


INNER = slice(8, 24)


def store_level(out, level, div, ocean):
    for t in range(SHT):
        cols = slice(COLS * t, COLS * (t + 1))
        out[t] = jnp.where(ocean[INNER, cols], level[t, 0:ROWS, :] - div[INNER, cols], 0.0)


def first_step_kernel(
    core, pot, from_core, from_chip, fields, sines,
    u, v, level, depth, damping, east_coef, coriolis, field,
):
    above, below = above_and_below(core, from_core, from_chip)
    for i, out in enumerate((u, v, depth)):
        for halo in (0, EROWS - 8):
            out[halo : halo + 8, :] = jnp.zeros((8, NLON), F32)
        out[7:8, :] = above[2 + i : 3 + i, :]
        out[24:25, :] = below[2 + i : 3 + i, :]
        for t in range(SHT):
            at = ROWS * (i + 2)
            out[INNER, COLS * t : COLS * (t + 1)] = fields[t, at : at + ROWS, :]
    coriolis[...] = jnp.zeros_like(coriolis)
    coriolis[7:8, :] = above[5:6, :]
    coriolis[INNER, :] = jnp.broadcast_to(column_of(sines[...]), (ROWS, NLON))
    coriolis[24:25, :] = below[5:6, :]
    x = coriolis[...]
    coriolis[...] = ROTATION * x
    east_coef[...] = COURANT / jnp.sqrt(1.0 - x * x)
    damping[...] = FRICTION / jnp.where(depth[...] > 0.0, depth[...], 1.0)
    new_u, new_v, div, ocean = advance(
        field, pot, above[0:2], below[0:2], u, v, depth, damping, east_coef, coriolis
    )
    u[...] = new_u
    v[...] = new_v
    store_level(level, fields, div, ocean)


def step_kernel(
    core, pot, from_core, from_chip, old_level, old_u, old_v, depth, damping, east_coef, coriolis,
    u, v, level, field,
):
    above, below = above_and_below(core, from_core, from_chip)
    new_u, new_v, div, ocean = advance(
        field, pot, above, below, old_u, old_v, depth, damping, east_coef, coriolis
    )
    u[...] = new_u
    v[...] = new_v
    store_level(level, old_level, div, ocean)


def last_step_kernel(
    sht, core, pot, from_core, from_chip, old_level, old_u, old_v, depth, damping, east_coef, coriolis,
    level, u, v, field,
):
    above, below = above_and_below(core, from_core, from_chip)
    new_u, new_v, div, _ = advance(
        field, pot, above, below, old_u, old_v, depth, damping, east_coef, coriolis
    )
    own = pl.ds(pl.multiple_of(sht[0] * COLS, COLS), COLS)
    field[...] = new_u
    u[...] = field[INNER, own]
    field[...] = new_v
    v[...] = field[INNER, own]
    field[...] = div
    level[...] = jnp.where(depth[INNER, own] > 0.0, old_level[sht[0]] - field[INNER, own], 0.0)


def shape(*dims):
    return jax.ShapeDtypeStruct(dims, F32)


PARAMS = pltpu.CompilerParams(vmem_limit_bytes=16 * 1024 * 1024)
START_PARAMS = pltpu.CompilerParams(vmem_limit_bytes=60 * 1024 * 1024)
COST = pl.CostEstimate(flops=ROWS * LDEG * ORD * 2, bytes_accessed=5 << 20, transcendentals=0)
WHOLE = pl.BlockSpec(memory_space=pltpu.VMEM)
SCALAR = pl.BlockSpec(memory_space=pltpu.SMEM)
HBM = pl.BlockSpec(memory_space=pltpu.HBM)


def whole(kernel, out_shape, scalars, *args, scratch=(), cost=None):
    return pl.pallas_call(
        kernel,
        in_specs=[SCALAR] * len(scalars) + [WHOLE] * len(args),
        out_specs=[WHOLE] * len(out_shape),
        out_shape=out_shape,
        scratch_shapes=list(scratch),
        compiler_params=PARAMS,
        cost_estimate=cost,
    )(*scalars, *args)


def per_device(height, east, north, depth, equilibrium, mask, sines, legendre, love):
    analysis, (s_high, s_low), turns, doubling = tables()
    ocean = lax.axis_index("ocean").astype(jnp.int32)
    sht = lax.axis_index("sht").astype(jnp.int32).reshape(1)
    core = (ocean & 1).reshape(1)
    y = (ocean >> 3).reshape(1)
    sines = sines.reshape(1, ROWS)
    love = love.reshape(LDEG // CHUNK, CHUNK)

    def swap(x, k):
        return lax.ppermute(x, "ocean", [(i, i ^ k) for i in range(OCEAN)])

    def swap_ring(x, k):
        pairs = [
            (SHT * i + t, SHT * (i ^ k) + t)
            for i in range(OCEAN)
            for t in range(SHT)
            if CHUNK * ((i % 2) * PEERS + i // 8 + 1) > ORD * t
        ]
        return lax.ppermute(x, ("ocean", "sht"), pairs)

    along_y = (8, 16, 24)
    along_z = (2, 4, 6)
    chips = [(i, i + 1 if i % 2 else i - 1) for i in range(1, OCEAN - 1)]

    spread = pl.pallas_call(
        start_kernel,
        in_specs=[HBM] * 6,
        out_specs=WHOLE,
        out_shape=shape(SHT, FIELDS * ROWS, COLS),
        scratch_shapes=[
            pltpu.VMEM((FIELDS, ROWS, COLS), F32),
            pltpu.VMEM((ROWS, COLS), jnp.int32),
            pltpu.SemaphoreType.DMA((6,)),
        ],
        compiler_params=START_PARAMS,
    )(height, equilibrium, east, north, depth, mask)
    spread, sht, core, y = lax.optimization_barrier((spread, sht, core, y))
    fields = lax.all_to_all(spread, "sht", 0, 0, tiled=True)

    extended = shape(EROWS, NLON)
    block = shape(ROWS, COLS)
    partial = shape(PEERS, 2, CHUNK, ORD)
    field = [pltpu.VMEM((EROWS, NLON), F32)]
    level = fields
    for step in range(STEPS):
        given, spectra = whole(
            transform_kernel,
            [partial, shape(2, ROWS, ORD)],
            (sht, core, y),
            *(level, turns, analysis, legendre),
            cost=COST,
        )
        taken = swap(given, 1)
        (kept,) = whole(rows_kernel, [partial], (core, y), spectra, legendre, cost=COST)
        parts = [kept[k] + taken[k] for k in range(PEERS)]
        others = [swap(parts[k], along_y[k - 1]) for k in range(1, PEERS)]
        ring = (parts[0] + others[0]) + (others[1] + others[2])
        rings = [swap_ring(ring, k) for k in along_z]
        (coefs,) = whole(
            love_kernel, [shape(2, CHUNK, ORD)], (core, y), ring, *rings, love
        )
        own_coefs = [coefs] + [swap(coefs, k) for k in along_y]
        other_coefs = [swap(x, 1) for x in own_coefs]
        (sums,) = whole(
            degrees_kernel,
            [shape(2 * ROWS, 8, ORD)],
            (core, y),
            *(*own_coefs, legendre),
            cost=COST,
        )
        (synth_spread,) = whole(
            finish_kernel,
            [shape(SHT, 2 * ROWS, ORD)],
            (core, y),
            *(sums, *other_coefs, legendre),
            scratch=[pltpu.VMEM((2 * ROWS, ORD), F32)],
            cost=COST,
        )
        synth = lax.all_to_all(synth_spread, "sht", 0, 0, tiled=True)
        halo = 8 if step == 0 else 2
        pot, to_core, to_chip = whole(
            potential_kernel,
            [shape(ROWS, NLON), shape(halo, NLON), shape(halo, NLON)],
            (core,),
            *(synth, turns, doubling, s_high, s_low, level, fields),
            *([sines] if step == 0 else []),
            scratch=[
                pltpu.VMEM((SHT * SHT * ROWS, 2 * ORD), F32),
                pltpu.VMEM((2, halo, NLON), F32),
            ],
        )
        from_chip = lax.ppermute(to_chip, "ocean", chips)
        from_core = swap(to_core, 1)
        given = (pot, from_core, from_chip)
        if step == 0:
            u, v, level, *constants = whole(
                first_step_kernel,
                [extended, extended, shape(SHT, ROWS, COLS)] + [extended] * 4,
                (core,),
                *(*given, fields, sines),
                scratch=field,
            )
        elif step < STEPS - 1:
            u, v, level = whole(
                step_kernel,
                [extended, extended, shape(SHT, ROWS, COLS)],
                (core,),
                *(*given, level, u, v, *constants),
                scratch=field,
            )
        else:
            level, u, v = whole(
                last_step_kernel,
                [block] * 3,
                (sht, core),
                *(*given, level, u, v, *constants),
                scratch=field,
            )
    return level, u, v


def solution(mesh):
    in_specs = (
        P("ocean", "sht"),
        P("ocean", "sht"),
        P("ocean", "sht"),
        P("ocean", "sht"),
        P("ocean", "sht"),
        P("ocean", "sht"),
        P("ocean"),
        P("ocean", None, "sht"),
        P(),
    )
    out_specs = (P("ocean", "sht"), P("ocean", "sht"), P("ocean", "sht"))
    return jax.shard_map(
        per_device, mesh=mesh, in_specs=in_specs, out_specs=out_specs, check_vma=False
    )
```

time: 1300 us -> 217 us (0.17); the launches traced: 1280 us -> 216 us
  waiting for transfers between devices: 983 us -> 56.8 us
  matrix products: 116 us -> 0 us
  blocking collectives: 67.5 us -> 39.7 us
  Pallas kernels: 0 us -> 16.6 us
  between operations: 15 us -> 1.07 us
    psum x3 -> x0, waiting for transfers between devices: 870 us -> none  [per_device(): coefs = lax.psum(partial_coefs, 'ocean')]
    dot_general x12 -> x0, matrix products: 116 us -> none  [the longest x3 34.3 us: per_device(): synth = jnp.einsum('jlm,lcm->jcm', legendre, loaded, precision=HIGHEST)]
    reduce_scatter x3 -> x0, waiting for transfers between devices: 103 us -> none  [per_device(): lax.psum_scatter(partial_spectra, 'sht', scatter_dimension=1, tiled=True)]
    all_gather x3 -> x0, blocking collectives: 67.5 us -> none  [per_device(): lax.all_gather(flat_synth, 'sht', axis=1, tiled=True)]
    ppermute x24 -> x48, waiting for transfers between devices: 10.2 us -> 56.8 us  [the longest x36 24 us: swap(): return lax.ppermute(x, 'ocean', [(i, i ^ k) for i in range(OCEAN)])]
    all_to_all x0 -> x4, blocking collectives: none -> 39.7 us  [the longest x3 23.5 us: per_device(): synth = lax.all_to_all(synth_spread, 'sht', 0, 0, tiled=True)]
    pallas_call x0 -> x22, Pallas kernels: none -> 16.6 us  [the longest x21 14.8 us: whole(): pl.pallas_call(kernel, in_specs=[SCALAR] * len(scalars) + [WHOLE] * len(a...]
    ppermute x24 -> x48, starting transfers between devices: 87.6 us -> 96.5 us  [the longest x36 50.3 us: swap(): return lax.ppermute(x, 'ocean', [(i, i ^ k) for i in range(OCEAN)])]
  transfers between devices with their start and end apart: 30 -> 48, of which waited for: 18 -> 28; matrix products, arithmetic and copies ran while one was open for 1% -> 0% of each run, Pallas kernels for 0% -> 2%
where the time goes in v2:
time: 217 us; the launch traced here: 216 us
  starting transfers between devices  96.5 us (44%)
  waiting for transfers between devices  56.8 us (26%)
  blocking collectives  39.7 us (18%)
  Pallas kernels  16.6 us (8%)
  local copies, waits for them, and re-layouts  5.12 us (2%)
    ppermute x36, starting transfers between devices, swap(): return lax.ppermute(x, 'ocean', [(i, i ^ k) for i in range(OCEAN)])  50.3 us
    ppermute x9, starting transfers between devices, swap_ring(): return lax.ppermute(x, ('ocean', 'sht'), pairs)  37.2 us
    ppermute x36, waiting for transfers between devices, swap(): return lax.ppermute(x, 'ocean', [(i, i ^ k) for i in range(OCEAN)])  24 us
    all_to_all x3, blocking collectives, per_device(): synth = lax.all_to_all(synth_spread, 'sht', 0, 0, tiled=True)  23.5 us
    ppermute x9, waiting for transfers between devices, swap_ring(): return lax.ppermute(x, ('ocean', 'sht'), pairs)  22.7 us
    all_to_all x1, blocking collectives, per_device(): fields = lax.all_to_all(spread, 'sht', 0, 0, tiled=True)  16.2 us
    pallas_call x21, Pallas kernels, whole(): pl.pallas_call(kernel, in_specs=[SCALAR] * len(scalars) + [WHOLE] * len(a...  14.8 us
    ppermute x3, waiting for transfers between devices, per_device(): from_chip = lax.ppermute(to_chip, 'ocean', chips)  10.1 us
  transfers between devices with their start and end apart: 48, of which 28 were waited for; matrix products, arithmetic and copies ran while one was open for 0% of the time, Pallas kernels for 2%

profile of v2, /device:TPU:1, one launch (start us, length us, event | category | flops | bytes accessed | tf_op | source)
XLA Modules:
  0.0 216.1 jit_solution(1589083108239423042)
XLA Ops:
  2.4 16.2 %all_to_all.20.level.fields = f32[8,80,256]{2,1,0:T(8,128)S(1)} all-to-all(f32[8,80,256]{2,1,0:T(8,128)} %shard_map.157), channel_id=1, replica_groups=mesh['ocean'=32,'sht'=8] {'sht'}, dimensions={0} | all-to-all | bytes 1310720 | tf_op jit(solution)/shard_map/all_to_all | solution.py:377
  18.6 3.4 %copy-done = f32[16,1024,128]{2,1,0:T(8,128)S(1)} copy-done((f32[16,1024,128]{2,1,0:T(8,128)S(1)}, f32[16,1024,128]{2,1,0:T(8,128)}, u32[]{:S(2)}) %copy-start) | copy-done | bytes 8388632
  32.4 3.9 %collective-permute-done.3 = f32[2,128,128]{2,1,0:T(8,128)S(1)} collective-permute-done((f32[2,128,128]{2,1,0:T(8,128)S(1)}, f32[2,128,128]{2,1,0:T(8,128)S(1)}, u32[]{:S(2)}, u32[]{:S(2)}) %collective-permute-start.3) | collective-permute-done | bytes 131104 | tf_op jit(solution)/shard_map/ppermute | solution.py:349
  37.2 7.0 %collective-permute-start.6 = (f32[2,128,128]{2,1,0:T(8,128)S(1)}, f32[2,128,128]{2,1,0:T(8,128)S(1)}, u32[]{:S(2)}, u32[]{:S(2)}) collective-permute-start(f32[2,128,128]{2,1,0:T(8,128)S(1)} %fusion.17.own), channel_id=1, source_target_pairs={{0,48},{8,56},{9,57},{10,58},{11,59},{12,60},{16,32},{24,40},{25,4... | collective-permute-start | bytes 393224 | tf_op jit(solution)/shard_map/ppermute | solution.py:358
  44.2 3.1 %collective-permute-start.5 = (f32[2,128,128]{2,1,0:T(8,128)S(1)}, f32[2,128,128]{2,1,0:T(8,128)S(1)}, u32[]{:S(2)}, u32[]{:S(2)}) collective-permute-start(f32[2,128,128]{2,1,0:T(8,128)S(1)} %fusion.17.own), channel_id=1, source_target_pairs={{0,32},{8,40},{9,41},{10,42},{11,43},{12,44},{16,48},{24,56},{25,5... | collective-permute-start | bytes 393224 | tf_op jit(solution)/shard_map/ppermute | solution.py:358
  50.2 4.5 %collective-permute-done.5.two = f32[2,128,128]{2,1,0:T(8,128)S(1)} collective-permute-done((f32[2,128,128]{2,1,0:T(8,128)S(1)}, f32[2,128,128]{2,1,0:T(8,128)S(1)}, u32[]{:S(2)}, u32[]{:S(2)}) %collective-permute-start.5) | collective-permute-done | bytes 131104 | tf_op jit(solution)/shard_map/ppermute | solution.py:358
  57.2 4.8 %collective-permute-start.9 = (f32[2,128,128]{2,1,0:T(8,128)S(1)}, f32[2,128,128]{2,1,0:T(8,128)S(1)}, u32[]{:S(2)}, u32[]{:S(2)}) collective-permute-start(f32[2,128,128]{2,1,0:T(8,128)S(1)} %shard_map.160.refs_0_), channel_id=1, source_target_pairs={{0,192},{8,200},{16,208},{24,216},{32,224},{40,232},{48,240},{56,2... | collective-permute-start | bytes 393224 | tf_op jit(solution)/shard_map/ppermute | solution.py:349
  65.4 3.3 %collective-permute-start.13 = (f32[2,128,128]{2,1,0:T(8,128)S(1)}, f32[2,128,128]{2,1,0:T(8,128)S(1)}, u32[]{:S(2)}, u32[]{:S(2)}) collective-permute-start(f32[2,128,128]{2,1,0:T(8,128)S(1)} %collective-permute-done.9.refs_3_), channel_id=1, source_target_pairs={{0,8},{8,0},{16,24},{24,16},{32,40},{40,32},{48,56},{56,48},{64,72... | collective-permute-start | bytes 393224 | tf_op jit(solution)/shard_map/ppermute | solution.py:349
  72.9 7.8 %all_to_all.21.synth = f32[8,32,128]{2,1,0:T(8,128)S(1)} all-to-all(f32[8,32,128]{2,1,0:T(8,128)S(1)} %shard_map.162), channel_id=1, replica_groups=mesh['ocean'=32,'sht'=8] {'sht'}, dimensions={0} | all-to-all | bytes 262144 | tf_op jit(solution)/shard_map/all_to_all | solution.py:418
  86.1 4.4 %collective-permute-done.15.from_chip = f32[8,2048]{1,0:T(8,128)S(1)} collective-permute-done((f32[8,2048]{1,0:T(8,128)S(1)}, f32[8,2048]{1,0:T(8,128)S(1)}, u32[]{:S(2)}, u32[]{:S(2)}) %collective-permute-start.15) | collective-permute-done | bytes 65568 | tf_op jit(solution)/shard_map/ppermute | solution.py:431
  97.5 4.7 %collective-permute-done.19 = f32[2,128,128]{2,1,0:T(8,128)S(1)} collective-permute-done((f32[2,128,128]{2,1,0:T(8,128)S(1)}, f32[2,128,128]{2,1,0:T(8,128)S(1)}, u32[]{:S(2)}, u32[]{:S(2)}) %collective-permute-start.19) | collective-permute-done | bytes 131104 | tf_op jit(solution)/shard_map/ppermute | solution.py:349
  103.6 6.2 %collective-permute-start.22 = (f32[2,128,128]{2,1,0:T(8,128)S(1)}, f32[2,128,128]{2,1,0:T(8,128)S(1)}, u32[]{:S(2)}, u32[]{:S(2)}) collective-permute-start(f32[2,128,128]{2,1,0:T(8,128)S(1)} %fusion.11.own), channel_id=1, source_target_pairs={{0,48},{8,56},{9,57},{10,58},{11,59},{12,60},{16,32},{24,40},{25,4... | collective-permute-start | bytes 393224 | tf_op jit(solution)/shard_map/ppermute | solution.py:358
  109.8 3.1 %collective-permute-start.21 = (f32[2,128,128]{2,1,0:T(8,128)S(1)}, f32[2,128,128]{2,1,0:T(8,128)S(1)}, u32[]{:S(2)}, u32[]{:S(2)}) collective-permute-start(f32[2,128,128]{2,1,0:T(8,128)S(1)} %fusion.11.own), channel_id=1, source_target_pairs={{0,32},{8,40},{9,41},{10,42},{11,43},{12,44},{16,48},{24,56},{25,5... | collective-permute-start | bytes 393224 | tf_op jit(solution)/shard_map/ppermute | solution.py:358
  115.7 7.2 %collective-permute-done.21.two = f32[2,128,128]{2,1,0:T(8,128)S(1)} collective-permute-done((f32[2,128,128]{2,1,0:T(8,128)S(1)}, f32[2,128,128]{2,1,0:T(8,128)S(1)}, u32[]{:S(2)}, u32[]{:S(2)}) %collective-permute-start.21) | collective-permute-done | bytes 131104 | tf_op jit(solution)/shard_map/ppermute | solution.py:358
  135.8 7.8 %all_to_all.22.synth = f32[8,32,128]{2,1,0:T(8,128)S(1)} all-to-all(f32[8,32,128]{2,1,0:T(8,128)S(1)} %shard_map.169), channel_id=1, replica_groups=mesh['ocean'=32,'sht'=8] {'sht'}, dimensions={0} | all-to-all | bytes 262144 | tf_op jit(solution)/shard_map/all_to_all | solution.py:418
  146.2 3.8 %collective-permute-start.31 = (f32[2,2048]{1,0:T(2,128)S(1)}, f32[2,2048]{1,0:T(2,128)S(1)}, u32[]{:S(2)}, u32[]{:S(2)}) collective-permute-start(f32[2,2048]{1,0:T(2,128)S(1)} %get-tuple-element.46), channel_id=1, source_target_pairs={{8,16},{16,8},{24,32},{32,24},{40,48},{48,40},{56,64},{64,56},{72,... | collective-permute-start | bytes 49160 | tf_op jit(solution)/shard_map/ppermute | solution.py:431
  155.7 3.1 %collective-permute-start.35 = (f32[2,128,128]{2,1,0:T(8,128)S(1)}, f32[2,128,128]{2,1,0:T(8,128)S(1)}, u32[]{:S(2)}, u32[]{:S(2)}) collective-permute-start(f32[2,128,128]{2,1,0:T(8,128)S(1)} %get-tuple-element.61), channel_id=1, source_target_pairs={{0,192},{8,200},{16,208},{24,216},{32,224},{40,232},{48,240},{56,2... | collective-permute-start | bytes 393224 | tf_op jit(solution)/shard_map/ppermute | solution.py:349
  159.4 4.8 %collective-permute-done.35 = f32[2,128,128]{2,1,0:T(8,128)S(1)} collective-permute-done((f32[2,128,128]{2,1,0:T(8,128)S(1)}, f32[2,128,128]{2,1,0:T(8,128)S(1)}, u32[]{:S(2)}, u32[]{:S(2)}) %collective-permute-start.35) | collective-permute-done | bytes 131104 | tf_op jit(solution)/shard_map/ppermute | solution.py:349
  165.6 6.2 %collective-permute-start.38 = (f32[2,128,128]{2,1,0:T(8,128)S(1)}, f32[2,128,128]{2,1,0:T(8,128)S(1)}, u32[]{:S(2)}, u32[]{:S(2)}) collective-permute-start(f32[2,128,128]{2,1,0:T(8,128)S(1)} %fusion.5.own), channel_id=1, source_target_pairs={{0,48},{8,56},{9,57},{10,58},{11,59},{12,60},{16,32},{24,40},{25,4... | collective-permute-start | bytes 393224 | tf_op jit(solution)/shard_map/ppermute | solution.py:358
  171.8 3.6 %collective-permute-start.37 = (f32[2,128,128]{2,1,0:T(8,128)S(1)}, f32[2,128,128]{2,1,0:T(8,128)S(1)}, u32[]{:S(2)}, u32[]{:S(2)}) collective-permute-start(f32[2,128,128]{2,1,0:T(8,128)S(1)} %fusion.5.own), channel_id=1, source_target_pairs={{0,32},{8,40},{9,41},{10,42},{11,43},{12,44},{16,48},{24,56},{25,5... | collective-permute-start | bytes 393224 | tf_op jit(solution)/shard_map/ppermute | solution.py:358
  177.7 7.4 %collective-permute-done.37.two = f32[2,128,128]{2,1,0:T(8,128)S(1)} collective-permute-done((f32[2,128,128]{2,1,0:T(8,128)S(1)}, f32[2,128,128]{2,1,0:T(8,128)S(1)}, u32[]{:S(2)}, u32[]{:S(2)}) %collective-permute-start.37) | collective-permute-done | bytes 131104 | tf_op jit(solution)/shard_map/ppermute | solution.py:358
  191.8 4.2 %collective-permute-start.45 = (f32[2,128,128]{2,1,0:T(8,128)S(1)}, f32[2,128,128]{2,1,0:T(8,128)S(1)}, u32[]{:S(2)}, u32[]{:S(2)}) collective-permute-start(f32[2,128,128]{2,1,0:T(8,128)S(1)} %collective-permute-done.41.refs_3_), channel_id=1, source_target_pairs={{0,8},{8,0},{16,24},{24,16},{32,40},{40,32},{48,56},{56,48},{64,72... | collective-permute-start | bytes 393224 | tf_op jit(solution)/shard_map/ppermute | solution.py:349
  198.4 7.8 %all_to_all.23.synth = f32[8,32,128]{2,1,0:T(8,128)S(1)} all-to-all(f32[8,32,128]{2,1,0:T(8,128)S(1)} %shard_map.176), channel_id=1, replica_groups=mesh['ocean'=32,'sht'=8] {'sht'}, dimensions={0} | all-to-all | bytes 262144 | tf_op jit(solution)/shard_map/all_to_all | solution.py:418
  211.3 3.5 %collective-permute-done.47.from_chip = f32[2,2048]{1,0:T(2,128)S(1)} collective-permute-done((f32[2,2048]{1,0:T(2,128)S(1)}, f32[2,2048]{1,0:T(2,128)S(1)}, u32[]{:S(2)}, u32[]{:S(2)}) %collective-permute-start.47) | collective-permute-done | bytes 16416 | tf_op jit(solution)/shard_map/ppermute | solution.py:431
  (126 shorter events, 83.0 us)
Async XLA Ops:
  28.9 7.4 %collective-permute-start.3 = (f32[2,128,128]{2,1,0:T(8,128)S(1)}, f32[2,128,128]{2,1,0:T(8,128)S(1)}, u32[]{:S(2)}, u32[]{:S(2)}) collective-permute-start(f32[2,128,128]{2,1,0:T(8,128)S(1)} %get-tuple-element.67), channel_id=1, source_target_pairs={{0,192},{8,200},{16,208},{24,216},{32,224},{40,232},{48,240},{56,2... | collective-permute-start | bytes 393224 | tf_op jit(solution)/shard_map/ppermute | solution.py:349
  37.2 13.0 %collective-permute-start.6 = (f32[2,128,128]{2,1,0:T(8,128)S(1)}, f32[2,128,128]{2,1,0:T(8,128)S(1)}, u32[]{:S(2)}, u32[]{:S(2)}) collective-permute-start(f32[2,128,128]{2,1,0:T(8,128)S(1)} %fusion.17.own), channel_id=1, source_target_pairs={{0,48},{8,56},{9,57},{10,58},{11,59},{12,60},{16,32},{24,40},{25,4... | collective-permute-start | bytes 393224 | tf_op jit(solution)/shard_map/ppermute | solution.py:358
  44.2 10.5 %collective-permute-start.5 = (f32[2,128,128]{2,1,0:T(8,128)S(1)}, f32[2,128,128]{2,1,0:T(8,128)S(1)}, u32[]{:S(2)}, u32[]{:S(2)}) collective-permute-start(f32[2,128,128]{2,1,0:T(8,128)S(1)} %fusion.17.own), channel_id=1, source_target_pairs={{0,32},{8,40},{9,41},{10,42},{11,43},{12,44},{16,48},{24,56},{25,5... | collective-permute-start | bytes 393224 | tf_op jit(solution)/shard_map/ppermute | solution.py:358
  47.3 9.7 %collective-permute-start.4 = (f32[2,128,128]{2,1,0:T(8,128)S(1)}, f32[2,128,128]{2,1,0:T(8,128)S(1)}, u32[]{:S(2)}, u32[]{:S(2)}) collective-permute-start(f32[2,128,128]{2,1,0:T(8,128)S(1)} %fusion.17.own), channel_id=1, source_target_pairs={{0,16},{8,24},{9,25},{10,26},{11,27},{12,28},{16,0},{24,8},{25,9},... | collective-permute-start | bytes 393224 | tf_op jit(solution)/shard_map/ppermute | solution.py:358
  57.2 8.2 %collective-permute-start.9 = (f32[2,128,128]{2,1,0:T(8,128)S(1)}, f32[2,128,128]{2,1,0:T(8,128)S(1)}, u32[]{:S(2)}, u32[]{:S(2)}) collective-permute-start(f32[2,128,128]{2,1,0:T(8,128)S(1)} %shard_map.160.refs_0_), channel_id=1, source_target_pairs={{0,192},{8,200},{16,208},{24,216},{32,224},{40,232},{48,240},{56,2... | collective-permute-start | bytes 393224 | tf_op jit(solution)/shard_map/ppermute | solution.py:349
  62.0 6.7 %collective-permute-start.8 = (f32[2,128,128]{2,1,0:T(8,128)S(1)}, f32[2,128,128]{2,1,0:T(8,128)S(1)}, u32[]{:S(2)}, u32[]{:S(2)}) collective-permute-start(f32[2,128,128]{2,1,0:T(8,128)S(1)} %shard_map.160.refs_0_), channel_id=1, source_target_pairs={{0,128},{8,136},{16,144},{24,152},{32,160},{40,168},{48,176},{56,1... | collective-permute-start | bytes 393224 | tf_op jit(solution)/shard_map/ppermute | solution.py:349
  62.0 8.9 %collective-permute-start.7 = (f32[2,128,128]{2,1,0:T(8,128)S(1)}, f32[2,128,128]{2,1,0:T(8,128)S(1)}, u32[]{:S(2)}, u32[]{:S(2)}) collective-permute-start(f32[2,128,128]{2,1,0:T(8,128)S(1)} %shard_map.160.refs_0_), channel_id=1, source_target_pairs={{0,64},{8,72},{16,80},{24,88},{32,96},{40,104},{48,112},{56,120},{... | collective-permute-start | bytes 393224 | tf_op jit(solution)/shard_map/ppermute | solution.py:349
  62.7 8.9 %collective-permute-start.10 = (f32[2,128,128]{2,1,0:T(8,128)S(1)}, f32[2,128,128]{2,1,0:T(8,128)S(1)}, u32[]{:S(2)}, u32[]{:S(2)}) collective-permute-start(f32[2,128,128]{2,1,0:T(8,128)S(1)} %shard_map.160.refs_0_), channel_id=1, source_target_pairs={{0,8},{8,0},{16,24},{24,16},{32,40},{40,32},{48,56},{56,48},{64,72... | collective-permute-start | bytes 393224 | tf_op jit(solution)/shard_map/ppermute | solution.py:349
  83.3 7.2 %collective-permute-start.15 = (f32[8,2048]{1,0:T(8,128)S(1)}, f32[8,2048]{1,0:T(8,128)S(1)}, u32[]{:S(2)}, u32[]{:S(2)}) collective-permute-start(f32[8,2048]{1,0:T(8,128)S(1)} %get-tuple-element.40), channel_id=1, source_target_pairs={{8,16},{16,8},{24,32},{32,24},{40,48},{48,40},{56,64},{64,56},{72,... | collective-permute-start | bytes 196616 | tf_op jit(solution)/shard_map/ppermute | solution.py:431
  94.1 8.0 %collective-permute-start.19 = (f32[2,128,128]{2,1,0:T(8,128)S(1)}, f32[2,128,128]{2,1,0:T(8,128)S(1)}, u32[]{:S(2)}, u32[]{:S(2)}) collective-permute-start(f32[2,128,128]{2,1,0:T(8,128)S(1)} %get-tuple-element.64), channel_id=1, source_target_pairs={{0,192},{8,200},{16,208},{24,216},{32,224},{40,232},{48,240},{56,2... | collective-permute-start | bytes 393224 | tf_op jit(solution)/shard_map/ppermute | solution.py:349
  103.6 12.2 %collective-permute-start.22 = (f32[2,128,128]{2,1,0:T(8,128)S(1)}, f32[2,128,128]{2,1,0:T(8,128)S(1)}, u32[]{:S(2)}, u32[]{:S(2)}) collective-permute-start(f32[2,128,128]{2,1,0:T(8,128)S(1)} %fusion.11.own), channel_id=1, source_target_pairs={{0,48},{8,56},{9,57},{10,58},{11,59},{12,60},{16,32},{24,40},{25,4... | collective-permute-start | bytes 393224 | tf_op jit(solution)/shard_map/ppermute | solution.py:358
  109.8 13.1 %collective-permute-start.21 = (f32[2,128,128]{2,1,0:T(8,128)S(1)}, f32[2,128,128]{2,1,0:T(8,128)S(1)}, u32[]{:S(2)}, u32[]{:S(2)}) collective-permute-start(f32[2,128,128]{2,1,0:T(8,128)S(1)} %fusion.11.own), channel_id=1, source_target_pairs={{0,32},{8,40},{9,41},{10,42},{11,43},{12,44},{16,48},{24,56},{25,5... | collective-permute-start | bytes 393224 | tf_op jit(solution)/shard_map/ppermute | solution.py:358
  112.9 10.5 %collective-permute-start.20 = (f32[2,128,128]{2,1,0:T(8,128)S(1)}, f32[2,128,128]{2,1,0:T(8,128)S(1)}, u32[]{:S(2)}, u32[]{:S(2)}) collective-permute-start(f32[2,128,128]{2,1,0:T(8,128)S(1)} %fusion.11.own), channel_id=1, source_target_pairs={{0,16},{8,24},{9,25},{10,26},{11,27},{12,28},{16,0},{24,8},{25,9},... | collective-permute-start | bytes 393224 | tf_op jit(solution)/shard_map/ppermute | solution.py:358
  123.5 7.3 %collective-permute-start.25 = (f32[2,128,128]{2,1,0:T(8,128)S(1)}, f32[2,128,128]{2,1,0:T(8,128)S(1)}, u32[]{:S(2)}, u32[]{:S(2)}) collective-permute-start(f32[2,128,128]{2,1,0:T(8,128)S(1)} %shard_map.167.refs_0_), channel_id=1, source_target_pairs={{0,192},{8,200},{16,208},{24,216},{32,224},{40,232},{48,240},{56,2... | collective-permute-start | bytes 393224 | tf_op jit(solution)/shard_map/ppermute | solution.py:349
  124.0 9.5 %collective-permute-start.24 = (f32[2,128,128]{2,1,0:T(8,128)S(1)}, f32[2,128,128]{2,1,0:T(8,128)S(1)}, u32[]{:S(2)}, u32[]{:S(2)}) collective-permute-start(f32[2,128,128]{2,1,0:T(8,128)S(1)} %shard_map.167.refs_0_), channel_id=1, source_target_pairs={{0,128},{8,136},{16,144},{24,152},{32,160},{40,168},{48,176},{56,1... | collective-permute-start | bytes 393224 | tf_op jit(solution)/shard_map/ppermute | solution.py:349
  125.1 8.4 %collective-permute-start.23 = (f32[2,128,128]{2,1,0:T(8,128)S(1)}, f32[2,128,128]{2,1,0:T(8,128)S(1)}, u32[]{:S(2)}, u32[]{:S(2)}) collective-permute-start(f32[2,128,128]{2,1,0:T(8,128)S(1)} %shard_map.167.refs_0_), channel_id=1, source_target_pairs={{0,64},{8,72},{16,80},{24,88},{32,96},{40,104},{48,112},{56,120},{... | collective-permute-start | bytes 393224 | tf_op jit(solution)/shard_map/ppermute | solution.py:349
  126.8 8.0 %collective-permute-start.26 = (f32[2,128,128]{2,1,0:T(8,128)S(1)}, f32[2,128,128]{2,1,0:T(8,128)S(1)}, u32[]{:S(2)}, u32[]{:S(2)}) collective-permute-start(f32[2,128,128]{2,1,0:T(8,128)S(1)} %shard_map.167.refs_0_), channel_id=1, source_target_pairs={{0,8},{8,0},{16,24},{24,16},{32,40},{40,32},{48,56},{56,48},{64,72... | collective-permute-start | bytes 393224 | tf_op jit(solution)/shard_map/ppermute | solution.py:349
  155.7 8.6 %collective-permute-start.35 = (f32[2,128,128]{2,1,0:T(8,128)S(1)}, f32[2,128,128]{2,1,0:T(8,128)S(1)}, u32[]{:S(2)}, u32[]{:S(2)}) collective-permute-start(f32[2,128,128]{2,1,0:T(8,128)S(1)} %get-tuple-element.61), channel_id=1, source_target_pairs={{0,192},{8,200},{16,208},{24,216},{32,224},{40,232},{48,240},{56,2... | collective-permute-start | bytes 393224 | tf_op jit(solution)/shard_map/ppermute | solution.py:349
  165.6 12.2 %collective-permute-start.38 = (f32[2,128,128]{2,1,0:T(8,128)S(1)}, f32[2,128,128]{2,1,0:T(8,128)S(1)}, u32[]{:S(2)}, u32[]{:S(2)}) collective-permute-start(f32[2,128,128]{2,1,0:T(8,128)S(1)} %fusion.5.own), channel_id=1, source_target_pairs={{0,48},{8,56},{9,57},{10,58},{11,59},{12,60},{16,32},{24,40},{25,4... | collective-permute-start | bytes 393224 | tf_op jit(solution)/shard_map/ppermute | solution.py:358
  171.8 13.4 %collective-permute-start.37 = (f32[2,128,128]{2,1,0:T(8,128)S(1)}, f32[2,128,128]{2,1,0:T(8,128)S(1)}, u32[]{:S(2)}, u32[]{:S(2)}) collective-permute-start(f32[2,128,128]{2,1,0:T(8,128)S(1)} %fusion.5.own), channel_id=1, source_target_pairs={{0,32},{8,40},{9,41},{10,42},{11,43},{12,44},{16,48},{24,56},{25,5... | collective-permute-start | bytes 393224 | tf_op jit(solution)/shard_map/ppermute | solution.py:358
  175.4 10.6 %collective-permute-start.36 = (f32[2,128,128]{2,1,0:T(8,128)S(1)}, f32[2,128,128]{2,1,0:T(8,128)S(1)}, u32[]{:S(2)}, u32[]{:S(2)}) collective-permute-start(f32[2,128,128]{2,1,0:T(8,128)S(1)} %fusion.5.own), channel_id=1, source_target_pairs={{0,16},{8,24},{9,25},{10,26},{11,27},{12,28},{16,0},{24,8},{25,9},... | collective-permute-start | bytes 393224 | tf_op jit(solution)/shard_map/ppermute | solution.py:358
  187.5 8.4 %collective-permute-start.40 = (f32[2,128,128]{2,1,0:T(8,128)S(1)}, f32[2,128,128]{2,1,0:T(8,128)S(1)}, u32[]{:S(2)}, u32[]{:S(2)}) collective-permute-start(f32[2,128,128]{2,1,0:T(8,128)S(1)} %shard_map.174.refs_0_), channel_id=1, source_target_pairs={{0,128},{8,136},{16,144},{24,152},{32,160},{40,168},{48,176},{56,1... | collective-permute-start | bytes 393224 | tf_op jit(solution)/shard_map/ppermute | solution.py:349
  188.0 8.2 %collective-permute-start.39 = (f32[2,128,128]{2,1,0:T(8,128)S(1)}, f32[2,128,128]{2,1,0:T(8,128)S(1)}, u32[]{:S(2)}, u32[]{:S(2)}) collective-permute-start(f32[2,128,128]{2,1,0:T(8,128)S(1)} %shard_map.174.refs_0_), channel_id=1, source_target_pairs={{0,64},{8,72},{16,80},{24,88},{32,96},{40,104},{48,112},{56,120},{... | collective-permute-start | bytes 393224 | tf_op jit(solution)/shard_map/ppermute | solution.py:349
  189.4 8.0 %collective-permute-start.42 = (f32[2,128,128]{2,1,0:T(8,128)S(1)}, f32[2,128,128]{2,1,0:T(8,128)S(1)}, u32[]{:S(2)}, u32[]{:S(2)}) collective-permute-start(f32[2,128,128]{2,1,0:T(8,128)S(1)} %shard_map.174.refs_0_), channel_id=1, source_target_pairs={{0,8},{8,0},{16,24},{24,16},{32,40},{40,32},{48,56},{56,48},{64,72... | collective-permute-start | bytes 393224 | tf_op jit(solution)/shard_map/ppermute | solution.py:349
  (35 other events, 280.3 us)

commit v3 on v2

--- a/solution.py
+++ b/solution.py
@@ -136,10 +136,10 @@
     return jnp.sum(jnp.where(row == lane, line, 0.0), axis=1, keepdims=True)
 
 
-def love_kernel(core, y, own, one, two, three, love, loaded):
+def love_kernel(core, y, cosine_sums, one, sine_sums, two, love, loaded):
     factor = column_of(love[pl.ds(core[0] * PEERS + y[0], 1), :])
-    for c in range(2):
-        loaded[c] = ((own[c] + one[c]) + (two[c] + three[c])) * factor
+    loaded[0] = (cosine_sums[...] + one[...]) * factor
+    loaded[1] = (sine_sums[...] + two[...]) * factor
 
 
 def add_degrees(half, y, before, coefs, legendre):
@@ -349,17 +349,15 @@
         return lax.ppermute(x, "ocean", [(i, i ^ k) for i in range(OCEAN)])
 
     def swap_ring(x, k):
-        pairs = [
-            (SHT * i + t, SHT * (i ^ k) + t)
-            for i in range(OCEAN)
-            for t in range(SHT)
-            if CHUNK * ((i % 2) * PEERS + i // 8 + 1) > ORD * t
-        ]
+        pairs = []
+        for i in range(OCEAN):
+            for t in range(SHT):
+                zeros = i % 2 == 0 and ORD * t >= LDEG // 2
+                pairs.append((SHT * i + t, SHT * (i ^ (8 * k if zeros else 2 * k)) + t))
         return lax.ppermute(x, ("ocean", "sht"), pairs)
 
     along_y = (8, 16, 24)
-    along_z = (2, 4, 6)
-    chips = [(i, i + 1 if i % 2 else i - 1) for i in range(1, OCEAN - 1)]
+    chips = [(i, (i + 1 if i % 2 else i - 1) % OCEAN) for i in range(OCEAN)]
 
     spread = pl.pallas_call(
         start_kernel,
@@ -394,9 +392,15 @@
         parts = [kept[k] + taken[k] for k in range(PEERS)]
         others = [swap(parts[k], along_y[k - 1]) for k in range(1, PEERS)]
         ring = (parts[0] + others[0]) + (others[1] + others[2])
-        rings = [swap_ring(ring, k) for k in along_z]
+        cosine_sums, sine_sums = ring[0], ring[1]
+        one, two = swap_ring(cosine_sums, 1), swap_ring(sine_sums, 3)
+        cosine_sums, sine_sums = cosine_sums + one, sine_sums + two
+        one, two = swap_ring(cosine_sums, 3), swap_ring(sine_sums, 1)
         (coefs,) = whole(
-            love_kernel, [shape(2, CHUNK, ORD)], (core, y), ring, *rings, love
+            love_kernel,
+            [shape(2, CHUNK, ORD)],
+            (core, y),
+            *(cosine_sums, one, sine_sums, two, love),
         )
         own_coefs = [coefs] + [swap(coefs, k) for k in along_y]
         other_coefs = [swap(x, 1) for x in own_coefs]

time: 217 us -> 201 us (0.926)
  starting transfers between devices: 96.5 us -> 86.8 us
  waiting for transfers between devices: 56.8 us -> 50 us
    ppermute x9 -> x12, starting transfers between devices: 37.2 us -> 16.8 us  [swap_ring(): return lax.ppermute(x, ('ocean', 'sht'), pairs)]
    ppermute x36, starting transfers between devices: 50.3 us -> 63.5 us  [swap(): return lax.ppermute(x, 'ocean', [(i, i ^ k) for i in range(OCEAN)])]
    ppermute x36, waiting for transfers between devices: 24 us -> 19.8 us  [swap(): return lax.ppermute(x, 'ocean', [(i, i ^ k) for i in range(OCEAN)])]
    ppermute x3, waiting for transfers between devices: 10.1 us -> 6.97 us  [per_device(): from_chip = lax.ppermute(to_chip, 'ocean', chips)]
    ppermute x3, starting transfers between devices: 8.96 us -> 6.46 us  [per_device(): from_chip = lax.ppermute(to_chip, 'ocean', chips)]
    ppermute x9 -> x12, waiting for transfers between devices: 22.7 us -> 23.2 us  [swap_ring(): return lax.ppermute(x, ('ocean', 'sht'), pairs)]
  transfers between devices with their start and end apart: 48 -> 51, of which waited for: 28 -> 24; matrix products, arithmetic and copies ran while one was open for 0% -> 0% of each run, Pallas kernels for 2% -> 2%
where the time goes in v3:
time: 201 us; the launch traced here: 200 us
  starting transfers between devices  86.8 us (43%)
  waiting for transfers between devices  50 us (25%)
  blocking collectives  39.8 us (20%)
  Pallas kernels  16.5 us (8%)
  local copies, waits for them, and re-layouts  5.15 us (3%)
    ppermute x36, starting transfers between devices, swap(): return lax.ppermute(x, 'ocean', [(i, i ^ k) for i in range(OCEAN)])  63.5 us
    all_to_all x3, blocking collectives, per_device(): synth = lax.all_to_all(synth_spread, 'sht', 0, 0, tiled=True)  23.7 us
    ppermute x12, waiting for transfers between devices, swap_ring(): return lax.ppermute(x, ('ocean', 'sht'), pairs)  23.2 us
    ppermute x36, waiting for transfers between devices, swap(): return lax.ppermute(x, 'ocean', [(i, i ^ k) for i in range(OCEAN)])  19.8 us
    ppermute x12, starting transfers between devices, swap_ring(): return lax.ppermute(x, ('ocean', 'sht'), pairs)  16.8 us
    all_to_all x1, blocking collectives, per_device(): fields = lax.all_to_all(spread, 'sht', 0, 0, tiled=True)  16.2 us
    pallas_call x21, Pallas kernels, whole(): pl.pallas_call(kernel, in_specs=[SCALAR] * len(scalars) + [WHOLE] * len(a...  14.8 us
    ppermute x3, waiting for transfers between devices, per_device(): from_chip = lax.ppermute(to_chip, 'ocean', chips)  6.97 us
  transfers between devices with their start and end apart: 51, of which 24 were waited for; matrix products, arithmetic and copies ran while one was open for 0% of the time, Pallas kernels for 2%

profile of v3, /device:TPU:1, one launch (start us, length us, event | category | flops | bytes accessed | tf_op | source)
XLA Modules:
  0.0 199.7 jit_solution(17497765622343273445)
XLA Ops:
  2.4 16.2 %all_to_all.20.level.fields = f32[8,80,256]{2,1,0:T(8,128)S(1)} all-to-all(f32[8,80,256]{2,1,0:T(8,128)} %shard_map.157), channel_id=1, replica_groups=mesh['ocean'=32,'sht'=8] {'sht'}, dimensions={0} | all-to-all | bytes 1310720 | tf_op jit(solution)/shard_map/all_to_all | solution.py:375
  18.6 3.4 %copy-done = f32[16,1024,128]{2,1,0:T(8,128)S(1)} copy-done((f32[16,1024,128]{2,1,0:T(8,128)S(1)}, f32[16,1024,128]{2,1,0:T(8,128)}, u32[]{:S(2)}) %copy-start) | copy-done | bytes 8388632
  24.6 2.6 %collective-permute-start = (f32[4,2,128,128]{3,2,1,0:T(8,128)S(1)}, f32[4,2,128,128]{3,2,1,0:T(8,128)S(1)}, u32[]{:S(2)}, u32[]{:S(2)}) collective-permute-start(f32[4,2,128,128]{3,2,1,0:T(8,128)S(1)} %get-tuple-element.37), channel_id=1, source_target_pairs={{0,8},{8,0},{16,24},{24,16},{32,40},{40,32},{48,56},{56,48},{64,72... | collective-permute-start | bytes 1572872 | tf_op jit(solution)/shard_map/ppermute | solution.py:349
  28.8 2.8 %collective-permute-start.3 = (f32[2,128,128]{2,1,0:T(8,128)S(1)}, f32[2,128,128]{2,1,0:T(8,128)S(1)}, u32[]{:S(2)}, u32[]{:S(2)}) collective-permute-start(f32[2,128,128]{2,1,0:T(8,128)S(1)} %get-tuple-element.67), channel_id=1, source_target_pairs={{0,192},{8,200},{16,208},{24,216},{32,224},{40,232},{48,240},{56,2... | collective-permute-start | bytes 393224 | tf_op jit(solution)/shard_map/ppermute | solution.py:349
  32.3 3.9 %collective-permute-done.3 = f32[2,128,128]{2,1,0:T(8,128)S(1)} collective-permute-done((f32[2,128,128]{2,1,0:T(8,128)S(1)}, f32[2,128,128]{2,1,0:T(8,128)S(1)}, u32[]{:S(2)}, u32[]{:S(2)}) %collective-permute-start.3) | collective-permute-done | bytes 131104 | tf_op jit(solution)/shard_map/ppermute | solution.py:349
  37.2 5.2 %collective-permute-start.6 = (f32[128,128]{1,0:T(8,128)S(1)}, f32[128,128]{1,0:T(8,128)S(1)}, u32[]{:S(2)}, u32[]{:S(2)}) collective-permute-start(f32[128,128]{1,0:T(8,128)S(1)} %get-tuple-element.80), channel_id=1, source_target_pairs={{0,48},{1,49},{2,50},{3,51},{4,196},{5,197},{6,198},{7,199},{8,56}... | collective-permute-start | bytes 196616 | tf_op jit(solution)/shard_map/ppermute | solution.py:357
  44.3 3.1 %collective-permute-done.4 = f32[128,128]{1,0:T(8,128)S(1)} collective-permute-done((f32[128,128]{1,0:T(8,128)S(1)}, f32[128,128]{1,0:T(8,128)S(1)}, u32[]{:S(2)}, u32[]{:S(2)}) %collective-permute-start.4) | collective-permute-done | bytes 65568 | tf_op jit(solution)/shard_map/ppermute | solution.py:357
  48.9 3.1 %collective-permute-done.7.two = f32[128,128]{1,0:T(8,128)S(1)} collective-permute-done((f32[128,128]{1,0:T(8,128)S(1)}, f32[128,128]{1,0:T(8,128)S(1)}, u32[]{:S(2)}, u32[]{:S(2)}) %collective-permute-start.7) | collective-permute-done | bytes 65568 | tf_op jit(solution)/shard_map/ppermute | solution.py:357
  53.1 3.8 %collective-permute-start.10 = (f32[2,128,128]{2,1,0:T(8,128)S(1)}, f32[2,128,128]{2,1,0:T(8,128)S(1)}, u32[]{:S(2)}, u32[]{:S(2)}) collective-permute-start(f32[2,128,128]{2,1,0:T(8,128)S(1)} %shard_map.160.refs_0_), channel_id=1, source_target_pairs={{0,192},{8,200},{16,208},{24,216},{32,224},{40,232},{48,240},{56,2... | collective-permute-start | bytes 393224 | tf_op jit(solution)/shard_map/ppermute | solution.py:349
  57.6 6.6 %collective-permute-start.11 = (f32[2,128,128]{2,1,0:T(8,128)S(1)}, f32[2,128,128]{2,1,0:T(8,128)S(1)}, u32[]{:S(2)}, u32[]{:S(2)}) collective-permute-start(f32[2,128,128]{2,1,0:T(8,128)S(1)} %shard_map.160.refs_0_), channel_id=1, source_target_pairs={{0,8},{8,0},{16,24},{24,16},{32,40},{40,32},{48,56},{56,48},{64,72... | collective-permute-start | bytes 393224 | tf_op jit(solution)/shard_map/ppermute | solution.py:349
  70.2 7.8 %all_to_all.21.synth = f32[8,32,128]{2,1,0:T(8,128)S(1)} all-to-all(f32[8,32,128]{2,1,0:T(8,128)S(1)} %shard_map.162), channel_id=1, replica_groups=mesh['ocean'=32,'sht'=8] {'sht'}, dimensions={0} | all-to-all | bytes 262144 | tf_op jit(solution)/shard_map/all_to_all | solution.py:422
  82.4 3.6 %collective-permute-done.16.from_chip = f32[8,2048]{1,0:T(8,128)S(1)} collective-permute-done((f32[8,2048]{1,0:T(8,128)S(1)}, f32[8,2048]{1,0:T(8,128)S(1)}, u32[]{:S(2)}, u32[]{:S(2)}) %collective-permute-start.16) | collective-permute-done | bytes 65568 | tf_op jit(solution)/shard_map/ppermute | solution.py:435
  87.6 3.0 %collective-permute-start.17 = (f32[4,2,128,128]{3,2,1,0:T(8,128)S(1)}, f32[4,2,128,128]{3,2,1,0:T(8,128)S(1)}, u32[]{:S(2)}, u32[]{:S(2)}) collective-permute-start(f32[4,2,128,128]{3,2,1,0:T(8,128)S(1)} %get-tuple-element.43), channel_id=1, source_target_pairs={{0,8},{8,0},{16,24},{24,16},{32,40},{40,32},{48,56},{56,48},{64,72... | collective-permute-start | bytes 1572872 | tf_op jit(solution)/shard_map/ppermute | solution.py:349
  95.5 5.8 %collective-permute-done.20 = f32[2,128,128]{2,1,0:T(8,128)S(1)} collective-permute-done((f32[2,128,128]{2,1,0:T(8,128)S(1)}, f32[2,128,128]{2,1,0:T(8,128)S(1)}, u32[]{:S(2)}, u32[]{:S(2)}) %collective-permute-start.20) | collective-permute-done | bytes 131104 | tf_op jit(solution)/shard_map/ppermute | solution.py:349
  102.1 4.7 %collective-permute-done.23 = f32[128,128]{1,0:T(8,128)S(1)} collective-permute-done((f32[128,128]{1,0:T(8,128)S(1)}, f32[128,128]{1,0:T(8,128)S(1)}, u32[]{:S(2)}, u32[]{:S(2)}) %collective-permute-start.23) | collective-permute-done | bytes 65568 | tf_op jit(solution)/shard_map/ppermute | solution.py:357
  107.5 2.5 %collective-permute-start.22 = (f32[128,128]{1,0:T(8,128)S(1)}, f32[128,128]{1,0:T(8,128)S(1)}, u32[]{:S(2)}, u32[]{:S(2)}) collective-permute-start(f32[128,128]{1,0:T(8,128)S(1)} %get-tuple-element.75.cosine_sums), channel_id=1, source_target_pairs={{0,48},{1,49},{2,50},{3,51},{4,196},{5,197},{6,198},{7,199},{8,56}... | collective-permute-start | bytes 196616 | tf_op jit(solution)/shard_map/ppermute | solution.py:357
  116.3 4.4 %collective-permute-start.28 = (f32[2,128,128]{2,1,0:T(8,128)S(1)}, f32[2,128,128]{2,1,0:T(8,128)S(1)}, u32[]{:S(2)}, u32[]{:S(2)}) collective-permute-start(f32[2,128,128]{2,1,0:T(8,128)S(1)} %shard_map.167.refs_0_), channel_id=1, source_target_pairs={{0,8},{8,0},{16,24},{24,16},{32,40},{40,32},{48,56},{56,48},{64,72... | collective-permute-start | bytes 393224 | tf_op jit(solution)/shard_map/ppermute | solution.py:349
  126.7 8.0 %all_to_all.22.synth = f32[8,32,128]{2,1,0:T(8,128)S(1)} all-to-all(f32[8,32,128]{2,1,0:T(8,128)S(1)} %shard_map.169), channel_id=1, replica_groups=mesh['ocean'=32,'sht'=8] {'sht'}, dimensions={0} | all-to-all | bytes 262144 | tf_op jit(solution)/shard_map/all_to_all | solution.py:422
  137.2 2.5 %collective-permute-start.33 = (f32[2,2048]{1,0:T(2,128)S(1)}, f32[2,2048]{1,0:T(2,128)S(1)}, u32[]{:S(2)}, u32[]{:S(2)}) collective-permute-start(f32[2,2048]{1,0:T(2,128)S(1)} %get-tuple-element.46), channel_id=1, source_target_pairs={{0,248},{8,16},{16,8},{24,32},{32,24},{40,48},{48,40},{56,64},{64,... | collective-permute-start | bytes 49160 | tf_op jit(solution)/shard_map/ppermute | solution.py:435
  142.8 3.7 %collective-permute-start.34 = (f32[4,2,128,128]{3,2,1,0:T(8,128)S(1)}, f32[4,2,128,128]{3,2,1,0:T(8,128)S(1)}, u32[]{:S(2)}, u32[]{:S(2)}) collective-permute-start(f32[4,2,128,128]{3,2,1,0:T(8,128)S(1)} %get-tuple-element.55), channel_id=1, source_target_pairs={{0,8},{8,0},{16,24},{24,16},{32,40},{40,32},{48,56},{56,48},{64,72... | collective-permute-start | bytes 1572872 | tf_op jit(solution)/shard_map/ppermute | solution.py:349
  151.4 5.8 %collective-permute-done.37 = f32[2,128,128]{2,1,0:T(8,128)S(1)} collective-permute-done((f32[2,128,128]{2,1,0:T(8,128)S(1)}, f32[2,128,128]{2,1,0:T(8,128)S(1)}, u32[]{:S(2)}, u32[]{:S(2)}) %collective-permute-start.37) | collective-permute-done | bytes 131104 | tf_op jit(solution)/shard_map/ppermute | solution.py:349
  159.9 2.7 %collective-permute-done.40 = f32[128,128]{1,0:T(8,128)S(1)} collective-permute-done((f32[128,128]{1,0:T(8,128)S(1)}, f32[128,128]{1,0:T(8,128)S(1)}, u32[]{:S(2)}, u32[]{:S(2)}) %collective-permute-start.40) | collective-permute-done | bytes 65568 | tf_op jit(solution)/shard_map/ppermute | solution.py:357
  173.7 4.2 %collective-permute-start.45 = (f32[2,128,128]{2,1,0:T(8,128)S(1)}, f32[2,128,128]{2,1,0:T(8,128)S(1)}, u32[]{:S(2)}, u32[]{:S(2)}) collective-permute-start(f32[2,128,128]{2,1,0:T(8,128)S(1)} %shard_map.174.refs_0_), channel_id=1, source_target_pairs={{0,8},{8,0},{16,24},{24,16},{32,40},{40,32},{48,56},{56,48},{64,72... | collective-permute-start | bytes 393224 | tf_op jit(solution)/shard_map/ppermute | solution.py:349
  183.9 7.8 %all_to_all.23.synth = f32[8,32,128]{2,1,0:T(8,128)S(1)} all-to-all(f32[8,32,128]{2,1,0:T(8,128)S(1)} %shard_map.176), channel_id=1, replica_groups=mesh['ocean'=32,'sht'=8] {'sht'}, dimensions={0} | all-to-all | bytes 262144 | tf_op jit(solution)/shard_map/all_to_all | solution.py:422
  (138 shorter events, 81.4 us)
Async XLA Ops:
  28.8 7.4 %collective-permute-start.3 = (f32[2,128,128]{2,1,0:T(8,128)S(1)}, f32[2,128,128]{2,1,0:T(8,128)S(1)}, u32[]{:S(2)}, u32[]{:S(2)}) collective-permute-start(f32[2,128,128]{2,1,0:T(8,128)S(1)} %get-tuple-element.67), channel_id=1, source_target_pairs={{0,192},{8,200},{16,208},{24,216},{32,224},{40,232},{48,240},{56,2... | collective-permute-start | bytes 393224 | tf_op jit(solution)/shard_map/ppermute | solution.py:349
  31.7 5.4 %collective-permute-start.2 = (f32[2,128,128]{2,1,0:T(8,128)S(1)}, f32[2,128,128]{2,1,0:T(8,128)S(1)}, u32[]{:S(2)}, u32[]{:S(2)}) collective-permute-start(f32[2,128,128]{2,1,0:T(8,128)S(1)} %get-tuple-element.68), channel_id=1, source_target_pairs={{0,128},{8,136},{16,144},{24,152},{32,160},{40,168},{48,176},{56,1... | collective-permute-start | bytes 393224 | tf_op jit(solution)/shard_map/ppermute | solution.py:349
  37.2 7.1 %collective-permute-start.6 = (f32[128,128]{1,0:T(8,128)S(1)}, f32[128,128]{1,0:T(8,128)S(1)}, u32[]{:S(2)}, u32[]{:S(2)}) collective-permute-start(f32[128,128]{1,0:T(8,128)S(1)} %get-tuple-element.80), channel_id=1, source_target_pairs={{0,48},{1,49},{2,50},{3,51},{4,196},{5,197},{6,198},{7,199},{8,56}... | collective-permute-start | bytes 196616 | tf_op jit(solution)/shard_map/ppermute | solution.py:357
  53.1 11.1 %collective-permute-start.10 = (f32[2,128,128]{2,1,0:T(8,128)S(1)}, f32[2,128,128]{2,1,0:T(8,128)S(1)}, u32[]{:S(2)}, u32[]{:S(2)}) collective-permute-start(f32[2,128,128]{2,1,0:T(8,128)S(1)} %shard_map.160.refs_0_), channel_id=1, source_target_pairs={{0,192},{8,200},{16,208},{24,216},{32,224},{40,232},{48,240},{56,2... | collective-permute-start | bytes 393224 | tf_op jit(solution)/shard_map/ppermute | solution.py:349
  56.9 9.4 %collective-permute-start.9 = (f32[2,128,128]{2,1,0:T(8,128)S(1)}, f32[2,128,128]{2,1,0:T(8,128)S(1)}, u32[]{:S(2)}, u32[]{:S(2)}) collective-permute-start(f32[2,128,128]{2,1,0:T(8,128)S(1)} %shard_map.160.refs_0_), channel_id=1, source_target_pairs={{0,128},{8,136},{16,144},{24,152},{32,160},{40,168},{48,176},{56,1... | collective-permute-start | bytes 393224 | tf_op jit(solution)/shard_map/ppermute | solution.py:349
  56.9 11.0 %collective-permute-start.8 = (f32[2,128,128]{2,1,0:T(8,128)S(1)}, f32[2,128,128]{2,1,0:T(8,128)S(1)}, u32[]{:S(2)}, u32[]{:S(2)}) collective-permute-start(f32[2,128,128]{2,1,0:T(8,128)S(1)} %shard_map.160.refs_0_), channel_id=1, source_target_pairs={{0,64},{8,72},{16,80},{24,88},{32,96},{40,104},{48,112},{56,120},{... | collective-permute-start | bytes 393224 | tf_op jit(solution)/shard_map/ppermute | solution.py:349
  57.6 11.6 %collective-permute-start.11 = (f32[2,128,128]{2,1,0:T(8,128)S(1)}, f32[2,128,128]{2,1,0:T(8,128)S(1)}, u32[]{:S(2)}, u32[]{:S(2)}) collective-permute-start(f32[2,128,128]{2,1,0:T(8,128)S(1)} %shard_map.160.refs_0_), channel_id=1, source_target_pairs={{0,8},{8,0},{16,24},{24,16},{32,40},{40,32},{48,56},{56,48},{64,72... | collective-permute-start | bytes 393224 | tf_op jit(solution)/shard_map/ppermute | solution.py:349
  92.2 9.2 %collective-permute-start.20 = (f32[2,128,128]{2,1,0:T(8,128)S(1)}, f32[2,128,128]{2,1,0:T(8,128)S(1)}, u32[]{:S(2)}, u32[]{:S(2)}) collective-permute-start(f32[2,128,128]{2,1,0:T(8,128)S(1)} %get-tuple-element.64), channel_id=1, source_target_pairs={{0,192},{8,200},{16,208},{24,216},{32,224},{40,232},{48,240},{56,2... | collective-permute-start | bytes 393224 | tf_op jit(solution)/shard_map/ppermute | solution.py:349
  92.3 9.0 %collective-permute-start.19 = (f32[2,128,128]{2,1,0:T(8,128)S(1)}, f32[2,128,128]{2,1,0:T(8,128)S(1)}, u32[]{:S(2)}, u32[]{:S(2)}) collective-permute-start(f32[2,128,128]{2,1,0:T(8,128)S(1)} %get-tuple-element.65), channel_id=1, source_target_pairs={{0,128},{8,136},{16,144},{24,152},{32,160},{40,168},{48,176},{56,1... | collective-permute-start | bytes 393224 | tf_op jit(solution)/shard_map/ppermute | solution.py:349
  93.2 8.2 %collective-permute-start.18 = (f32[2,128,128]{2,1,0:T(8,128)S(1)}, f32[2,128,128]{2,1,0:T(8,128)S(1)}, u32[]{:S(2)}, u32[]{:S(2)}) collective-permute-start(f32[2,128,128]{2,1,0:T(8,128)S(1)} %get-tuple-element.66), channel_id=1, source_target_pairs={{0,64},{8,72},{16,80},{24,88},{32,96},{40,104},{48,112},{56,120},{... | collective-permute-start | bytes 393224 | tf_op jit(solution)/shard_map/ppermute | solution.py:349
  101.4 5.3 %collective-permute-start.23 = (f32[128,128]{1,0:T(8,128)S(1)}, f32[128,128]{1,0:T(8,128)S(1)}, u32[]{:S(2)}, u32[]{:S(2)}) collective-permute-start(f32[128,128]{1,0:T(8,128)S(1)} %get-tuple-element.76), channel_id=1, source_target_pairs={{0,48},{1,49},{2,50},{3,51},{4,196},{5,197},{6,198},{7,199},{8,56}... | collective-permute-start | bytes 196616 | tf_op jit(solution)/shard_map/ppermute | solution.py:357
  107.5 5.3 %collective-permute-start.22 = (f32[128,128]{1,0:T(8,128)S(1)}, f32[128,128]{1,0:T(8,128)S(1)}, u32[]{:S(2)}, u32[]{:S(2)}) collective-permute-start(f32[128,128]{1,0:T(8,128)S(1)} %get-tuple-element.75.cosine_sums), channel_id=1, source_target_pairs={{0,48},{1,49},{2,50},{3,51},{4,196},{5,197},{6,198},{7,199},{8,56}... | collective-permute-start | bytes 196616 | tf_op jit(solution)/shard_map/ppermute | solution.py:357
  113.0 7.7 %collective-permute-start.27 = (f32[2,128,128]{2,1,0:T(8,128)S(1)}, f32[2,128,128]{2,1,0:T(8,128)S(1)}, u32[]{:S(2)}, u32[]{:S(2)}) collective-permute-start(f32[2,128,128]{2,1,0:T(8,128)S(1)} %shard_map.167.refs_0_), channel_id=1, source_target_pairs={{0,192},{8,200},{16,208},{24,216},{32,224},{40,232},{48,240},{56,2... | collective-permute-start | bytes 393224 | tf_op jit(solution)/shard_map/ppermute | solution.py:349
  114.4 8.3 %collective-permute-start.26 = (f32[2,128,128]{2,1,0:T(8,128)S(1)}, f32[2,128,128]{2,1,0:T(8,128)S(1)}, u32[]{:S(2)}, u32[]{:S(2)}) collective-permute-start(f32[2,128,128]{2,1,0:T(8,128)S(1)} %shard_map.167.refs_0_), channel_id=1, source_target_pairs={{0,128},{8,136},{16,144},{24,152},{32,160},{40,168},{48,176},{56,1... | collective-permute-start | bytes 393224 | tf_op jit(solution)/shard_map/ppermute | solution.py:349
  115.1 9.6 %collective-permute-start.25 = (f32[2,128,128]{2,1,0:T(8,128)S(1)}, f32[2,128,128]{2,1,0:T(8,128)S(1)}, u32[]{:S(2)}, u32[]{:S(2)}) collective-permute-start(f32[2,128,128]{2,1,0:T(8,128)S(1)} %shard_map.167.refs_0_), channel_id=1, source_target_pairs={{0,64},{8,72},{16,80},{24,88},{32,96},{40,104},{48,112},{56,120},{... | collective-permute-start | bytes 393224 | tf_op jit(solution)/shard_map/ppermute | solution.py:349
  116.3 9.3 %collective-permute-start.28 = (f32[2,128,128]{2,1,0:T(8,128)S(1)}, f32[2,128,128]{2,1,0:T(8,128)S(1)}, u32[]{:S(2)}, u32[]{:S(2)}) collective-permute-start(f32[2,128,128]{2,1,0:T(8,128)S(1)} %shard_map.167.refs_0_), channel_id=1, source_target_pairs={{0,8},{8,0},{16,24},{24,16},{32,40},{40,32},{48,56},{56,48},{64,72... | collective-permute-start | bytes 393224 | tf_op jit(solution)/shard_map/ppermute | solution.py:349
  148.1 9.2 %collective-permute-start.37 = (f32[2,128,128]{2,1,0:T(8,128)S(1)}, f32[2,128,128]{2,1,0:T(8,128)S(1)}, u32[]{:S(2)}, u32[]{:S(2)}) collective-permute-start(f32[2,128,128]{2,1,0:T(8,128)S(1)} %get-tuple-element.61), channel_id=1, source_target_pairs={{0,192},{8,200},{16,208},{24,216},{32,224},{40,232},{48,240},{56,2... | collective-permute-start | bytes 393224 | tf_op jit(solution)/shard_map/ppermute | solution.py:349
  148.2 9.1 %collective-permute-start.36 = (f32[2,128,128]{2,1,0:T(8,128)S(1)}, f32[2,128,128]{2,1,0:T(8,128)S(1)}, u32[]{:S(2)}, u32[]{:S(2)}) collective-permute-start(f32[2,128,128]{2,1,0:T(8,128)S(1)} %get-tuple-element.62), channel_id=1, source_target_pairs={{0,128},{8,136},{16,144},{24,152},{32,160},{40,168},{48,176},{56,1... | collective-permute-start | bytes 393224 | tf_op jit(solution)/shard_map/ppermute | solution.py:349
  149.0 8.3 %collective-permute-start.35 = (f32[2,128,128]{2,1,0:T(8,128)S(1)}, f32[2,128,128]{2,1,0:T(8,128)S(1)}, u32[]{:S(2)}, u32[]{:S(2)}) collective-permute-start(f32[2,128,128]{2,1,0:T(8,128)S(1)} %get-tuple-element.63), channel_id=1, source_target_pairs={{0,64},{8,72},{16,80},{24,88},{32,96},{40,104},{48,112},{56,120},{... | collective-permute-start | bytes 393224 | tf_op jit(solution)/shard_map/ppermute | solution.py:349
  157.3 5.3 %collective-permute-start.40 = (f32[128,128]{1,0:T(8,128)S(1)}, f32[128,128]{1,0:T(8,128)S(1)}, u32[]{:S(2)}, u32[]{:S(2)}) collective-permute-start(f32[128,128]{1,0:T(8,128)S(1)} %get-tuple-element.72), channel_id=1, source_target_pairs={{0,48},{1,49},{2,50},{3,51},{4,196},{5,197},{6,198},{7,199},{8,56}... | collective-permute-start | bytes 196616 | tf_op jit(solution)/shard_map/ppermute | solution.py:357
  170.4 7.5 %collective-permute-start.44 = (f32[2,128,128]{2,1,0:T(8,128)S(1)}, f32[2,128,128]{2,1,0:T(8,128)S(1)}, u32[]{:S(2)}, u32[]{:S(2)}) collective-permute-start(f32[2,128,128]{2,1,0:T(8,128)S(1)} %shard_map.174.refs_0_), channel_id=1, source_target_pairs={{0,192},{8,200},{16,208},{24,216},{32,224},{40,232},{48,240},{56,2... | collective-permute-start | bytes 393224 | tf_op jit(solution)/shard_map/ppermute | solution.py:349
  171.5 8.5 %collective-permute-start.43 = (f32[2,128,128]{2,1,0:T(8,128)S(1)}, f32[2,128,128]{2,1,0:T(8,128)S(1)}, u32[]{:S(2)}, u32[]{:S(2)}) collective-permute-start(f32[2,128,128]{2,1,0:T(8,128)S(1)} %shard_map.174.refs_0_), channel_id=1, source_target_pairs={{0,128},{8,136},{16,144},{24,152},{32,160},{40,168},{48,176},{56,1... | collective-permute-start | bytes 393224 | tf_op jit(solution)/shard_map/ppermute | solution.py:349
  171.8 9.9 %collective-permute-start.42 = (f32[2,128,128]{2,1,0:T(8,128)S(1)}, f32[2,128,128]{2,1,0:T(8,128)S(1)}, u32[]{:S(2)}, u32[]{:S(2)}) collective-permute-start(f32[2,128,128]{2,1,0:T(8,128)S(1)} %shard_map.174.refs_0_), channel_id=1, source_target_pairs={{0,64},{8,72},{16,80},{24,88},{32,96},{40,104},{48,112},{56,120},{... | collective-permute-start | bytes 393224 | tf_op jit(solution)/shard_map/ppermute | solution.py:349
  173.7 9.2 %collective-permute-start.45 = (f32[2,128,128]{2,1,0:T(8,128)S(1)}, f32[2,128,128]{2,1,0:T(8,128)S(1)}, u32[]{:S(2)}, u32[]{:S(2)}) collective-permute-start(f32[2,128,128]{2,1,0:T(8,128)S(1)} %shard_map.174.refs_0_), channel_id=1, source_target_pairs={{0,8},{8,0},{16,24},{24,16},{32,40},{40,32},{48,56},{56,48},{64,72... | collective-permute-start | bytes 393224 | tf_op jit(solution)/shard_map/ppermute | solution.py:349
  (38 other events, 291.5 us)

commit v4 on v3

--- a/solution.py
+++ b/solution.py
@@ -82,12 +82,11 @@
             spread[t, ROWS * i : ROWS * (i + 1), :] = field
 
 
-def degrees_of(half, y, k, tile):
-    first = (half * PEERS + (y ^ k)) * CHUNK + tile * 8
-    return pl.ds(pl.multiple_of(first, 8), 8)
-
-
-def multiply_rows(half, y, weights, legendre, partial):
+def degrees_of(y, k, tile):
+    return pl.ds(pl.multiple_of((y ^ k) * CHUNK + tile * 8, 8), 8)
+
+
+def multiply_rows(y, before, weights, legendre, partial):
     wide = [
         [jnp.broadcast_to(weights[c, j : j + 1, :], (8, ORD)) for j in range(ROWS)]
         for c in range(2)
@@ -97,21 +96,22 @@
         for k in range(PEERS):
             for n in range(2):
                 tile = 2 * i + n
-                degrees = degrees_of(half, y, k, tile)
-                sums = [None, None]
+                degrees = degrees_of(y, k, tile)
+                at = pl.ds(pl.multiple_of(8 * tile, 8), 8)
+                sums = [before[k][c, at, :] if before else None for c in range(2)]
                 for j in range(ROWS):
                     p = legendre[j, degrees, :]
                     for c in range(2):
                         term = p * wide[c][j]
                         sums[c] = term if sums[c] is None else sums[c] + term
                 for c in range(2):
-                    partial[k, c, pl.ds(pl.multiple_of(8 * tile, 8), 8), :] = sums[c]
+                    partial[k][c, at, :] = sums[c]
         return 0
 
     lax.fori_loop(0, CHUNK // 16, some, 0)
 
 
-def transform_kernel(sht, core, y, level, turns, table, legendre, partial, spectra):
+def transform_kernel(sht, level, turns, table, spectra):
     z = level[:, 0:ROWS, :].reshape(SHT * ROWS, COLS)
     c, s = turns[0, pl.ds(sht[0], 1), :COLS], turns[1, pl.ds(sht[0], 1), :COLS]
     a = jnp.concatenate([z * c, z * -s], 0)
@@ -122,11 +122,15 @@
     scale = 1.0 / NLON * (2.0 / (ROWS * OCEAN))
     spectra[0] = jnp.sum(re * c + im * s, axis=0) * scale
     spectra[1] = jnp.sum(im * c - re * s, axis=0) * scale
-    multiply_rows(1 - core[0], y[0], spectra[...], legendre, partial)
-
-
-def rows_kernel(core, y, spectra, legendre, partial):
-    multiply_rows(core[0], y[0], spectra[...], legendre, partial)
+
+
+def near_rows_kernel(y, spectra, legendre, *partial):
+    multiply_rows(y[0], (), spectra[...], legendre, partial)
+
+
+def far_rows_kernel(y, *refs):
+    before, (spectra, legendre), partial = refs[:PEERS], refs[PEERS:-PEERS], refs[-PEERS:]
+    multiply_rows(y[0], before, spectra[...], legendre, partial)
 
 
 def column_of(line):
@@ -142,13 +146,15 @@
     loaded[1] = (sine_sums[...] + two[...]) * factor
 
 
-def add_degrees(half, y, before, coefs, legendre):
+def synth_kernel(y, *refs):
+    *coefs, legendre, synth = refs
+
     def some(i, acc):
         acc = list(acc)
         for k in range(PEERS):
             for n in range(2):
                 tile = 2 * i + n
-                degrees = degrees_of(half, y, k, tile)
+                degrees = degrees_of(y[0], k, tile)
                 at = pl.ds(pl.multiple_of(8 * tile, 8), 8)
                 x = [coefs[k][c, at, :] for c in range(2)]
                 for j in range(ROWS):
@@ -157,25 +163,10 @@
                         acc[c * ROWS + j] = acc[c * ROWS + j] + p * x[c]
         return tuple(acc)
 
-    return lax.fori_loop(0, CHUNK // 16, some, tuple(before))
-
-
-def degrees_kernel(core, y, *refs):
-    *coefs, legendre, sums = refs
     zero = jnp.zeros((8, ORD), F32)
-    acc = add_degrees(core[0], y[0], [zero] * (2 * ROWS), coefs, legendre)
-    for i in range(2 * ROWS):
-        sums[i] = acc[i]
-
-
-def finish_kernel(core, y, before, *refs):
-    *coefs, legendre, spread, synth = refs
-    acc = add_degrees(1 - core[0], y[0], [before[i] for i in range(2 * ROWS)], coefs, legendre)
+    acc = lax.fori_loop(0, CHUNK // 16, some, (zero,) * (2 * ROWS))
     for i in range(2 * ROWS):
         synth[i : i + 1, :] = jnp.sum(acc[i], axis=0, keepdims=True)
-    value = synth[...]
-    for t in range(SHT):
-        spread[t] = value
 
 
 def potential_kernel(
@@ -371,26 +362,29 @@
         ],
         compiler_params=START_PARAMS,
     )(height, equilibrium, east, north, depth, mask)
-    spread, sht, core, y = lax.optimization_barrier((spread, sht, core, y))
+    spread, legendre = lax.optimization_barrier((spread, legendre))
+    half = LDEG // 2
+    near = lax.dynamic_slice_in_dim(legendre, core[0] * half, half, 1)
+    far = lax.dynamic_slice_in_dim(legendre, (1 - core[0]) * half, half, 1)
+    spread, near, far, sht, core, y = lax.optimization_barrier((spread, near, far, sht, core, y))
+    far = swap(far, 1)
     fields = lax.all_to_all(spread, "sht", 0, 0, tiled=True)
 
     extended = shape(EROWS, NLON)
     block = shape(ROWS, COLS)
-    partial = shape(PEERS, 2, CHUNK, ORD)
+    chunk = shape(2, CHUNK, ORD)
     field = [pltpu.VMEM((EROWS, NLON), F32)]
     level = fields
     for step in range(STEPS):
-        given, spectra = whole(
-            transform_kernel,
-            [partial, shape(2, ROWS, ORD)],
-            (sht, core, y),
-            *(level, turns, analysis, legendre),
-            cost=COST,
+        (spectra,) = whole(
+            transform_kernel, [shape(2, ROWS, ORD)], (sht,), level, turns, analysis
         )
-        taken = swap(given, 1)
-        (kept,) = whole(rows_kernel, [partial], (core, y), spectra, legendre, cost=COST)
-        parts = [kept[k] + taken[k] for k in range(PEERS)]
-        others = [swap(parts[k], along_y[k - 1]) for k in range(1, PEERS)]
+        far_spectra = swap(spectra, 1)
+        parts = whole(near_rows_kernel, [chunk] * PEERS, (y,), spectra, near, cost=COST)
+        parts = whole(
+            far_rows_kernel, [chunk] * PEERS, (y,), *parts, far_spectra, far, cost=COST
+        )
+        others = [swap(parts[k], along_y[k - 1]) for k in range(PEERS - 1, 0, -1)]
         ring = (parts[0] + others[0]) + (others[1] + others[2])
         cosine_sums, sine_sums = ring[0], ring[1]
         one, two = swap_ring(cosine_sums, 1), swap_ring(sine_sums, 3)
@@ -398,27 +392,16 @@
         one, two = swap_ring(cosine_sums, 3), swap_ring(sine_sums, 1)
         (coefs,) = whole(
             love_kernel,
-            [shape(2, CHUNK, ORD)],
+            [chunk],
             (core, y),
             *(cosine_sums, one, sine_sums, two, love),
         )
         own_coefs = [coefs] + [swap(coefs, k) for k in along_y]
-        other_coefs = [swap(x, 1) for x in own_coefs]
-        (sums,) = whole(
-            degrees_kernel,
-            [shape(2 * ROWS, 8, ORD)],
-            (core, y),
-            *(*own_coefs, legendre),
-            cost=COST,
-        )
-        (synth_spread,) = whole(
-            finish_kernel,
-            [shape(SHT, 2 * ROWS, ORD)],
-            (core, y),
-            *(sums, *other_coefs, legendre),
-            scratch=[pltpu.VMEM((2 * ROWS, ORD), F32)],
-            cost=COST,
-        )
+        rows = [shape(2 * ROWS, ORD)]
+        (far_synth,) = whole(synth_kernel, rows, (y,), *own_coefs, far, cost=COST)
+        returned = swap(far_synth, 1)
+        (near_synth,) = whole(synth_kernel, rows, (y,), *own_coefs, near, cost=COST)
+        synth_spread = jnp.broadcast_to(near_synth + returned, (SHT, 2 * ROWS, ORD))
         synth = lax.all_to_all(synth_spread, "sht", 0, 0, tiled=True)
         halo = 8 if step == 0 else 2
         pot, to_core, to_chip = whole(

time: 201 us -> 198 us (0.985)
  starting transfers between devices: 86.8 us -> 76.2 us
  waiting for transfers between devices: 50 us -> 60.5 us
  blocking collectives: 39.8 us -> 37.6 us
    ppermute x36 -> x28, starting transfers between devices: 63.5 us -> 51.9 us  [swap(): return lax.ppermute(x, 'ocean', [(i, i ^ k) for i in range(OCEAN)])]
    ppermute x36 -> x28, waiting for transfers between devices: 19.8 us -> 31 us  [swap(): return lax.ppermute(x, 'ocean', [(i, i ^ k) for i in range(OCEAN)])]
    unnamed x22 -> x16, local copies, waits for them, and re-layouts: 5.12 us -> 0.05 us
    dynamic_slice x0 -> x1, local copies, waits for them, and re-layouts: none -> 4.24 us  [per_device(): far = lax.dynamic_slice_in_dim(legendre, (1 - core[0]) * half, half, 1)]
    all_to_all x1, blocking collectives: 16.2 us -> 14.1 us  [per_device(): fields = lax.all_to_all(spread, 'sht', 0, 0, tiled=True)]
    pallas_call x21 -> x24, Pallas kernels: 14.8 us -> 14.9 us  [whole(): pl.pallas_call(kernel, in_specs=[SCALAR] * len(scalars) + [WHOLE] * len(a...]
  transfers between devices with their start and end apart: 51 -> 43, of which waited for: 24 -> 34; matrix products, arithmetic and copies ran while one was open for 0% -> 0% of each run, Pallas kernels for 2% -> 2%
where the time goes in v4:
time: 198 us; the launch traced here: 196 us
  starting transfers between devices  76.2 us (38%)
  waiting for transfers between devices  60.5 us (31%)
  blocking collectives  37.6 us (19%)
  Pallas kernels  16.6 us (8%)
  local copies, waits for them, and re-layouts  4.36 us (2%)
    ppermute x28, starting transfers between devices, swap(): return lax.ppermute(x, 'ocean', [(i, i ^ k) for i in range(OCEAN)])  51.9 us
    ppermute x28, waiting for transfers between devices, swap(): return lax.ppermute(x, 'ocean', [(i, i ^ k) for i in range(OCEAN)])  31 us
    all_to_all x3, blocking collectives, per_device(): synth = lax.all_to_all(synth_spread, 'sht', 0, 0, tiled=True)  23.5 us
    ppermute x12, waiting for transfers between devices, swap_ring(): return lax.ppermute(x, ('ocean', 'sht'), pairs)  21.9 us
    ppermute x12, starting transfers between devices, swap_ring(): return lax.ppermute(x, ('ocean', 'sht'), pairs)  18.2 us
    pallas_call x24, Pallas kernels, whole(): pl.pallas_call(kernel, in_specs=[SCALAR] * len(scalars) + [WHOLE] * len(a...  14.9 us
    all_to_all x1, blocking collectives, per_device(): fields = lax.all_to_all(spread, 'sht', 0, 0, tiled=True)  14.1 us
    ppermute x3, waiting for transfers between devices, per_device(): from_chip = lax.ppermute(to_chip, 'ocean', chips)  7.51 us
  transfers between devices with their start and end apart: 43, of which 34 were waited for; matrix products, arithmetic and copies ran while one was open for 0% of the time, Pallas kernels for 2%

profile of v4, /device:TPU:1, one launch (start us, length us, event | category | flops | bytes accessed | tf_op | source)
XLA Modules:
  0.0 196.3 jit_solution(3977418711496152586)
XLA Ops:
  2.5 4.2 %constant_dynamic-slice_fusion = (f32[16,512,128]{2,1,0:T(8,128)S(1)}, f32[16,512,128]{2,1,0:T(8,128)S(1)}) fusion(f32[16,1024,128]{2,1,0:T(8,128)} %param.21, s32[]{:T(128)S(6)} %select_n.7, s32[]{:T(128)S(6)} %select_n.6), kind=kLoop, calls=%fused_computation.9 | loop fusion | bytes 16777224 | tf_op jit(solution)/shard_map/dynamic_slice | solution.py:368
  6.7 3.3 %collective-permute-start.1 = (f32[16,512,128]{2,1,0:T(8,128)S(1)}, f32[16,512,128]{2,1,0:T(8,128)S(1)}, u32[]{:S(2)}, u32[]{:S(2)}) collective-permute-start(f32[16,512,128]{2,1,0:T(8,128)S(1)} %get-tuple-element.65), channel_id=1, source_target_pairs={{0,8},{8,0},{16,24},{24,16},{32,40},{40,32},{48,56},{56,48},{64,72... | collective-permute-start | bytes 12582920 | tf_op jit(solution)/shard_map/ppermute | solution.py:340
  10.0 14.1 %all_to_all.20.level.fields = f32[8,80,256]{2,1,0:T(8,128)S(1)} all-to-all(f32[8,80,256]{2,1,0:T(8,128)S(1)} %copy-done.7), channel_id=1, replica_groups=mesh['ocean'=32,'sht'=8] {'sht'}, dimensions={0} | all-to-all | bytes 1310720 | tf_op jit(solution)/shard_map/all_to_all | solution.py:371
  27.9 2.8 %collective-permute-start.2 = (f32[2,128,128]{2,1,0:T(8,128)S(1)}, f32[2,128,128]{2,1,0:T(8,128)S(1)}, u32[]{:S(2)}, u32[]{:S(2)}) collective-permute-start(f32[2,128,128]{2,1,0:T(8,128)S(1)} %get-tuple-element.67), channel_id=1, source_target_pairs={{0,192},{8,200},{16,208},{24,216},{32,224},{40,232},{48,240},{56,2... | collective-permute-start | bytes 393224 | tf_op jit(solution)/shard_map/ppermute | solution.py:340
  31.4 4.8 %collective-permute-done.2 = f32[2,128,128]{2,1,0:T(8,128)S(1)} collective-permute-done((f32[2,128,128]{2,1,0:T(8,128)S(1)}, f32[2,128,128]{2,1,0:T(8,128)S(1)}, u32[]{:S(2)}, u32[]{:S(2)}) %collective-permute-start.2) | collective-permute-done | bytes 131104 | tf_op jit(solution)/shard_map/ppermute | solution.py:340
  37.4 5.2 %collective-permute-start.7 = (f32[128,128]{1,0:T(8,128)S(1)}, f32[128,128]{1,0:T(8,128)S(1)}, u32[]{:S(2)}, u32[]{:S(2)}) collective-permute-start(f32[128,128]{1,0:T(8,128)S(1)} %get-tuple-element.117), channel_id=1, source_target_pairs={{0,48},{1,49},{2,50},{3,51},{4,196},{5,197},{6,198},{7,199},{8,56}... | collective-permute-start | bytes 196616 | tf_op jit(solution)/shard_map/ppermute | solution.py:348
  44.5 2.8 %collective-permute-done.5 = f32[128,128]{1,0:T(8,128)S(1)} collective-permute-done((f32[128,128]{1,0:T(8,128)S(1)}, f32[128,128]{1,0:T(8,128)S(1)}, u32[]{:S(2)}, u32[]{:S(2)}) %collective-permute-start.5) | collective-permute-done | bytes 65568 | tf_op jit(solution)/shard_map/ppermute | solution.py:348
  49.1 2.7 %collective-permute-done.8.two = f32[128,128]{1,0:T(8,128)S(1)} collective-permute-done((f32[128,128]{1,0:T(8,128)S(1)}, f32[128,128]{1,0:T(8,128)S(1)}, u32[]{:S(2)}, u32[]{:S(2)}) %collective-permute-start.8) | collective-permute-done | bytes 65568 | tf_op jit(solution)/shard_map/ppermute | solution.py:348
  61.9 5.7 %collective-permute-start.12 = (f32[32,128]{1,0:T(8,128)S(1)}, f32[32,128]{1,0:T(8,128)S(1)}, u32[]{:S(2)}, u32[]{:S(2)}) collective-permute-start(f32[32,128]{1,0:T(8,128)S(1)} %shard_map.163), channel_id=1, source_target_pairs={{0,8},{8,0},{16,24},{24,16},{32,40},{40,32},{48,56},{56,48},{64,72... | collective-permute-start | bytes 49160 | tf_op jit(solution)/shard_map/ppermute | solution.py:340
  68.4 7.8 %all_to_all.21.synth = f32[8,32,128]{2,1,0:T(8,128)S(1)} all-to-all(f32[8,32,128]{2,1,0:T(8,128)S(1)} %broadcast_in_dim.9), channel_id=1, replica_groups=mesh['ocean'=32,'sht'=8] {'sht'}, dimensions={0} | all-to-all | bytes 262144 | tf_op jit(solution)/shard_map/all_to_all | solution.py:405
  80.1 4.2 %collective-permute-done.14.from_chip = f32[8,2048]{1,0:T(8,128)S(1)} collective-permute-done((f32[8,2048]{1,0:T(8,128)S(1)}, f32[8,2048]{1,0:T(8,128)S(1)}, u32[]{:S(2)}, u32[]{:S(2)}) %collective-permute-start.14) | collective-permute-done | bytes 65568 | tf_op jit(solution)/shard_map/ppermute | solution.py:418
  85.2 2.9 %collective-permute-start.15 = (f32[2,16,128]{2,1,0:T(8,128)S(1)}, f32[2,16,128]{2,1,0:T(8,128)S(1)}, u32[]{:S(2)}, u32[]{:S(2)}) collective-permute-start(f32[2,16,128]{2,1,0:T(8,128)S(1)} %shard_map.166.spectra), channel_id=1, source_target_pairs={{0,8},{8,0},{16,24},{24,16},{32,40},{40,32},{48,56},{56,48},{64,72... | collective-permute-start | bytes 49160 | tf_op jit(solution)/shard_map/ppermute | solution.py:340
  93.0 5.5 %collective-permute-done.16 = f32[2,128,128]{2,1,0:T(8,128)S(1)} collective-permute-done((f32[2,128,128]{2,1,0:T(8,128)S(1)}, f32[2,128,128]{2,1,0:T(8,128)S(1)}, u32[]{:S(2)}, u32[]{:S(2)}) %collective-permute-start.16) | collective-permute-done | bytes 131104 | tf_op jit(solution)/shard_map/ppermute | solution.py:340
  100.6 3.6 %collective-permute-done.21 = f32[128,128]{1,0:T(8,128)S(1)} collective-permute-done((f32[128,128]{1,0:T(8,128)S(1)}, f32[128,128]{1,0:T(8,128)S(1)}, u32[]{:S(2)}, u32[]{:S(2)}) %collective-permute-start.21) | collective-permute-done | bytes 65568 | tf_op jit(solution)/shard_map/ppermute | solution.py:348
  105.3 2.6 %collective-permute-start.20 = (f32[128,128]{1,0:T(8,128)S(1)}, f32[128,128]{1,0:T(8,128)S(1)}, u32[]{:S(2)}, u32[]{:S(2)}) collective-permute-start(f32[128,128]{1,0:T(8,128)S(1)} %get-tuple-element.112.cosine_sums), channel_id=1, source_target_pairs={{0,48},{1,49},{2,50},{3,51},{4,196},{5,197},{6,198},{7,199},{8,56}... | collective-permute-start | bytes 196616 | tf_op jit(solution)/shard_map/ppermute | solution.py:348
  119.0 4.8 %collective-permute-start.26 = (f32[32,128]{1,0:T(8,128)S(1)}, f32[32,128]{1,0:T(8,128)S(1)}, u32[]{:S(2)}, u32[]{:S(2)}) collective-permute-start(f32[32,128]{1,0:T(8,128)S(1)} %shard_map.171), channel_id=1, source_target_pairs={{0,8},{8,0},{16,24},{24,16},{32,40},{40,32},{48,56},{56,48},{64,72... | collective-permute-start | bytes 49160 | tf_op jit(solution)/shard_map/ppermute | solution.py:340
  124.7 7.8 %all_to_all.22.synth = f32[8,32,128]{2,1,0:T(8,128)S(1)} all-to-all(f32[8,32,128]{2,1,0:T(8,128)S(1)} %broadcast_in_dim.10), channel_id=1, replica_groups=mesh['ocean'=32,'sht'=8] {'sht'}, dimensions={0} | all-to-all | bytes 262144 | tf_op jit(solution)/shard_map/all_to_all | solution.py:405
  140.0 3.5 %collective-permute-start.29 = (f32[2,16,128]{2,1,0:T(8,128)S(1)}, f32[2,16,128]{2,1,0:T(8,128)S(1)}, u32[]{:S(2)}, u32[]{:S(2)}) collective-permute-start(f32[2,16,128]{2,1,0:T(8,128)S(1)} %shard_map.174.spectra), channel_id=1, source_target_pairs={{0,8},{8,0},{16,24},{24,16},{32,40},{40,32},{48,56},{56,48},{64,72... | collective-permute-start | bytes 49160 | tf_op jit(solution)/shard_map/ppermute | solution.py:340
  145.8 2.6 %collective-permute-start.32 = (f32[2,128,128]{2,1,0:T(8,128)S(1)}, f32[2,128,128]{2,1,0:T(8,128)S(1)}, u32[]{:S(2)}, u32[]{:S(2)}) collective-permute-start(f32[2,128,128]{2,1,0:T(8,128)S(1)} %get-tuple-element.99), channel_id=1, source_target_pairs={{0,64},{8,72},{16,80},{24,88},{32,96},{40,104},{48,112},{56,120},{... | collective-permute-start | bytes 393224 | tf_op jit(solution)/shard_map/ppermute | solution.py:340
  148.4 5.5 %collective-permute-done.30 = f32[2,128,128]{2,1,0:T(8,128)S(1)} collective-permute-done((f32[2,128,128]{2,1,0:T(8,128)S(1)}, f32[2,128,128]{2,1,0:T(8,128)S(1)}, u32[]{:S(2)}, u32[]{:S(2)}) %collective-permute-start.30) | collective-permute-done | bytes 131104 | tf_op jit(solution)/shard_map/ppermute | solution.py:340
  156.7 3.2 %collective-permute-done.35 = f32[128,128]{1,0:T(8,128)S(1)} collective-permute-done((f32[128,128]{1,0:T(8,128)S(1)}, f32[128,128]{1,0:T(8,128)S(1)}, u32[]{:S(2)}, u32[]{:S(2)}) %collective-permute-start.35) | collective-permute-done | bytes 65568 | tf_op jit(solution)/shard_map/ppermute | solution.py:348
  161.5 2.7 %collective-permute-start.34 = (f32[128,128]{1,0:T(8,128)S(1)}, f32[128,128]{1,0:T(8,128)S(1)}, u32[]{:S(2)}, u32[]{:S(2)}) collective-permute-start(f32[128,128]{1,0:T(8,128)S(1)} %get-tuple-element.108.cosine_sums), channel_id=1, source_target_pairs={{0,48},{1,49},{2,50},{3,51},{4,196},{5,197},{6,198},{7,199},{8,56}... | collective-permute-start | bytes 196616 | tf_op jit(solution)/shard_map/ppermute | solution.py:348
  174.8 4.9 %collective-permute-start.40 = (f32[32,128]{1,0:T(8,128)S(1)}, f32[32,128]{1,0:T(8,128)S(1)}, u32[]{:S(2)}, u32[]{:S(2)}) collective-permute-start(f32[32,128]{1,0:T(8,128)S(1)} %shard_map.179), channel_id=1, source_target_pairs={{0,8},{8,0},{16,24},{24,16},{32,40},{40,32},{48,56},{56,48},{64,72... | collective-permute-start | bytes 49160 | tf_op jit(solution)/shard_map/ppermute | solution.py:340
  180.6 7.8 %all_to_all.23.synth = f32[8,32,128]{2,1,0:T(8,128)S(1)} all-to-all(f32[8,32,128]{2,1,0:T(8,128)S(1)} %broadcast_in_dim.11), channel_id=1, replica_groups=mesh['ocean'=32,'sht'=8] {'sht'}, dimensions={0} | all-to-all | bytes 262144 | tf_op jit(solution)/shard_map/all_to_all | solution.py:405
  (123 shorter events, 80.1 us)
Async XLA Ops:
  6.7 20.4 %collective-permute-start.1 = (f32[16,512,128]{2,1,0:T(8,128)S(1)}, f32[16,512,128]{2,1,0:T(8,128)S(1)}, u32[]{:S(2)}, u32[]{:S(2)}) collective-permute-start(f32[16,512,128]{2,1,0:T(8,128)S(1)} %get-tuple-element.65), channel_id=1, source_target_pairs={{0,8},{8,0},{16,24},{24,16},{32,40},{40,32},{48,56},{56,48},{64,72... | collective-permute-start | bytes 12582920 | tf_op jit(solution)/shard_map/ppermute | solution.py:340
  27.9 8.3 %collective-permute-start.2 = (f32[2,128,128]{2,1,0:T(8,128)S(1)}, f32[2,128,128]{2,1,0:T(8,128)S(1)}, u32[]{:S(2)}, u32[]{:S(2)}) collective-permute-start(f32[2,128,128]{2,1,0:T(8,128)S(1)} %get-tuple-element.67), channel_id=1, source_target_pairs={{0,192},{8,200},{16,208},{24,216},{32,224},{40,232},{48,240},{56,2... | collective-permute-start | bytes 393224 | tf_op jit(solution)/shard_map/ppermute | solution.py:340
  30.7 5.9 %collective-permute-start.3 = (f32[2,128,128]{2,1,0:T(8,128)S(1)}, f32[2,128,128]{2,1,0:T(8,128)S(1)}, u32[]{:S(2)}, u32[]{:S(2)}) collective-permute-start(f32[2,128,128]{2,1,0:T(8,128)S(1)} %get-tuple-element.68), channel_id=1, source_target_pairs={{0,128},{8,136},{16,144},{24,152},{32,160},{40,168},{48,176},{56,1... | collective-permute-start | bytes 393224 | tf_op jit(solution)/shard_map/ppermute | solution.py:340
  31.0 6.3 %collective-permute-start.4 = (f32[2,128,128]{2,1,0:T(8,128)S(1)}, f32[2,128,128]{2,1,0:T(8,128)S(1)}, u32[]{:S(2)}, u32[]{:S(2)}) collective-permute-start(f32[2,128,128]{2,1,0:T(8,128)S(1)} %get-tuple-element.69), channel_id=1, source_target_pairs={{0,64},{8,72},{16,80},{24,88},{32,96},{40,104},{48,112},{56,120},{... | collective-permute-start | bytes 393224 | tf_op jit(solution)/shard_map/ppermute | solution.py:340
  37.4 7.1 %collective-permute-start.7 = (f32[128,128]{1,0:T(8,128)S(1)}, f32[128,128]{1,0:T(8,128)S(1)}, u32[]{:S(2)}, u32[]{:S(2)}) collective-permute-start(f32[128,128]{1,0:T(8,128)S(1)} %get-tuple-element.117), channel_id=1, source_target_pairs={{0,48},{1,49},{2,50},{3,51},{4,196},{5,197},{6,198},{7,199},{8,56}... | collective-permute-start | bytes 196616 | tf_op jit(solution)/shard_map/ppermute | solution.py:348
  53.6 5.6 %collective-permute-start.11 = (f32[2,128,128]{2,1,0:T(8,128)S(1)}, f32[2,128,128]{2,1,0:T(8,128)S(1)}, u32[]{:S(2)}, u32[]{:S(2)}) collective-permute-start(f32[2,128,128]{2,1,0:T(8,128)S(1)} %shard_map.161.refs_0_), channel_id=1, source_target_pairs={{0,192},{8,200},{16,208},{24,216},{32,224},{40,232},{48,240},{56,2... | collective-permute-start | bytes 393224 | tf_op jit(solution)/shard_map/ppermute | solution.py:340
  55.9 5.3 %collective-permute-start.10 = (f32[2,128,128]{2,1,0:T(8,128)S(1)}, f32[2,128,128]{2,1,0:T(8,128)S(1)}, u32[]{:S(2)}, u32[]{:S(2)}) collective-permute-start(f32[2,128,128]{2,1,0:T(8,128)S(1)} %shard_map.161.refs_0_), channel_id=1, source_target_pairs={{0,128},{8,136},{16,144},{24,152},{32,160},{40,168},{48,176},{56,1... | collective-permute-start | bytes 393224 | tf_op jit(solution)/shard_map/ppermute | solution.py:340
  61.9 6.6 %collective-permute-start.12 = (f32[32,128]{1,0:T(8,128)S(1)}, f32[32,128]{1,0:T(8,128)S(1)}, u32[]{:S(2)}, u32[]{:S(2)}) collective-permute-start(f32[32,128]{1,0:T(8,128)S(1)} %shard_map.163), channel_id=1, source_target_pairs={{0,8},{8,0},{16,24},{24,16},{32,40},{40,32},{48,56},{56,48},{64,72... | collective-permute-start | bytes 49160 | tf_op jit(solution)/shard_map/ppermute | solution.py:340
  78.9 5.4 %collective-permute-start.14 = (f32[8,2048]{1,0:T(8,128)S(1)}, f32[8,2048]{1,0:T(8,128)S(1)}, u32[]{:S(2)}, u32[]{:S(2)}) collective-permute-start(f32[8,2048]{1,0:T(8,128)S(1)} %get-tuple-element.72), channel_id=1, source_target_pairs={{0,248},{8,16},{16,8},{24,32},{32,24},{40,48},{48,40},{56,64},{64,... | collective-permute-start | bytes 196616 | tf_op jit(solution)/shard_map/ppermute | solution.py:418
  89.7 8.9 %collective-permute-start.16 = (f32[2,128,128]{2,1,0:T(8,128)S(1)}, f32[2,128,128]{2,1,0:T(8,128)S(1)}, u32[]{:S(2)}, u32[]{:S(2)}) collective-permute-start(f32[2,128,128]{2,1,0:T(8,128)S(1)} %get-tuple-element.79), channel_id=1, source_target_pairs={{0,192},{8,200},{16,208},{24,216},{32,224},{40,232},{48,240},{56,2... | collective-permute-start | bytes 393224 | tf_op jit(solution)/shard_map/ppermute | solution.py:340
  90.2 8.3 %collective-permute-start.17 = (f32[2,128,128]{2,1,0:T(8,128)S(1)}, f32[2,128,128]{2,1,0:T(8,128)S(1)}, u32[]{:S(2)}, u32[]{:S(2)}) collective-permute-start(f32[2,128,128]{2,1,0:T(8,128)S(1)} %get-tuple-element.80), channel_id=1, source_target_pairs={{0,128},{8,136},{16,144},{24,152},{32,160},{40,168},{48,176},{56,1... | collective-permute-start | bytes 393224 | tf_op jit(solution)/shard_map/ppermute | solution.py:340
  90.6 8.2 %collective-permute-start.18 = (f32[2,128,128]{2,1,0:T(8,128)S(1)}, f32[2,128,128]{2,1,0:T(8,128)S(1)}, u32[]{:S(2)}, u32[]{:S(2)}) collective-permute-start(f32[2,128,128]{2,1,0:T(8,128)S(1)} %get-tuple-element.81), channel_id=1, source_target_pairs={{0,64},{8,72},{16,80},{24,88},{32,96},{40,104},{48,112},{56,120},{... | collective-permute-start | bytes 393224 | tf_op jit(solution)/shard_map/ppermute | solution.py:340
  98.9 5.3 %collective-permute-start.21 = (f32[128,128]{1,0:T(8,128)S(1)}, f32[128,128]{1,0:T(8,128)S(1)}, u32[]{:S(2)}, u32[]{:S(2)}) collective-permute-start(f32[128,128]{1,0:T(8,128)S(1)} %get-tuple-element.113), channel_id=1, source_target_pairs={{0,48},{1,49},{2,50},{3,51},{4,196},{5,197},{6,198},{7,199},{8,56}... | collective-permute-start | bytes 196616 | tf_op jit(solution)/shard_map/ppermute | solution.py:348
  105.3 5.4 %collective-permute-start.20 = (f32[128,128]{1,0:T(8,128)S(1)}, f32[128,128]{1,0:T(8,128)S(1)}, u32[]{:S(2)}, u32[]{:S(2)}) collective-permute-start(f32[128,128]{1,0:T(8,128)S(1)} %get-tuple-element.112.cosine_sums), channel_id=1, source_target_pairs={{0,48},{1,49},{2,50},{3,51},{4,196},{5,197},{6,198},{7,199},{8,56}... | collective-permute-start | bytes 196616 | tf_op jit(solution)/shard_map/ppermute | solution.py:348
  110.7 5.6 %collective-permute-start.25 = (f32[2,128,128]{2,1,0:T(8,128)S(1)}, f32[2,128,128]{2,1,0:T(8,128)S(1)}, u32[]{:S(2)}, u32[]{:S(2)}) collective-permute-start(f32[2,128,128]{2,1,0:T(8,128)S(1)} %shard_map.169.refs_0_), channel_id=1, source_target_pairs={{0,192},{8,200},{16,208},{24,216},{32,224},{40,232},{48,240},{56,2... | collective-permute-start | bytes 393224 | tf_op jit(solution)/shard_map/ppermute | solution.py:340
  113.0 5.3 %collective-permute-start.24 = (f32[2,128,128]{2,1,0:T(8,128)S(1)}, f32[2,128,128]{2,1,0:T(8,128)S(1)}, u32[]{:S(2)}, u32[]{:S(2)}) collective-permute-start(f32[2,128,128]{2,1,0:T(8,128)S(1)} %shard_map.169.refs_0_), channel_id=1, source_target_pairs={{0,128},{8,136},{16,144},{24,152},{32,160},{40,168},{48,176},{56,1... | collective-permute-start | bytes 393224 | tf_op jit(solution)/shard_map/ppermute | solution.py:340
  119.0 5.7 %collective-permute-start.26 = (f32[32,128]{1,0:T(8,128)S(1)}, f32[32,128]{1,0:T(8,128)S(1)}, u32[]{:S(2)}, u32[]{:S(2)}) collective-permute-start(f32[32,128]{1,0:T(8,128)S(1)} %shard_map.171), channel_id=1, source_target_pairs={{0,8},{8,0},{16,24},{24,16},{32,40},{40,32},{48,56},{56,48},{64,72... | collective-permute-start | bytes 49160 | tf_op jit(solution)/shard_map/ppermute | solution.py:340
  145.0 8.9 %collective-permute-start.30 = (f32[2,128,128]{2,1,0:T(8,128)S(1)}, f32[2,128,128]{2,1,0:T(8,128)S(1)}, u32[]{:S(2)}, u32[]{:S(2)}) collective-permute-start(f32[2,128,128]{2,1,0:T(8,128)S(1)} %get-tuple-element.97), channel_id=1, source_target_pairs={{0,192},{8,200},{16,208},{24,216},{32,224},{40,232},{48,240},{56,2... | collective-permute-start | bytes 393224 | tf_op jit(solution)/shard_map/ppermute | solution.py:340
  145.6 8.3 %collective-permute-start.31 = (f32[2,128,128]{2,1,0:T(8,128)S(1)}, f32[2,128,128]{2,1,0:T(8,128)S(1)}, u32[]{:S(2)}, u32[]{:S(2)}) collective-permute-start(f32[2,128,128]{2,1,0:T(8,128)S(1)} %get-tuple-element.98), channel_id=1, source_target_pairs={{0,128},{8,136},{16,144},{24,152},{32,160},{40,168},{48,176},{56,1... | collective-permute-start | bytes 393224 | tf_op jit(solution)/shard_map/ppermute | solution.py:340
  145.8 8.5 %collective-permute-start.32 = (f32[2,128,128]{2,1,0:T(8,128)S(1)}, f32[2,128,128]{2,1,0:T(8,128)S(1)}, u32[]{:S(2)}, u32[]{:S(2)}) collective-permute-start(f32[2,128,128]{2,1,0:T(8,128)S(1)} %get-tuple-element.99), channel_id=1, source_target_pairs={{0,64},{8,72},{16,80},{24,88},{32,96},{40,104},{48,112},{56,120},{... | collective-permute-start | bytes 393224 | tf_op jit(solution)/shard_map/ppermute | solution.py:340
  154.3 5.5 %collective-permute-start.35 = (f32[128,128]{1,0:T(8,128)S(1)}, f32[128,128]{1,0:T(8,128)S(1)}, u32[]{:S(2)}, u32[]{:S(2)}) collective-permute-start(f32[128,128]{1,0:T(8,128)S(1)} %get-tuple-element.109), channel_id=1, source_target_pairs={{0,48},{1,49},{2,50},{3,51},{4,196},{5,197},{6,198},{7,199},{8,56}... | collective-permute-start | bytes 196616 | tf_op jit(solution)/shard_map/ppermute | solution.py:348
  161.5 5.3 %collective-permute-start.34 = (f32[128,128]{1,0:T(8,128)S(1)}, f32[128,128]{1,0:T(8,128)S(1)}, u32[]{:S(2)}, u32[]{:S(2)}) collective-permute-start(f32[128,128]{1,0:T(8,128)S(1)} %get-tuple-element.108.cosine_sums), channel_id=1, source_target_pairs={{0,48},{1,49},{2,50},{3,51},{4,196},{5,197},{6,198},{7,199},{8,56}... | collective-permute-start | bytes 196616 | tf_op jit(solution)/shard_map/ppermute | solution.py:348
  168.8 5.3 %collective-permute-start.38 = (f32[2,128,128]{2,1,0:T(8,128)S(1)}, f32[2,128,128]{2,1,0:T(8,128)S(1)}, u32[]{:S(2)}, u32[]{:S(2)}) collective-permute-start(f32[2,128,128]{2,1,0:T(8,128)S(1)} %shard_map.177.refs_0_), channel_id=1, source_target_pairs={{0,128},{8,136},{16,144},{24,152},{32,160},{40,168},{48,176},{56,1... | collective-permute-start | bytes 393224 | tf_op jit(solution)/shard_map/ppermute | solution.py:340
  174.8 5.7 %collective-permute-start.40 = (f32[32,128]{1,0:T(8,128)S(1)}, f32[32,128]{1,0:T(8,128)S(1)}, u32[]{:S(2)}, u32[]{:S(2)}) collective-permute-start(f32[32,128]{1,0:T(8,128)S(1)} %shard_map.179), channel_id=1, source_target_pairs={{0,8},{8,0},{16,24},{24,16},{32,40},{40,32},{48,56},{56,48},{64,72... | collective-permute-start | bytes 49160 | tf_op jit(solution)/shard_map/ppermute | solution.py:340
  (27 other events, 253.9 us)

commit v5 on v4

--- a/solution.py
+++ b/solution.py
@@ -80,6 +80,20 @@
             field = jnp.where(ocean, field, 0.0)
         for t in range(SHT):
             spread[t, ROWS * i : ROWS * (i + 1), :] = field
+
+
+def halves_kernel(core, legendre, near, far, sems):
+    half = LDEG // 2
+    copies = [
+        pltpu.make_async_copy(
+            legendre.at[:, pl.ds(pl.multiple_of(first * half, half), half), :], out, sems.at[i]
+        )
+        for i, (first, out) in enumerate(((1 - core[0], far), (core[0], near)))
+    ]
+    for copy in copies:
+        copy.start()
+    for copy in copies:
+        copy.wait()
 
 
 def degrees_of(y, k, tile):
@@ -309,6 +323,7 @@
 
 PARAMS = pltpu.CompilerParams(vmem_limit_bytes=16 * 1024 * 1024)
 START_PARAMS = pltpu.CompilerParams(vmem_limit_bytes=60 * 1024 * 1024)
+HALVES_PARAMS = pltpu.CompilerParams(vmem_limit_bytes=48 * 1024 * 1024)
 COST = pl.CostEstimate(flops=ROWS * LDEG * ORD * 2, bytes_accessed=5 << 20, transcendentals=0)
 WHOLE = pl.BlockSpec(memory_space=pltpu.VMEM)
 SCALAR = pl.BlockSpec(memory_space=pltpu.SMEM)
@@ -363,9 +378,14 @@
         compiler_params=START_PARAMS,
     )(height, equilibrium, east, north, depth, mask)
     spread, legendre = lax.optimization_barrier((spread, legendre))
-    half = LDEG // 2
-    near = lax.dynamic_slice_in_dim(legendre, core[0] * half, half, 1)
-    far = lax.dynamic_slice_in_dim(legendre, (1 - core[0]) * half, half, 1)
+    near, far = pl.pallas_call(
+        halves_kernel,
+        in_specs=[SCALAR, HBM],
+        out_specs=[WHOLE] * 2,
+        out_shape=[shape(ROWS, LDEG // 2, ORD)] * 2,
+        scratch_shapes=[pltpu.SemaphoreType.DMA((2,))],
+        compiler_params=HALVES_PARAMS,
+    )(core, legendre)
     spread, near, far, sht, core, y = lax.optimization_barrier((spread, near, far, sht, core, y))
     far = swap(far, 1)
     fields = lax.all_to_all(spread, "sht", 0, 0, tiled=True)
@@ -384,7 +404,7 @@
         parts = whole(
             far_rows_kernel, [chunk] * PEERS, (y,), *parts, far_spectra, far, cost=COST
         )
-        others = [swap(parts[k], along_y[k - 1]) for k in range(PEERS - 1, 0, -1)]
+        others = [swap(parts[k], along_y[k - 1]) for k in (2, 1, 3)]
         ring = (parts[0] + others[0]) + (others[1] + others[2])
         cosine_sums, sine_sums = ring[0], ring[1]
         one, two = swap_ring(cosine_sums, 1), swap_ring(sine_sums, 3)
@@ -396,7 +416,8 @@
             (core, y),
             *(cosine_sums, one, sine_sums, two, love),
         )
-        own_coefs = [coefs] + [swap(coefs, k) for k in along_y]
+        from_y = {k: swap(coefs, along_y[k - 1]) for k in (3, 1, 2)}
+        own_coefs = [coefs] + [from_y[k] for k in range(1, PEERS)]
         rows = [shape(2 * ROWS, ORD)]
         (far_synth,) = whole(synth_kernel, rows, (y,), *own_coefs, far, cost=COST)
         returned = swap(far_synth, 1)

time: 198 us -> 199 us (level)
  Pallas kernels: 16.6 us -> 22.2 us
  local copies, waits for them, and re-layouts: 4.36 us -> 0.12 us
  starting transfers between devices: 76.2 us -> 73.2 us
  waiting for transfers between devices: 60.5 us -> 63.1 us
    pallas_call x0 -> x1, Pallas kernels: none -> 5.53 us  [per_device(): pl.pallas_call(halves_kernel, in_specs=[SCALAR, HBM], out_specs=[WHOLE] *...]
    dynamic_slice x1 -> x0, local copies, waits for them, and re-layouts: 4.24 us -> none  [per_device(): far = lax.dynamic_slice_in_dim(legendre, (1 - core[0]) * half, half, 1)]
    ppermute x28, waiting for transfers between devices: 31 us -> 33.4 us  [swap(): return lax.ppermute(x, 'ocean', [(i, i ^ k) for i in range(OCEAN)])]
where the time goes in v5:
time: 199 us; the launch traced here: 197 us
  starting transfers between devices  73.2 us (37%)
  waiting for transfers between devices  63.1 us (32%)
  blocking collectives  37.6 us (19%)
  Pallas kernels  22.2 us (11%)
    ppermute x28, starting transfers between devices, swap(): return lax.ppermute(x, 'ocean', [(i, i ^ k) for i in range(OCEAN)])  50.1 us
    ppermute x28, waiting for transfers between devices, swap(): return lax.ppermute(x, 'ocean', [(i, i ^ k) for i in range(OCEAN)])  33.4 us
    all_to_all x3, blocking collectives, per_device(): synth = lax.all_to_all(synth_spread, 'sht', 0, 0, tiled=True)  23.5 us
    ppermute x12, waiting for transfers between devices, swap_ring(): return lax.ppermute(x, ('ocean', 'sht'), pairs)  22.4 us
    ppermute x12, starting transfers between devices, swap_ring(): return lax.ppermute(x, ('ocean', 'sht'), pairs)  16.9 us
    pallas_call x24, Pallas kernels, whole(): pl.pallas_call(kernel, in_specs=[SCALAR] * len(scalars) + [WHOLE] * len(a...  14.8 us
    all_to_all x1, blocking collectives, per_device(): fields = lax.all_to_all(spread, 'sht', 0, 0, tiled=True)  14.1 us
    ppermute x3, waiting for transfers between devices, per_device(): from_chip = lax.ppermute(to_chip, 'ocean', chips)  7.24 us
  transfers between devices with their start and end apart: 43, of which 34 were waited for; matrix products, arithmetic and copies ran while one was open for 0% of the time, Pallas kernels for 2%

profile of v5, /device:TPU:1, one launch (start us, length us, event | category | flops | bytes accessed | tf_op | source)
XLA Modules:
  0.0 197.3 jit_solution(697072690227292680)
XLA Ops:
  2.5 5.5 %shard_map.158 = (f32[16,512,128]{2,1,0:T(8,128)S(1)}, f32[16,512,128]{2,1,0:T(8,128)}) custom-call(s32[1]{0:T(128)} %bitcast.core, f32[16,1024,128]{2,1,0:T(8,128)} %legendre), custom_call_target="tpu_custom_call" | custom-call | tf_op jit(solution)/shard_map/pallas_call | solution.py:381
  8.0 3.3 %collective-permute-start.1 = (f32[16,512,128]{2,1,0:T(8,128)}, f32[16,512,128]{2,1,0:T(8,128)S(1)}, u32[]{:S(2)}, u32[]{:S(2)}) collective-permute-start(f32[16,512,128]{2,1,0:T(8,128)} %get-tuple-element.69), channel_id=1, source_target_pairs={{0,8},{8,0},{16,24},{24,16},{32,40},{40,32},{48,56},{56,48},{64,72... | collective-permute-start | bytes 12582920 | tf_op jit(solution)/shard_map/ppermute | solution.py:355
  11.3 14.1 %all_to_all.20.level.fields = f32[8,80,256]{2,1,0:T(8,128)S(1)} all-to-all(f32[8,80,256]{2,1,0:T(8,128)S(1)} %copy-done.7), channel_id=1, replica_groups=mesh['ocean'=32,'sht'=8] {'sht'}, dimensions={0} | all-to-all | bytes 1310720 | tf_op jit(solution)/shard_map/all_to_all | solution.py:391
  29.2 3.0 %collective-permute-start.2 = (f32[2,128,128]{2,1,0:T(8,128)S(1)}, f32[2,128,128]{2,1,0:T(8,128)S(1)}, u32[]{:S(2)}, u32[]{:S(2)}) collective-permute-start(f32[2,128,128]{2,1,0:T(8,128)S(1)} %get-tuple-element.71), channel_id=1, source_target_pairs={{0,128},{8,136},{16,144},{24,152},{32,160},{40,168},{48,176},{56,1... | collective-permute-start | bytes 393224 | tf_op jit(solution)/shard_map/ppermute | solution.py:355
  35.5 3.2 %collective-permute-done.3 = f32[2,128,128]{2,1,0:T(8,128)S(1)} collective-permute-done((f32[2,128,128]{2,1,0:T(8,128)S(1)}, f32[2,128,128]{2,1,0:T(8,128)S(1)}, u32[]{:S(2)}, u32[]{:S(2)}) %collective-permute-start.3) | collective-permute-done | bytes 131104 | tf_op jit(solution)/shard_map/ppermute | solution.py:355
  38.7 5.2 %collective-permute-start.7 = (f32[128,128]{1,0:T(8,128)S(1)}, f32[128,128]{1,0:T(8,128)S(1)}, u32[]{:S(2)}, u32[]{:S(2)}) collective-permute-start(f32[128,128]{1,0:T(8,128)S(1)} %get-tuple-element.119), channel_id=1, source_target_pairs={{0,48},{1,49},{2,50},{3,51},{4,196},{5,197},{6,198},{7,199},{8,56}... | collective-permute-start | bytes 196616 | tf_op jit(solution)/shard_map/ppermute | solution.py:363
  50.4 2.7 %collective-permute-done.8.two = f32[128,128]{1,0:T(8,128)S(1)} collective-permute-done((f32[128,128]{1,0:T(8,128)S(1)}, f32[128,128]{1,0:T(8,128)S(1)}, u32[]{:S(2)}, u32[]{:S(2)}) %collective-permute-start.8) | collective-permute-done | bytes 65568 | tf_op jit(solution)/shard_map/ppermute | solution.py:363
  54.6 3.2 %collective-permute-start.11 = (f32[2,128,128]{2,1,0:T(8,128)S(1)}, f32[2,128,128]{2,1,0:T(8,128)S(1)}, u32[]{:S(2)}, u32[]{:S(2)}) collective-permute-start(f32[2,128,128]{2,1,0:T(8,128)S(1)} %shard_map.162.refs_0_), channel_id=1, source_target_pairs={{0,192},{8,200},{16,208},{24,216},{32,224},{40,232},{48,240},{56,2... | collective-permute-start | bytes 393224 | tf_op jit(solution)/shard_map/ppermute | solution.py:355
  58.4 2.6 %collective-permute-done.11.refs_3_ = f32[2,128,128]{2,1,0:T(8,128)S(1)} collective-permute-done((f32[2,128,128]{2,1,0:T(8,128)S(1)}, f32[2,128,128]{2,1,0:T(8,128)S(1)}, u32[]{:S(2)}, u32[]{:S(2)}) %collective-permute-start.11) | collective-permute-done | bytes 131104 | tf_op jit(solution)/shard_map/ppermute | solution.py:355
  63.8 4.8 %collective-permute-start.12 = (f32[32,128]{1,0:T(8,128)S(1)}, f32[32,128]{1,0:T(8,128)S(1)}, u32[]{:S(2)}, u32[]{:S(2)}) collective-permute-start(f32[32,128]{1,0:T(8,128)S(1)} %shard_map.164), channel_id=1, source_target_pairs={{0,8},{8,0},{16,24},{24,16},{32,40},{40,32},{48,56},{56,48},{64,72... | collective-permute-start | bytes 49160 | tf_op jit(solution)/shard_map/ppermute | solution.py:355
  69.5 7.8 %all_to_all.21.synth = f32[8,32,128]{2,1,0:T(8,128)S(1)} all-to-all(f32[8,32,128]{2,1,0:T(8,128)S(1)} %broadcast_in_dim.9), channel_id=1, replica_groups=mesh['ocean'=32,'sht'=8] {'sht'}, dimensions={0} | all-to-all | bytes 262144 | tf_op jit(solution)/shard_map/all_to_all | solution.py:426
  81.5 3.8 %collective-permute-done.14.from_chip = f32[8,2048]{1,0:T(8,128)S(1)} collective-permute-done((f32[8,2048]{1,0:T(8,128)S(1)}, f32[8,2048]{1,0:T(8,128)S(1)}, u32[]{:S(2)}, u32[]{:S(2)}) %collective-permute-start.14) | collective-permute-done | bytes 65568 | tf_op jit(solution)/shard_map/ppermute | solution.py:439
  86.2 2.8 %collective-permute-start.15 = (f32[2,16,128]{2,1,0:T(8,128)S(1)}, f32[2,16,128]{2,1,0:T(8,128)S(1)}, u32[]{:S(2)}, u32[]{:S(2)}) collective-permute-start(f32[2,16,128]{2,1,0:T(8,128)S(1)} %shard_map.167.spectra), channel_id=1, source_target_pairs={{0,8},{8,0},{16,24},{24,16},{32,40},{40,32},{48,56},{56,48},{64,72... | collective-permute-start | bytes 49160 | tf_op jit(solution)/shard_map/ppermute | solution.py:355
  94.1 3.0 %collective-permute-done.16 = f32[2,128,128]{2,1,0:T(8,128)S(1)} collective-permute-done((f32[2,128,128]{2,1,0:T(8,128)S(1)}, f32[2,128,128]{2,1,0:T(8,128)S(1)}, u32[]{:S(2)}, u32[]{:S(2)}) %collective-permute-start.16) | collective-permute-done | bytes 131104 | tf_op jit(solution)/shard_map/ppermute | solution.py:355
  97.9 2.6 %collective-permute-done.18 = f32[2,128,128]{2,1,0:T(8,128)S(1)} collective-permute-done((f32[2,128,128]{2,1,0:T(8,128)S(1)}, f32[2,128,128]{2,1,0:T(8,128)S(1)}, u32[]{:S(2)}, u32[]{:S(2)}) %collective-permute-start.18) | collective-permute-done | bytes 131104 | tf_op jit(solution)/shard_map/ppermute | solution.py:355
  102.1 3.8 %collective-permute-done.21 = f32[128,128]{1,0:T(8,128)S(1)} collective-permute-done((f32[128,128]{1,0:T(8,128)S(1)}, f32[128,128]{1,0:T(8,128)S(1)}, u32[]{:S(2)}, u32[]{:S(2)}) %collective-permute-start.21) | collective-permute-done | bytes 65568 | tf_op jit(solution)/shard_map/ppermute | solution.py:363
  112.3 2.6 %collective-permute-start.25 = (f32[2,128,128]{2,1,0:T(8,128)S(1)}, f32[2,128,128]{2,1,0:T(8,128)S(1)}, u32[]{:S(2)}, u32[]{:S(2)}) collective-permute-start(f32[2,128,128]{2,1,0:T(8,128)S(1)} %shard_map.170.refs_0_), channel_id=1, source_target_pairs={{0,192},{8,200},{16,208},{24,216},{32,224},{40,232},{48,240},{56,2... | collective-permute-start | bytes 393224 | tf_op jit(solution)/shard_map/ppermute | solution.py:355
  120.9 4.4 %collective-permute-start.26 = (f32[32,128]{1,0:T(8,128)S(1)}, f32[32,128]{1,0:T(8,128)S(1)}, u32[]{:S(2)}, u32[]{:S(2)}) collective-permute-start(f32[32,128]{1,0:T(8,128)S(1)} %shard_map.172), channel_id=1, source_target_pairs={{0,8},{8,0},{16,24},{24,16},{32,40},{40,32},{48,56},{56,48},{64,72... | collective-permute-start | bytes 49160 | tf_op jit(solution)/shard_map/ppermute | solution.py:355
  126.2 7.8 %all_to_all.22.synth = f32[8,32,128]{2,1,0:T(8,128)S(1)} all-to-all(f32[8,32,128]{2,1,0:T(8,128)S(1)} %broadcast_in_dim.10), channel_id=1, replica_groups=mesh['ocean'=32,'sht'=8] {'sht'}, dimensions={0} | all-to-all | bytes 262144 | tf_op jit(solution)/shard_map/all_to_all | solution.py:426
  141.5 3.5 %collective-permute-start.29 = (f32[2,16,128]{2,1,0:T(8,128)S(1)}, f32[2,16,128]{2,1,0:T(8,128)S(1)}, u32[]{:S(2)}, u32[]{:S(2)}) collective-permute-start(f32[2,16,128]{2,1,0:T(8,128)S(1)} %shard_map.175.spectra), channel_id=1, source_target_pairs={{0,8},{8,0},{16,24},{24,16},{32,40},{40,32},{48,56},{56,48},{64,72... | collective-permute-start | bytes 49160 | tf_op jit(solution)/shard_map/ppermute | solution.py:355
  149.9 3.0 %collective-permute-done.30 = f32[2,128,128]{2,1,0:T(8,128)S(1)} collective-permute-done((f32[2,128,128]{2,1,0:T(8,128)S(1)}, f32[2,128,128]{2,1,0:T(8,128)S(1)}, u32[]{:S(2)}, u32[]{:S(2)}) %collective-permute-start.30) | collective-permute-done | bytes 131104 | tf_op jit(solution)/shard_map/ppermute | solution.py:355
  157.4 4.4 %collective-permute-done.35 = f32[128,128]{1,0:T(8,128)S(1)} collective-permute-done((f32[128,128]{1,0:T(8,128)S(1)}, f32[128,128]{1,0:T(8,128)S(1)}, u32[]{:S(2)}, u32[]{:S(2)}) %collective-permute-start.35) | collective-permute-done | bytes 65568 | tf_op jit(solution)/shard_map/ppermute | solution.py:363
  177.2 3.5 %collective-permute-start.40 = (f32[32,128]{1,0:T(8,128)S(1)}, f32[32,128]{1,0:T(8,128)S(1)}, u32[]{:S(2)}, u32[]{:S(2)}) collective-permute-start(f32[32,128]{1,0:T(8,128)S(1)} %shard_map.180), channel_id=1, source_target_pairs={{0,8},{8,0},{16,24},{24,16},{32,40},{40,32},{48,56},{56,48},{64,72... | collective-permute-start | bytes 49160 | tf_op jit(solution)/shard_map/ppermute | solution.py:355
  181.5 7.8 %all_to_all.23.synth = f32[8,32,128]{2,1,0:T(8,128)S(1)} all-to-all(f32[8,32,128]{2,1,0:T(8,128)S(1)} %broadcast_in_dim.11), channel_id=1, replica_groups=mesh['ocean'=32,'sht'=8] {'sht'}, dimensions={0} | all-to-all | bytes 262144 | tf_op jit(solution)/shard_map/all_to_all | solution.py:426
  (123 shorter events, 87.9 us)
Async XLA Ops:
  8.0 20.4 %collective-permute-start.1 = (f32[16,512,128]{2,1,0:T(8,128)}, f32[16,512,128]{2,1,0:T(8,128)S(1)}, u32[]{:S(2)}, u32[]{:S(2)}) collective-permute-start(f32[16,512,128]{2,1,0:T(8,128)} %get-tuple-element.69), channel_id=1, source_target_pairs={{0,8},{8,0},{16,24},{24,16},{32,40},{40,32},{48,56},{56,48},{64,72... | collective-permute-start | bytes 12582920 | tf_op jit(solution)/shard_map/ppermute | solution.py:355
  29.2 6.3 %collective-permute-start.2 = (f32[2,128,128]{2,1,0:T(8,128)S(1)}, f32[2,128,128]{2,1,0:T(8,128)S(1)}, u32[]{:S(2)}, u32[]{:S(2)}) collective-permute-start(f32[2,128,128]{2,1,0:T(8,128)S(1)} %get-tuple-element.71), channel_id=1, source_target_pairs={{0,128},{8,136},{16,144},{24,152},{32,160},{40,168},{48,176},{56,1... | collective-permute-start | bytes 393224 | tf_op jit(solution)/shard_map/ppermute | solution.py:355
  32.2 6.5 %collective-permute-start.3 = (f32[2,128,128]{2,1,0:T(8,128)S(1)}, f32[2,128,128]{2,1,0:T(8,128)S(1)}, u32[]{:S(2)}, u32[]{:S(2)}) collective-permute-start(f32[2,128,128]{2,1,0:T(8,128)S(1)} %get-tuple-element.72), channel_id=1, source_target_pairs={{0,64},{8,72},{16,80},{24,88},{32,96},{40,104},{48,112},{56,120},{... | collective-permute-start | bytes 393224 | tf_op jit(solution)/shard_map/ppermute | solution.py:355
  32.6 6.1 %collective-permute-start.4 = (f32[2,128,128]{2,1,0:T(8,128)S(1)}, f32[2,128,128]{2,1,0:T(8,128)S(1)}, u32[]{:S(2)}, u32[]{:S(2)}) collective-permute-start(f32[2,128,128]{2,1,0:T(8,128)S(1)} %get-tuple-element.73), channel_id=1, source_target_pairs={{0,192},{8,200},{16,208},{24,216},{32,224},{40,232},{48,240},{56,2... | collective-permute-start | bytes 393224 | tf_op jit(solution)/shard_map/ppermute | solution.py:355
  38.7 7.1 %collective-permute-start.7 = (f32[128,128]{1,0:T(8,128)S(1)}, f32[128,128]{1,0:T(8,128)S(1)}, u32[]{:S(2)}, u32[]{:S(2)}) collective-permute-start(f32[128,128]{1,0:T(8,128)S(1)} %get-tuple-element.119), channel_id=1, source_target_pairs={{0,48},{1,49},{2,50},{3,51},{4,196},{5,197},{6,198},{7,199},{8,56}... | collective-permute-start | bytes 196616 | tf_op jit(solution)/shard_map/ppermute | solution.py:363
  54.6 6.5 %collective-permute-start.11 = (f32[2,128,128]{2,1,0:T(8,128)S(1)}, f32[2,128,128]{2,1,0:T(8,128)S(1)}, u32[]{:S(2)}, u32[]{:S(2)}) collective-permute-start(f32[2,128,128]{2,1,0:T(8,128)S(1)} %shard_map.162.refs_0_), channel_id=1, source_target_pairs={{0,192},{8,200},{16,208},{24,216},{32,224},{40,232},{48,240},{56,2... | collective-permute-start | bytes 393224 | tf_op jit(solution)/shard_map/ppermute | solution.py:355
  57.8 5.3 %collective-permute-start.10 = (f32[2,128,128]{2,1,0:T(8,128)S(1)}, f32[2,128,128]{2,1,0:T(8,128)S(1)}, u32[]{:S(2)}, u32[]{:S(2)}) collective-permute-start(f32[2,128,128]{2,1,0:T(8,128)S(1)} %shard_map.162.refs_0_), channel_id=1, source_target_pairs={{0,128},{8,136},{16,144},{24,152},{32,160},{40,168},{48,176},{56,1... | collective-permute-start | bytes 393224 | tf_op jit(solution)/shard_map/ppermute | solution.py:355
  63.8 5.7 %collective-permute-start.12 = (f32[32,128]{1,0:T(8,128)S(1)}, f32[32,128]{1,0:T(8,128)S(1)}, u32[]{:S(2)}, u32[]{:S(2)}) collective-permute-start(f32[32,128]{1,0:T(8,128)S(1)} %shard_map.164), channel_id=1, source_target_pairs={{0,8},{8,0},{16,24},{24,16},{32,40},{40,32},{48,56},{56,48},{64,72... | collective-permute-start | bytes 49160 | tf_op jit(solution)/shard_map/ppermute | solution.py:355
  79.9 5.3 %collective-permute-start.14 = (f32[8,2048]{1,0:T(8,128)S(1)}, f32[8,2048]{1,0:T(8,128)S(1)}, u32[]{:S(2)}, u32[]{:S(2)}) collective-permute-start(f32[8,2048]{1,0:T(8,128)S(1)} %get-tuple-element.76), channel_id=1, source_target_pairs={{0,248},{8,16},{16,8},{24,32},{32,24},{40,48},{48,40},{56,64},{64,... | collective-permute-start | bytes 196616 | tf_op jit(solution)/shard_map/ppermute | solution.py:439
  90.5 6.5 %collective-permute-start.16 = (f32[2,128,128]{2,1,0:T(8,128)S(1)}, f32[2,128,128]{2,1,0:T(8,128)S(1)}, u32[]{:S(2)}, u32[]{:S(2)}) collective-permute-start(f32[2,128,128]{2,1,0:T(8,128)S(1)} %get-tuple-element.83), channel_id=1, source_target_pairs={{0,128},{8,136},{16,144},{24,152},{32,160},{40,168},{48,176},{56,1... | collective-permute-start | bytes 393224 | tf_op jit(solution)/shard_map/ppermute | solution.py:355
  91.5 6.5 %collective-permute-start.17 = (f32[2,128,128]{2,1,0:T(8,128)S(1)}, f32[2,128,128]{2,1,0:T(8,128)S(1)}, u32[]{:S(2)}, u32[]{:S(2)}) collective-permute-start(f32[2,128,128]{2,1,0:T(8,128)S(1)} %get-tuple-element.84), channel_id=1, source_target_pairs={{0,64},{8,72},{16,80},{24,88},{32,96},{40,104},{48,112},{56,120},{... | collective-permute-start | bytes 393224 | tf_op jit(solution)/shard_map/ppermute | solution.py:355
  91.8 8.7 %collective-permute-start.18 = (f32[2,128,128]{2,1,0:T(8,128)S(1)}, f32[2,128,128]{2,1,0:T(8,128)S(1)}, u32[]{:S(2)}, u32[]{:S(2)}) collective-permute-start(f32[2,128,128]{2,1,0:T(8,128)S(1)} %get-tuple-element.85), channel_id=1, source_target_pairs={{0,192},{8,200},{16,208},{24,216},{32,224},{40,232},{48,240},{56,2... | collective-permute-start | bytes 393224 | tf_op jit(solution)/shard_map/ppermute | solution.py:355
  100.6 5.3 %collective-permute-start.21 = (f32[128,128]{1,0:T(8,128)S(1)}, f32[128,128]{1,0:T(8,128)S(1)}, u32[]{:S(2)}, u32[]{:S(2)}) collective-permute-start(f32[128,128]{1,0:T(8,128)S(1)} %get-tuple-element.115), channel_id=1, source_target_pairs={{0,48},{1,49},{2,50},{3,51},{4,196},{5,197},{6,198},{7,199},{8,56}... | collective-permute-start | bytes 196616 | tf_op jit(solution)/shard_map/ppermute | solution.py:363
  106.8 5.4 %collective-permute-start.20 = (f32[128,128]{1,0:T(8,128)S(1)}, f32[128,128]{1,0:T(8,128)S(1)}, u32[]{:S(2)}, u32[]{:S(2)}) collective-permute-start(f32[128,128]{1,0:T(8,128)S(1)} %get-tuple-element.114.cosine_sums), channel_id=1, source_target_pairs={{0,48},{1,49},{2,50},{3,51},{4,196},{5,197},{6,198},{7,199},{8,56}... | collective-permute-start | bytes 196616 | tf_op jit(solution)/shard_map/ppermute | solution.py:363
  112.3 5.9 %collective-permute-start.25 = (f32[2,128,128]{2,1,0:T(8,128)S(1)}, f32[2,128,128]{2,1,0:T(8,128)S(1)}, u32[]{:S(2)}, u32[]{:S(2)}) collective-permute-start(f32[2,128,128]{2,1,0:T(8,128)S(1)} %shard_map.170.refs_0_), channel_id=1, source_target_pairs={{0,192},{8,200},{16,208},{24,216},{32,224},{40,232},{48,240},{56,2... | collective-permute-start | bytes 393224 | tf_op jit(solution)/shard_map/ppermute | solution.py:355
  114.9 5.4 %collective-permute-start.24 = (f32[2,128,128]{2,1,0:T(8,128)S(1)}, f32[2,128,128]{2,1,0:T(8,128)S(1)}, u32[]{:S(2)}, u32[]{:S(2)}) collective-permute-start(f32[2,128,128]{2,1,0:T(8,128)S(1)} %shard_map.170.refs_0_), channel_id=1, source_target_pairs={{0,128},{8,136},{16,144},{24,152},{32,160},{40,168},{48,176},{56,1... | collective-permute-start | bytes 393224 | tf_op jit(solution)/shard_map/ppermute | solution.py:355
  120.9 5.3 %collective-permute-start.26 = (f32[32,128]{1,0:T(8,128)S(1)}, f32[32,128]{1,0:T(8,128)S(1)}, u32[]{:S(2)}, u32[]{:S(2)}) collective-permute-start(f32[32,128]{1,0:T(8,128)S(1)} %shard_map.172), channel_id=1, source_target_pairs={{0,8},{8,0},{16,24},{24,16},{32,40},{40,32},{48,56},{56,48},{64,72... | collective-permute-start | bytes 49160 | tf_op jit(solution)/shard_map/ppermute | solution.py:355
  146.6 6.3 %collective-permute-start.30 = (f32[2,128,128]{2,1,0:T(8,128)S(1)}, f32[2,128,128]{2,1,0:T(8,128)S(1)}, u32[]{:S(2)}, u32[]{:S(2)}) collective-permute-start(f32[2,128,128]{2,1,0:T(8,128)S(1)} %get-tuple-element.101), channel_id=1, source_target_pairs={{0,128},{8,136},{16,144},{24,152},{32,160},{40,168},{48,176},{56,1... | collective-permute-start | bytes 393224 | tf_op jit(solution)/shard_map/ppermute | solution.py:355
  147.2 6.7 %collective-permute-start.31 = (f32[2,128,128]{2,1,0:T(8,128)S(1)}, f32[2,128,128]{2,1,0:T(8,128)S(1)}, u32[]{:S(2)}, u32[]{:S(2)}) collective-permute-start(f32[2,128,128]{2,1,0:T(8,128)S(1)} %get-tuple-element.102), channel_id=1, source_target_pairs={{0,64},{8,72},{16,80},{24,88},{32,96},{40,104},{48,112},{56,120},{... | collective-permute-start | bytes 393224 | tf_op jit(solution)/shard_map/ppermute | solution.py:355
  147.8 8.6 %collective-permute-start.32 = (f32[2,128,128]{2,1,0:T(8,128)S(1)}, f32[2,128,128]{2,1,0:T(8,128)S(1)}, u32[]{:S(2)}, u32[]{:S(2)}) collective-permute-start(f32[2,128,128]{2,1,0:T(8,128)S(1)} %get-tuple-element.103), channel_id=1, source_target_pairs={{0,192},{8,200},{16,208},{24,216},{32,224},{40,232},{48,240},{56,2... | collective-permute-start | bytes 393224 | tf_op jit(solution)/shard_map/ppermute | solution.py:355
  156.4 5.3 %collective-permute-start.35 = (f32[128,128]{1,0:T(8,128)S(1)}, f32[128,128]{1,0:T(8,128)S(1)}, u32[]{:S(2)}, u32[]{:S(2)}) collective-permute-start(f32[128,128]{1,0:T(8,128)S(1)} %get-tuple-element.111), channel_id=1, source_target_pairs={{0,48},{1,49},{2,50},{3,51},{4,196},{5,197},{6,198},{7,199},{8,56}... | collective-permute-start | bytes 196616 | tf_op jit(solution)/shard_map/ppermute | solution.py:363
  168.6 5.8 %collective-permute-start.39 = (f32[2,128,128]{2,1,0:T(8,128)S(1)}, f32[2,128,128]{2,1,0:T(8,128)S(1)}, u32[]{:S(2)}, u32[]{:S(2)}) collective-permute-start(f32[2,128,128]{2,1,0:T(8,128)S(1)} %shard_map.178.refs_0_), channel_id=1, source_target_pairs={{0,192},{8,200},{16,208},{24,216},{32,224},{40,232},{48,240},{56,2... | collective-permute-start | bytes 393224 | tf_op jit(solution)/shard_map/ppermute | solution.py:355
  171.1 5.4 %collective-permute-start.38 = (f32[2,128,128]{2,1,0:T(8,128)S(1)}, f32[2,128,128]{2,1,0:T(8,128)S(1)}, u32[]{:S(2)}, u32[]{:S(2)}) collective-permute-start(f32[2,128,128]{2,1,0:T(8,128)S(1)} %shard_map.178.refs_0_), channel_id=1, source_target_pairs={{0,128},{8,136},{16,144},{24,152},{32,160},{40,168},{48,176},{56,1... | collective-permute-start | bytes 393224 | tf_op jit(solution)/shard_map/ppermute | solution.py:355
  171.3 5.2 %collective-permute-start.37 = (f32[2,128,128]{2,1,0:T(8,128)S(1)}, f32[2,128,128]{2,1,0:T(8,128)S(1)}, u32[]{:S(2)}, u32[]{:S(2)}) collective-permute-start(f32[2,128,128]{2,1,0:T(8,128)S(1)} %shard_map.178.refs_0_), channel_id=1, source_target_pairs={{0,64},{8,72},{16,80},{24,88},{32,96},{40,104},{48,112},{56,120},{... | collective-permute-start | bytes 393224 | tf_op jit(solution)/shard_map/ppermute | solution.py:355
  (27 other events, 257.0 us)
